TPU v7x, 32 devices: a whole 2x2x4 slice. The times are simulated.
32 devices in a mesh: dp: 8 (over z, y), section: 2 (over x), tensor: 2 (over core).
Axes of the slice: x: 2, y: 2, z: 4, core: 2. Of those that a mesh axis runs over, the one named last changes fastest.
Arguments:
- layer_input: bfloat16 [2, 8, 1024, 1024], P(None, 'dp', 'tensor'), may hold values from -6 to 6
- segment_ids: int32 [2, 8, 1024], P(None, 'dp'), may hold values from 0 to 127, never falling along the last dimension, each value on 1 to 256 neighbouring positions
- buckets: int32 [2047], replicated, may hold values from 0 to 31, as said below
- attn_in: bfloat16 [2, 1024, 3, 1024], P('section', None, None, 'tensor'), may hold values from -0.1875 to 0.1875
- attn_out: bfloat16 [2, 1024, 1024], P('section', 'tensor'), may hold values from -0.75 to 0.75
- ffn_in: bfloat16 [2, 1024, 4096], P('section', None, 'tensor'), may hold values from -0.1875 to 0.1875
- ffn_out: bfloat16 [2, 4096, 1024], P('section', 'tensor'), may hold values from -0.09375 to 0.09375
- norm_gain: float32 [2, 2, 1024], replicated, may hold values from 0.5 to 1.5
- bert_shift: float32 [4, 1024], replicated, may hold values from -2 to 2
- head_bias: float32 [2, 1024], P(None, 'tensor'), may hold values from -3 to 3
- ffn_bias: float32 [4096], P('tensor'), may hold values from -2 to 2
- position_bias: float32 [16, 32], P('tensor'), may hold values from -4 to 4
- decoder_grads: bfloat16 [2, 2, 8, 1024, 1024], P('section', None, 'dp', 'tensor'), may hold values from -6 to 6
Outputs:
- delivered: bfloat16 [2, 2, 8, 1024, 1024], P('section', None, 'dp', 'tensor')
- input_grad: float32 [2, 8, 1024, 1024], P(None, 'dp', 'tensor', 'section')
- attn_in_grad: float32 [2, 1024, 3, 1024], P('section', 'dp', None, 'tensor')
- attn_out_grad: float32 [2, 1024, 1024], P('section', 'tensor', 'dp')
- ffn_in_grad: float32 [2, 1024, 4096], P('section', 'dp', 'tensor')
- ffn_out_grad: float32 [2, 4096, 1024], P('section', 'tensor', 'dp')
- norm_gain_grad: float32 [2, 2, 1024], replicated
- bert_shift_grad: float32 [4, 1024], replicated
- head_bias_grad: float32 [2, 1024], P(None, 'tensor')
- ffn_bias_grad: float32 [4096], P('tensor')
- position_bias_grad: float32 [16, 32], P('tensor')
Inputs may be any that keep to these rules, and one draw needn't show every extreme that they name: `segment_ids`: segment numbers never fall along a packed row; a token attends to the keys of its own row and segment. Entry o + 1023 is the bucket of the offset o = key position minus query position; negative offsets take buckets below 16, the others the rest, and on either side buckets never fall as the distance grows.
All inputs are finite; a program needn't handle non-finite values.
Results may differ from a plain program's by a relative error of at most 0.025.
Values may be sent and summed in bfloat16 or wider, within the bound.
A program may use at most 448 MiB of HBM per device.

v0:
```python
import functools

import jax
import jax.numpy as jnp
from jax import lax
from jax.experimental import pallas as pl
from jax.experimental.pallas import tpu as pltpu
from jax.sharding import PartitionSpec as P

DH = 64
QB = 128
PAD = 2
REACH = 256
VMEM = 56 * 1024 * 1024
LOW = jnp.bfloat16
F32 = jnp.float32


def dot_nt(left, right):
    return lax.dot_general(left, right, (((1,), (1,)), ((), ())), preferred_element_type=F32)


def dot_nn(left, right):
    return lax.dot_general(left, right, (((1,), (0,)), ((), ())), preferred_element_type=F32)


def params():
    return pltpu.CompilerParams(vmem_limit_bytes=VMEM)


def slotted(shape, dtype):
    return jax.ShapeDtypeStruct((3,) + shape, dtype)


def call_with_slots(kernel, scalars, inputs, in_specs, outputs, out_specs, previous, grid, scratch, name):
    count = len(inputs)
    kept = [] if previous is None else [item for item in previous if item is not None]
    aliases = {}
    if previous is not None:
        at = len(scalars) + count
        for index, item in enumerate(previous):
            if item is not None:
                aliases[at] = index
                at += 1

    def run(*refs):
        front = len(scalars) + count
        kernel(*refs[:front], *refs[front + len(kept) :])

    return pl.pallas_call(
        run,
        grid_spec=pltpu.PrefetchScalarGridSpec(
            num_scalar_prefetch=len(scalars),
            grid=grid,
            in_specs=list(in_specs) + [pl.BlockSpec(memory_space=pl.ANY)] * len(kept),
            out_specs=out_specs,
            scratch_shapes=scratch,
        ),
        out_shape=outputs,
        input_output_aliases=aliases,
        compiler_params=params(),
        name=name,
    )(*scalars, *inputs, *kept)


def toeplitz_kernel(w_ref, t_ref):
    width = w_ref.shape[2]
    half = []
    for head in range(2):
        rows = jnp.broadcast_to(w_ref[0, head : head + 1, :], (QB, width))
        rolled = pltpu.roll(rows, 0, 1, stride=1, stride_axis=0)
        half.append(rolled.T[QB:, :])
    t_ref[0] = jnp.concatenate(half, axis=1)


def toeplitz(offset_bias):
    heads, width = offset_bias.shape
    pairs = heads // 2
    return pl.pallas_call(
        toeplitz_kernel,
        grid=(pairs,),
        in_specs=[pl.BlockSpec((1, 2, width), lambda p: (p, 0, 0))],
        out_specs=pl.BlockSpec((1, width - QB, 2 * QB), lambda p: (p, 0, 0)),
        out_shape=jax.ShapeDtypeStruct((pairs, width - QB, 2 * QB), F32),
        compiler_params=params(),
        name="toeplitz",
    )(offset_bias.reshape(pairs, 2, width))


def diagonal_kernel(a_ref, s_ref):
    total = a_ref[0, 0]
    for extra in range(1, a_ref.shape[0]):
        total = total + a_ref[extra, 0]
    total = jnp.concatenate([jnp.zeros((QB, 2 * QB), F32), total], axis=0)
    width = total.shape[0]
    row = lax.broadcasted_iota(jnp.int32, (QB, QB), 0)
    col = lax.broadcasted_iota(jnp.int32, (QB, QB), 1)
    mirror = jnp.where(row + col == QB - 1, 1.0, 0.0)
    for head in range(2):
        turned = lax.dot_general(
            mirror,
            total[:, head * QB : (head + 1) * QB],
            (((1,), (1,)), ((), ())),
            precision=lax.Precision.HIGHEST,
            preferred_element_type=F32,
        )
        aligned = pltpu.roll(turned, width - QB + 1, 1, stride=1, stride_axis=0)
        s_ref[0, head : head + 1, :] = jnp.sum(aligned, axis=0, keepdims=True)


def diagonals(tables, steps):
    _, pairs, rows, _ = tables.shape
    width = rows + QB
    out = pl.pallas_call(
        diagonal_kernel,
        grid=(pairs,),
        in_specs=[pl.BlockSpec((steps, 1, rows, 2 * QB), lambda p: (0, p, 0, 0))],
        out_specs=pl.BlockSpec((1, 2, width), lambda p: (p, 0, 0)),
        out_shape=jax.ShapeDtypeStruct((pairs, 2, width), F32),
        compiler_params=params(),
        name="diagonals",
    )(tables)
    return out.reshape(2 * pairs, width)


def two_heads(block, first):
    zero = jnp.zeros_like(block)
    return jnp.concatenate([jnp.where(first, block, zero), jnp.where(first, zero, block)], axis=0)


def joined_heads(turned):
    return jnp.concatenate([turned[:DH, :QB], turned[DH:, QB:]], axis=0).T


def fill_columns(segq_ref, segk_ref):
    for block in range(segq_ref.shape[0]):
        rows = jnp.broadcast_to(segq_ref[block : block + 1, :], (QB, QB))
        segk_ref[block * QB : (block + 1) * QB, :] = rows.T


def visit_blocks(seg_ref, origin, count, block):
    @pl.loop(0, count)
    def _(i):
        at = i + origin
        first = seg_ref[at * QB]
        last = seg_ref[at * QB + QB - 1]
        far = (seg_ref[(at - 1) * QB - 1] == first) | (seg_ref[(at + 2) * QB] == last)

        @pl.when(far)
        def _():
            block(i, at, 2)

        @pl.when(jnp.logical_not(far))
        def _():
            block(i, at, 1)


def placed_rows(info, source, halo, target, halo_count):
    edge = PAD * QB
    rows = source.shape[0]
    target[:edge, :] = jnp.zeros((edge, target.shape[1]), target.dtype)
    target[target.shape[0] - edge :, :] = jnp.zeros((edge, target.shape[1]), target.dtype)
    target[pl.ds(pl.multiple_of(info[2] * QB, QB), rows), :] = source[...]
    if halo_count:
        target[pl.ds(pl.multiple_of(info[3] * QB, QB), halo_count), :] = halo[...]


def attend_kernel(halo_count, info, seg_ref, *refs):
    if halo_count:
        segq_ref, q_ref, k_ref, v_ref, t_ref, kh_ref, vh_ref, o_ref, lse_ref, kk_ref, vk_ref = refs[:11]
        segk_ref, kp_ref, vp_ref, vt_ref = refs[11:]
        kk_ref[0] = kh_ref[...]
        vk_ref[0] = vh_ref[...]
    else:
        segq_ref, q_ref, k_ref, v_ref, t_ref, o_ref, lse_ref = refs[:7]
        segk_ref, kp_ref, vp_ref, vt_ref = refs[7:]
        kh_ref = vh_ref = None
    rows = q_ref.shape[1]
    pairs = q_ref.shape[2] // (2 * DH)
    first = lax.broadcasted_iota(jnp.int32, (QB, 2 * DH), 1) < DH

    @pl.when(pl.program_id(0) == 0)
    def _():
        fill_columns(segq_ref, segk_ref)

    placed_rows(info, k_ref.at[0], kh_ref, kp_ref, halo_count)
    placed_rows(info, v_ref.at[0], vh_ref, vp_ref, halo_count)
    vt_ref[...] = vp_ref[...].T

    def block(i, at, reach):
        span = (2 * reach + 1) * QB
        keys = pl.ds(pl.multiple_of((at - reach) * QB, QB), span)
        mine = pl.ds(pl.multiple_of(i * QB, QB), QB)
        shifted = pl.ds((2 - reach) * QB, span)
        allowed = segk_ref[keys, :] == segq_ref[pl.ds(at, 1), :]
        allowed = jnp.concatenate([allowed, allowed], axis=1)
        for pair in range(pairs):
            lanes = slice(pair * 2 * DH, (pair + 1) * 2 * DH)
            both = two_heads(q_ref[0, mine, lanes] * LOW(0.125), first)
            scores = dot_nt(kp_ref[keys, lanes], both) + t_ref[pair, shifted, :]
            scores = jnp.where(allowed, scores, -jnp.inf)
            highest = jnp.max(scores, axis=0, keepdims=True)
            weights = jnp.exp(scores - highest)
            totals = jnp.sum(weights, axis=0, keepdims=True)
            probs = (weights * (1.0 / totals)).astype(LOW)
            turned = dot_nn(vt_ref[lanes, keys], probs)
            o_ref[0, mine, lanes] = joined_heads(turned).astype(LOW)
            lse_ref[0, pair, pl.ds(i, 1), :] = highest + jnp.log(totals)

    visit_blocks(seg_ref, info[2], rows // QB, block)


def head_specs(rows, span, groups, halo_count):
    column = lambda part: pl.BlockSpec((1, rows, span), lambda g, s, t: (s[1], 0, g + part * groups))
    halo = lambda part: pl.BlockSpec((halo_count, span), lambda g, s, t: (0, g + part * groups))
    return column, halo


def attend(info, segments, qkv, halo, bias, previous):
    _, rows, width = qkv.shape
    width = width // 3
    span = min(256, width)
    groups = width // span
    pairs = span // (2 * DH)
    count = rows // QB
    blocks = segments.shape[0] // QB
    halo_count = 0 if halo is None else halo.shape[0]
    column, halo_spec = head_specs(rows, span, groups, halo_count)
    slot_pairs = pl.BlockSpec((1, pairs, count, 2 * QB), lambda g, s, t: (s[1], g, 0, 0))
    in_specs = [
        pl.BlockSpec((blocks, QB), lambda g, s, t: (0, 0)),
        column(0),
        column(1),
        column(2),
        pl.BlockSpec((pairs,) + bias.shape[1:], lambda g, s, t: (g, 0, 0)),
    ]
    inputs = [segments.reshape(blocks, QB), qkv, qkv, qkv, bias]
    outputs = [slotted((rows, width), LOW), slotted((groups * pairs, count, 2 * QB), F32)]
    out_specs = [column(0), slot_pairs]
    if halo_count:
        in_specs += [halo_spec(0), halo_spec(1)]
        inputs += [halo, halo]
        outputs += [slotted((halo_count, width), LOW)] * 2
        kept = pl.BlockSpec((1, halo_count, span), lambda g, s, t: (s[1], 0, g))
        out_specs += [kept, kept]
    return call_with_slots(
        functools.partial(attend_kernel, halo_count),
        [info, segments],
        inputs,
        in_specs,
        outputs,
        out_specs,
        previous,
        (groups,),
        [
            pltpu.VMEM((blocks * QB, QB), jnp.int32),
            pltpu.VMEM((blocks * QB, span), LOW),
            pltpu.VMEM((blocks * QB, span), LOW),
            pltpu.VMEM((span, blocks * QB), LOW),
        ],
        "attend",
    )


def attend_back_kernel(halo_count, info, seg_ref, *refs):
    if halo_count:
        segq_ref, q_ref, k_ref, v_ref, g_ref, t_ref, lse_ref, kh_ref, vh_ref = refs[:9]
        dq_ref, dk_ref, dv_ref, diag_ref, dh_ref = refs[9:14]
        segk_ref, kp_ref, vp_ref, kt_ref, dk_acc, dv_acc = refs[14:]
        kh_ref, vh_ref = kh_ref.at[0], vh_ref.at[0]
    else:
        segq_ref, q_ref, k_ref, v_ref, g_ref, t_ref, lse_ref = refs[:7]
        dq_ref, dk_ref, dv_ref, diag_ref = refs[7:11]
        segk_ref, kp_ref, vp_ref, kt_ref, dk_acc, dv_acc = refs[11:]
        kh_ref = vh_ref = None
    rows = q_ref.shape[1]
    pairs = q_ref.shape[2] // (2 * DH)
    first = lax.broadcasted_iota(jnp.int32, (QB, 2 * DH), 1) < DH

    @pl.when(pl.program_id(0) == 0)
    def _():
        fill_columns(segq_ref, segk_ref)

    placed_rows(info, k_ref.at[0], kh_ref, kp_ref, halo_count)
    placed_rows(info, v_ref.at[0], vh_ref, vp_ref, halo_count)
    kt_ref[...] = kp_ref[...].T
    dk_acc[...] = jnp.zeros_like(dk_acc)
    dv_acc[...] = jnp.zeros_like(dv_acc)
    diag_ref[...] = jnp.zeros_like(diag_ref)

    def block(i, at, reach):
        span = (2 * reach + 1) * QB
        keys = pl.ds(pl.multiple_of((at - reach) * QB, QB), span)
        mine = pl.ds(pl.multiple_of(i * QB, QB), QB)
        shifted = pl.ds((2 - reach) * QB, span)
        allowed = segk_ref[keys, :] == segq_ref[pl.ds(at, 1), :]
        allowed = jnp.concatenate([allowed, allowed], axis=1)
        for pair in range(pairs):
            lanes = slice(pair * 2 * DH, (pair + 1) * 2 * DH)
            both = two_heads(q_ref[0, mine, lanes] * LOW(0.125), first)
            grads = two_heads(g_ref[mine, lanes], first)
            scores = dot_nt(kp_ref[keys, lanes], both) + t_ref[pair, shifted, :]
            scores = jnp.where(allowed, scores - lse_ref[0, pair, pl.ds(i, 1), :], -jnp.inf)
            probs = jnp.exp(scores)
            grad_probs = dot_nt(vp_ref[keys, lanes], grads)
            dv_acc[keys, lanes] += dot_nn(probs.astype(LOW), grads)
            inner = jnp.sum(probs * grad_probs, axis=0, keepdims=True)
            rounded = (probs * (grad_probs - inner)).astype(LOW)
            dk_acc[keys, lanes] += dot_nn(rounded, both)
            diag_ref[0, pair, shifted, :] += rounded.astype(F32)
            turned = dot_nn(kt_ref[lanes, keys], rounded)
            dq_ref[mine, lanes] = (joined_heads(turned) * 0.125).astype(LOW)

    visit_blocks(seg_ref, info[2], rows // QB, block)
    own = pl.ds(pl.multiple_of(info[2] * QB, QB), rows)
    dk_ref[...] = dk_acc[own, :].astype(LOW)
    dv_ref[...] = dv_acc[own, :].astype(LOW)
    if halo_count:
        far = pl.ds(pl.multiple_of(info[3] * QB, QB), halo_count)
        dh_ref[0] = dk_acc[far, :].astype(LOW)
        dh_ref[1] = dv_acc[far, :].astype(LOW)


def attend_back(info, segments, qkv, halo_kept, grad_context, bias, lse, previous):
    _, rows, width = qkv.shape
    width = width // 3
    span = min(256, width)
    groups = width // span
    pairs = span // (2 * DH)
    count = rows // QB
    blocks = segments.shape[0] // QB
    halo_count = 0 if halo_kept is None else halo_kept[0].shape[1]
    column, _ = head_specs(rows, span, groups, halo_count)
    plain = pl.BlockSpec((rows, span), lambda g, s, t: (0, g))
    in_specs = [
        pl.BlockSpec((blocks, QB), lambda g, s, t: (0, 0)),
        column(0),
        column(1),
        column(2),
        plain,
        pl.BlockSpec((pairs,) + bias.shape[1:], lambda g, s, t: (g, 0, 0)),
        pl.BlockSpec((1, pairs, count, 2 * QB), lambda g, s, t: (s[1], g, 0, 0)),
    ]
    inputs = [segments.reshape(blocks, QB), qkv, qkv, qkv, grad_context, bias, lse]
    plain_shape = jax.ShapeDtypeStruct((rows, width), LOW)
    outputs = [plain_shape] * 3 + [slotted(bias.shape, F32)]
    out_specs = [plain] * 3 + [
        pl.BlockSpec((1, pairs) + bias.shape[1:], lambda g, s, t: (s[1], g, 0, 0))
    ]
    if halo_count:
        kept = pl.BlockSpec((1, halo_count, span), lambda g, s, t: (s[1], 0, g))
        in_specs += [kept, kept]
        inputs += list(halo_kept)
        outputs.append(jax.ShapeDtypeStruct((2, halo_count, width), LOW))
        out_specs.append(pl.BlockSpec((2, halo_count, span), lambda g, s, t: (0, 0, lax.rem(g + groups // 2, groups))))
    keep = None if previous is None else [None] * 3 + [previous] + [None] * (len(outputs) - 4)
    return call_with_slots(
        functools.partial(attend_back_kernel, halo_count),
        [info, segments],
        inputs,
        in_specs,
        outputs,
        out_specs,
        keep,
        (groups,),
        [
            pltpu.VMEM((blocks * QB, QB), jnp.int32),
            pltpu.VMEM((blocks * QB, span), LOW),
            pltpu.VMEM((blocks * QB, span), LOW),
            pltpu.VMEM((span, blocks * QB), LOW),
            pltpu.VMEM((blocks * QB, span), F32),
            pltpu.VMEM((blocks * QB, span), F32),
        ],
        "attend_back",
    )


def mean_of(block):
    return jnp.mean(block, axis=-1, keepdims=True)


def rms_scale(block):
    return lax.rsqrt(mean_of(block * block) + 1e-06)


def sum_rows(block):
    return jnp.sum(block, axis=0, keepdims=True)


def gelu_parts(u):
    depth = jnp.abs(u) * 0.7071067811865476
    divisor = 1.0 + 0.3275911 * depth
    t = pl.reciprocal(divisor, approx=True)
    t = t * (2.0 - divisor * t)
    series = ((((1.061405429 * t - 1.453152027) * t + 1.421413741) * t - 0.284496736) * t + 0.254829592) * t
    bell = jnp.exp(-0.5 * u * u)
    tail = 0.5 * series * bell
    below = jnp.where(u >= 0.0, 1.0 - tail, tail)
    return u * below, below + u * bell * 0.3989422804014327


def enter_kernel(info, first_ref, second_ref, gain_ref, shift_ref, own_ref, oth_ref, x_ref, e_ref, qkv_ref, halo_ref):
    m = pl.program_id(0)
    half = own_ref.shape[1]

    @pl.when((m == 0) & (info[0] == 1))
    def _():
        x_ref[0] = first_ref[...]
        e_ref[0] = first_ref[...]

    @pl.when((m == 0) & (info[0] == 0))
    def _():
        x_ref[0] = second_ref[...]
        x = second_ref[...].astype(F32)
        e_ref[0] = (x * rms_scale(x) * gain_ref[...]).astype(LOW)

    e = e_ref[0]
    for part, weight in enumerate((own_ref, oth_ref)):
        lanes = slice(part * half, (part + 1) * half)
        block = (dot_nn(e, weight[...]) + shift_ref[:, lanes]).astype(LOW)
        qkv_ref[0, :, lanes] = block
    start = pl.ds(pl.multiple_of(info[4], QB), halo_ref.shape[0])
    halo_ref[:, :half] = qkv_ref[0, start, half:]
    halo_ref[:, half:] = qkv_ref[0, start, :half]


def enter(info, first, second, gain, shift, own, oth, previous):
    rows, width = first.shape
    half = own.shape[1] // 3
    whole = pl.BlockSpec((rows, width), lambda m, s: (0, 0))
    weight = pl.BlockSpec((width, half), lambda m, s: (0, m))
    kept = pl.BlockSpec((1, rows, width), lambda m, s: (s[1], 0, 0))
    keep = None if previous is None else list(previous) + [None]
    return call_with_slots(
        enter_kernel,
        [info],
        [first, second, gain, shift, own, oth],
        [
            whole,
            whole,
            pl.BlockSpec((1, width), lambda m, s: (0, 0)),
            pl.BlockSpec((1, 2 * half), lambda m, s: (0, m)),
            weight,
            weight,
        ],
        [
            slotted((rows, width), LOW),
            slotted((rows, width), LOW),
            slotted((rows, 6 * half), LOW),
            jax.ShapeDtypeStruct((REACH, 4 * half), LOW),
        ],
        [
            kept,
            kept,
            pl.BlockSpec((1, rows, 2 * half), lambda m, s: (s[1], 0, m)),
            pl.BlockSpec((REACH, 2 * half), lambda m, s: (0, jnp.maximum(m - 1, 0))),
        ],
        keep,
        (3,),
        [],
        "enter",
    )


def feed_kernel(
    info, x_ref, c_ref, wo_own, wo_oth, up_own, up_oth, down_own, down_oth, bias_ref, gain_ref, shift_ref,
    f_ref, slope_ref, n_ref, one_ref, two_ref, out_ref, acc_ref, carry_ref
):
    j = pl.program_id(0)
    steps = pl.num_programs(0)
    half = wo_own.shape[0]
    rows = x_ref.shape[1]

    @pl.when(j == 0)
    def _():
        joined = (
            dot_nn(c_ref[0, :, :half], wo_own[...])
            + dot_nn(c_ref[0, :, half:], wo_oth[...])
            + x_ref[0].astype(F32)
        )

        @pl.when(info[0] == 1)
        def _():
            before = joined + shift_ref[0:1, :]
            one_ref[0] = before
            center = before - mean_of(before)
            normed = center * lax.rsqrt(mean_of(center * center) + 1e-05) * gain_ref[0:1, :] + shift_ref[2:3, :]
            carry_ref[...] = normed
            n_ref[0] = normed.astype(LOW)

        @pl.when(info[0] == 0)
        def _():
            one_ref[0] = joined
            carry_ref[...] = joined
            n_ref[0] = (joined * rms_scale(joined) * gain_ref[1:2, :]).astype(LOW)

        acc_ref[...] = jnp.zeros_like(acc_ref)

    def part(up, down):
        for at in range(0, rows, 256):
            piece = slice(at, at + 256)
            u = dot_nn(n_ref[0, piece, :], up[...]) + bias_ref[...]
            f, slope = gelu_parts(u)
            low = f.astype(LOW)
            f_ref[0, piece, :] = low
            slope_ref[0, piece, :] = slope.astype(LOW)
            acc_ref[piece, :] += dot_nn(low, down[...])

    @pl.when(j < steps // 2)
    def _():
        part(up_own, down_own)

    @pl.when(j >= steps // 2)
    def _():
        part(up_oth, down_oth)

    @pl.when(j == steps - 1)
    def _():
        joined = carry_ref[...] + acc_ref[...]

        @pl.when(info[0] == 1)
        def _():
            before = joined + shift_ref[1:2, :]
            two_ref[0] = before
            center = before - mean_of(before)
            normed = center * lax.rsqrt(mean_of(center * center) + 1e-05) * gain_ref[1:2, :] + shift_ref[3:4, :]
            out_ref[...] = normed.astype(LOW)

        @pl.when(info[0] == 0)
        def _():
            two_ref[0] = joined
            out_ref[...] = joined.astype(LOW)


def split_steps(hidden, chunk):
    each = hidden // chunk
    near = lambda j: jnp.minimum(j, each - 1)
    far = lambda j: jnp.maximum(j - each, 0)
    return 2 * each, near, far


def feed(info, x, context, wo, up, down, bias, gains, shifts, previous):
    _, rows, width = x.shape
    hidden = up[0].shape[1]
    chunk = min(512, hidden)
    steps, near, far = split_steps(hidden, chunk)
    kept = pl.BlockSpec((1, rows, width), lambda j, s: (s[1], 0, 0))
    fixed = lambda a: pl.BlockSpec(a.shape, lambda j, s: (0, 0))
    moving = pl.BlockSpec((1, rows, chunk), lambda j, s: (s[1], 0, j))
    keep = None if previous is None else list(previous) + [None]
    return call_with_slots(
        feed_kernel,
        [info],
        [x, context, wo[0], wo[1], up[0], up[1], down[0], down[1], bias, gains, shifts],
        [
            kept,
            kept,
            fixed(wo[0]),
            fixed(wo[1]),
            pl.BlockSpec((width, chunk), lambda j, s: (0, near(j))),
            pl.BlockSpec((width, chunk), lambda j, s: (0, far(j))),
            pl.BlockSpec((chunk, width), lambda j, s: (near(j), 0)),
            pl.BlockSpec((chunk, width), lambda j, s: (far(j), 0)),
            pl.BlockSpec((1, chunk), lambda j, s: (0, j)),
            fixed(gains),
            fixed(shifts),
        ],
        [
            slotted((rows, 2 * hidden), LOW),
            slotted((rows, 2 * hidden), LOW),
            slotted((rows, width), LOW),
            slotted((rows, width), F32),
            slotted((rows, width), F32),
            jax.ShapeDtypeStruct((rows, width), LOW),
        ],
        [moving, moving, kept, kept, kept, pl.BlockSpec((rows, width), lambda j, s: (0, 0))],
        keep,
        (steps,),
        [pltpu.VMEM((rows, width), F32), pltpu.VMEM((rows, width), F32)],
        "feed",
    )


def layer_norm_back(before, grad, gain_row):
    center = before - mean_of(before)
    scale = lax.rsqrt(mean_of(center * center) + 1e-05)
    unit = center * scale
    inner = grad * gain_row
    back = scale * (inner - mean_of(inner) - unit * mean_of(inner * unit))
    return back, sum_rows(grad * unit)


def rms_norm_back(before, grad, gain_row):
    scale = rms_scale(before)
    unit = before * scale
    inner = grad * gain_row
    back = scale * (inner - unit * mean_of(inner * unit))
    return back, sum_rows(grad * unit)


def feed_back_kernel(
    info, got_ref, mine_ref, other_ref, one_ref, two_ref, slope_ref, wo_own, wo_oth, up_own, up_oth, down_own, down_oth,
    gain_ref, dy_ref, du_ref, db_ref, stat_ref, bias_ref, dz_ref, dc_ref, acc_ref, carry_ref
):
    j = pl.program_id(0)
    steps = pl.num_programs(0)
    half = wo_own.shape[0]
    rows = got_ref.shape[0]

    @pl.when(j == 0)
    def _():
        stat_ref[...] = jnp.zeros_like(stat_ref)
        acc_ref[...] = jnp.zeros_like(acc_ref)

        @pl.when(info[0] == 1)
        def _():
            grad = got_ref[...].astype(F32)
            back, gain = layer_norm_back(two_ref[0], grad, gain_ref[1:2, :])
            stat_ref[0, 1:2, :] = gain
            stat_ref[0, 5:6, :] = sum_rows(grad)
            stat_ref[0, 3:4, :] = sum_rows(back)
            carry_ref[...] = back
            dy_ref[0] = back.astype(LOW)

        @pl.when(info[0] == 0)
        def _():
            grad = mine_ref[...].astype(F32) + other_ref[...].astype(F32)
            carry_ref[...] = grad
            dy_ref[0] = grad.astype(LOW)

    def part(up, down):
        for at in range(0, rows, 256):
            piece = slice(at, at + 256)
            grad = dot_nt(dy_ref[0, piece, :], down[...])
            low = (grad * slope_ref[0, piece, :].astype(F32)).astype(LOW)
            du_ref[0, piece, :] = low
            acc_ref[piece, :] += dot_nt(low, up[...])
        bias_ref[0] = sum_rows(du_ref[0].astype(F32))

    @pl.when(j < steps // 2)
    def _():
        part(up_own, down_own)

    @pl.when(j >= steps // 2)
    def _():
        part(up_oth, down_oth)

    @pl.when(j == steps - 1)
    def _():
        @pl.when(info[0] == 1)
        def _():
            grad = acc_ref[...] + carry_ref[...]
            back, gain = layer_norm_back(one_ref[0], grad, gain_ref[0:1, :])
            stat_ref[0, 0:1, :] = gain
            stat_ref[0, 4:5, :] = sum_rows(grad)
            stat_ref[0, 2:3, :] = sum_rows(back)
            dz_ref[...] = back

        @pl.when(info[0] == 0)
        def _():
            back, gain = rms_norm_back(one_ref[0], acc_ref[...], gain_ref[1:2, :])
            stat_ref[0, 1:2, :] = gain
            dz_ref[...] = carry_ref[...] + back

        low = dz_ref[...].astype(LOW)
        db_ref[0] = low
        dc_ref[:, :half] = dot_nt(low, wo_own[...]).astype(LOW)
        dc_ref[:, half:] = dot_nt(low, wo_oth[...]).astype(LOW)


def feed_back(info, got, mine, other, one, two, slope, wo, up, down, gains, previous):
    _, rows, width = one.shape
    hidden = up[0].shape[1]
    chunk = min(512, hidden)
    steps, near, far = split_steps(hidden, chunk)
    kept = pl.BlockSpec((1, rows, width), lambda j, s: (s[1], 0, 0))
    fixed = lambda a: pl.BlockSpec(a.shape, lambda j, s: (0, 0))
    plain = pl.BlockSpec((rows, width), lambda j, s: (0, 0))
    moving = pl.BlockSpec((1, rows, chunk), lambda j, s: (s[1], 0, j))
    keep = None if previous is None else list(previous) + [None, None]
    return call_with_slots(
        feed_back_kernel,
        [info],
        [got, mine, other, one, two, slope, wo[0], wo[1], up[0], up[1], down[0], down[1], gains],
        [
            plain,
            plain,
            plain,
            kept,
            kept,
            moving,
            fixed(wo[0]),
            fixed(wo[1]),
            pl.BlockSpec((width, chunk), lambda j, s: (0, near(j))),
            pl.BlockSpec((width, chunk), lambda j, s: (0, far(j))),
            pl.BlockSpec((chunk, width), lambda j, s: (near(j), 0)),
            pl.BlockSpec((chunk, width), lambda j, s: (far(j), 0)),
            fixed(gains),
        ],
        [
            slotted((rows, width), LOW),
            slotted((rows, 2 * hidden), LOW),
            slotted((rows, width), LOW),
            slotted((8, width), F32),
            slotted((1, 2 * hidden), F32),
            jax.ShapeDtypeStruct((rows, width), F32),
            jax.ShapeDtypeStruct((rows, width), LOW),
        ],
        [
            kept,
            moving,
            kept,
            pl.BlockSpec((1, 8, width), lambda j, s: (s[1], 0, 0)),
            pl.BlockSpec((1, 1, chunk), lambda j, s: (s[1], 0, j)),
            plain,
            plain,
        ],
        keep,
        (steps,),
        [pltpu.VMEM((rows, width), F32), pltpu.VMEM((rows, width), F32)],
        "feed_back",
    )


def enter_back_kernel(
    info, dq_ref, dk_ref, dv_ref, far_ref, x_ref, dz_ref, own_ref, oth_ref, gain_ref,
    d_ref, stat_ref, low_ref, lower_ref, acc_ref
):
    m = pl.program_id(0)
    half = own_ref.shape[1]
    start = pl.ds(pl.multiple_of(info[4], QB), far_ref.shape[1])

    @pl.when(m == 0)
    def _():
        stat_ref[...] = jnp.zeros_like(stat_ref)
        acc_ref[...] = jnp.zeros_like(acc_ref)
        d_ref[0] = dq_ref[...]
        stat_ref[0, 0:1, :] = sum_rows(dq_ref[...].astype(F32))

    def with_far(block_ref, part):
        d_ref[0] = block_ref[...]
        d_ref[0, start, :] = (block_ref[start, :].astype(F32) + far_ref[part].astype(F32)).astype(LOW)

    @pl.when(m == 1)
    def _():
        with_far(dk_ref, 0)

    @pl.when(m == 2)
    def _():
        with_far(dv_ref, 1)
        stat_ref[0, 1:2, :] = sum_rows(d_ref[0].astype(F32))

    acc_ref[...] += dot_nt(d_ref[0, :, :half], own_ref[...]) + dot_nt(d_ref[0, :, half:], oth_ref[...])

    @pl.when(m == 2)
    def _():
        split = lower_ref.shape[1]

        @pl.when(info[0] == 1)
        def _():
            total = dz_ref[...] + acc_ref[...]
            low_ref[...] = total.astype(LOW)
            lower_ref[...] = total[:, :split]

        @pl.when(info[0] == 0)
        def _():
            back, gain = rms_norm_back(x_ref[0].astype(F32), acc_ref[...], gain_ref[...])
            stat_ref[0, 2:3, :] = gain
            total = dz_ref[...] + back
            low_ref[...] = total.astype(LOW)
            lower_ref[...] = total[:, :split]


def enter_back(info, dq, dk, dv, far, x, dz, own, oth, gain, previous):
    _, rows, width = x.shape
    half = own.shape[1] // 3
    plain = pl.BlockSpec((rows, width), lambda m, s: (0, 0))
    kept = pl.BlockSpec((1, rows, width), lambda m, s: (s[1], 0, 0))
    weight = pl.BlockSpec((width, half), lambda m, s: (0, m))
    keep = None if previous is None else list(previous) + [None, None]
    return call_with_slots(
        enter_back_kernel,
        [info],
        [dq, dk, dv, far, x, dz, own, oth, gain],
        [
            plain,
            plain,
            plain,
            pl.BlockSpec(far.shape, lambda m, s: (0, 0, 0)),
            kept,
            plain,
            weight,
            weight,
            pl.BlockSpec((1, width), lambda m, s: (0, 0)),
        ],
        [
            slotted((rows, 6 * half), LOW),
            slotted((8, width), F32),
            jax.ShapeDtypeStruct((rows, width), LOW),
            jax.ShapeDtypeStruct((rows, width // 2), F32),
        ],
        [
            pl.BlockSpec((1, rows, 2 * half), lambda m, s: (s[1], 0, m)),
            pl.BlockSpec((1, 8, width), lambda m, s: (s[1], 0, 0)),
            plain,
            pl.BlockSpec((rows, width // 2), lambda m, s: (0, 0)),
        ],
        keep,
        (3,),
        [pltpu.VMEM((rows, width), F32)],
        "enter_back",
    )


def wide_kernel(left_ref, right_ref, own_ref, oth_ref, turned_ref):
    j = pl.program_id(0)
    rows = left_ref.shape[1]

    @pl.when(j == 0)
    def _():
        for slot in range(2):
            turned_ref[:, slot * rows : (slot + 1) * rows] = left_ref[slot].T

    both = jnp.concatenate([right_ref[0], right_ref[1]], axis=0)
    product = dot_nn(turned_ref[...], both).astype(LOW)

    @pl.when(lax.rem(j, 2) == 0)
    def _():
        own_ref[...] = product

    @pl.when(lax.rem(j, 2) == 1)
    def _():
        oth_ref[...] = product


def wide_grad(left, right, chunk, position, name):
    _, rows, width = left.shape
    total = right.shape[2]
    steps = total // chunk
    out = jax.ShapeDtypeStruct((width, total // 2), LOW)
    spec = pl.BlockSpec((width, chunk), lambda j: (0, j // 2))
    return pl.pallas_call(
        wide_kernel,
        grid=(steps,),
        in_specs=[
            pl.BlockSpec((2, rows, width), lambda j: (0, 0, 0)),
            pl.BlockSpec((2, rows, chunk), lambda j: (0, 0, position(j))),
        ],
        out_specs=[spec, spec],
        out_shape=[out, out],
        scratch_shapes=[pltpu.VMEM((width, 2 * rows), LOW)],
        compiler_params=params(),
        name=name,
    )(left, right)


def tall_kernel(left_ref, right_ref, own_ref, oth_ref):
    j = pl.program_id(0)
    piece = own_ref.shape[2]
    turned = jnp.concatenate([left_ref[0].T, left_ref[1].T], axis=1)
    both = jnp.concatenate([right_ref[0], right_ref[1]], axis=0)
    product = dot_nn(turned, both).astype(LOW)

    def store(ref):
        for at in range(ref.shape[0]):
            ref[at] = product[:, at * piece : (at + 1) * piece]

    @pl.when(lax.rem(j, 2) == 0)
    def _():
        store(own_ref)

    @pl.when(lax.rem(j, 2) == 1)
    def _():
        store(oth_ref)


def tall_grad(left, right, chunk, pieces, name):
    _, rows, total = left.shape
    width = right.shape[2]
    each = total // 2 // chunk
    out = jax.ShapeDtypeStruct((pieces, total // 2, width // pieces), LOW)
    spec = pl.BlockSpec((pieces, chunk, width // pieces), lambda j: (0, j // 2, 0))
    return pl.pallas_call(
        tall_kernel,
        grid=(2 * each,),
        in_specs=[
            pl.BlockSpec((2, rows, chunk), lambda j: (0, 0, lax.rem(j, 2) * each + j // 2)),
            pl.BlockSpec((2, rows, width), lambda j: (0, 0, 0)),
        ],
        out_specs=[spec, spec],
        out_shape=[out, out],
        compiler_params=params(),
        name=name,
    )(left, right)


def passed_along(value, axis, steps):
    count = lax.axis_size(axis)
    initial, last = (max(0, -steps), min(count, count - steps))
    return lax.ppermute(value, axis, [(source, source + steps) for source in range(initial, last)])


def spread(block, axis, source):
    block = jnp.where(lax.axis_index(axis) == source, block, jnp.zeros_like(block))
    return lax.psum(block, axis)


def layer_norm(operand, gain_row, shift_row):
    center = operand - jnp.mean(operand, axis=-1, keepdims=True)
    variance = jnp.mean(center * center, axis=-1, keepdims=True)
    return center * lax.rsqrt(variance + 1e-05) * gain_row + shift_row


def rms_norm(operand, gain_row):
    return (
        operand * lax.rsqrt(jnp.mean(operand * operand, axis=-1, keepdims=True) + 1e-06) * gain_row
    )


def gelu_act(operand):
    return jax.nn.gelu(operand, approximate=False)


def gelu_slope(operand):
    return (
        0.5 * (1.0 + jax.scipy.special.erf(operand * 0.7071067811865476))
        + operand * jnp.exp(-0.5 * operand * operand) * 0.3989422804014327
    )


def entry_norm(residual, gain_rows, leading):
    return jnp.where(leading, residual, rms_norm(residual, gain_rows[0]))


def middle(residual, branch, gain_rows, shift_rows, leading):
    joined = residual + branch
    bert_rows = layer_norm(joined + shift_rows[0], gain_rows[0], shift_rows[2])
    carried = jnp.where(leading, bert_rows, joined)
    normed = jnp.where(leading, bert_rows, rms_norm(joined, gain_rows[1]))
    return (carried, normed)


def final(carried, second, gain_rows, shift_rows, leading):
    joined = carried + second
    return jnp.where(
        leading, layer_norm(joined + shift_rows[1], gain_rows[1], shift_rows[3]), joined
    )


def contract_rows(left, right):
    return lax.dot_general(
        left, right, (((0,), (0,)), ((), ())), preferred_element_type=jnp.float32
    )


def contract_cols(left, right):
    return lax.dot_general(
        left, right, (((1,), (1,)), ((), ())), preferred_element_type=jnp.float32
    )


def gather_rows(operand, weight):
    return (
        jnp.dot(
            lax.all_gather(operand, "tensor", axis=0, tiled=True),
            weight,
            preferred_element_type=jnp.float32,
        ),
        None,
    )


def collect(full_rows, weight):
    return lax.psum_scatter(
        jnp.dot(full_rows, weight, preferred_element_type=jnp.float32),
        "tensor",
        scatter_dimension=0,
        tiled=True,
    )


def scatter_back(grad_rows, weight):
    return lax.psum_scatter(
        contract_cols(grad_rows, weight).astype(jnp.bfloat16),
        "tensor",
        scatter_dimension=0,
        tiled=True,
    ).astype(jnp.float32)


def fold_back(grad_share, weight, activations):
    fragment = lax.all_gather(grad_share, "tensor", axis=0, tiled=True)
    product_rows = contract_cols(fragment, weight)
    return (product_rows, contract_rows(activations, fragment))


def weight_grad(operand, grad_rows):
    return contract_rows(lax.all_gather(operand, "tensor", axis=0, tiled=True), grad_rows)


DH = 64
QB = 128
NARROW = 3
WIDE = 5
VMEM = 56 * 1024 * 1024


def padded(segments):
    return jnp.pad(segments, (PAD * QB, PAD * QB), constant_values=-1)


def general_body(
    layer_input,
    segment_ids,
    buckets,
    attn_in,
    attn_out,
    ffn_in,
    ffn_out,
    norm_gain,
    bert_shift,
    head_bias,
    ffn_bias,
    position_bias,
    decoder_grads,
):
    micro_count = layer_input.shape[0]
    shard_rows = layer_input.shape[2]
    model_width = layer_input.shape[3]
    length = segment_ids.shape[2]
    leading = lax.axis_index("section") == 0
    weighting = jnp.where(leading, 1.0, 0.0)
    qkv_weight = attn_in[0].reshape(model_width, -1)
    out_weight = attn_out[0]
    ffn_up = ffn_in[0]
    ffn_down = ffn_out[0]
    gain_rows = jnp.where(leading, norm_gain[0], norm_gain[1])
    head_shift = head_bias * weighting
    qkv_shift = jnp.concatenate([head_shift[0], jnp.zeros_like(head_shift[0]), head_shift[1]])
    ffn_shift = ffn_bias * weighting
    bias_table = position_bias * (1.0 - weighting)
    bucket_hits = (buckets[None, :] == jnp.arange(bias_table.shape[1])[:, None]).astype(jnp.float32)
    offset_bias = jnp.dot(bias_table, bucket_hits, precision=lax.Precision.HIGHEST)
    near = length - 1 - 3 * QB
    bias = toeplitz(offset_bias[:, near : near + 6 * QB])
    info = jnp.array([0, 0, PAD, 0, 0], jnp.int32)
    segment_rows = segment_ids[:, 0]

    def middle_part(residual_in, branch_in, gain_in, shift_in):
        return middle(residual_in, branch_in, gain_in, shift_in, leading)

    def final_part(carried_in, second_in, gain_in, shift_in):
        return final(carried_in, second_in, gain_in, shift_in, leading)

    def entry_part(residual_in, gain_in):
        return entry_norm(residual_in, gain_in, leading)

    received = jnp.zeros((shard_rows, model_width), jnp.bfloat16)
    saved_steps = []
    encoded = []
    for moment in range(micro_count + 1):
        own_rows = layer_input[min(moment, micro_count - 1), 0]
        if moment >= micro_count:
            own_rows = jnp.zeros_like(own_rows)
        segment_row = jnp.where(
            leading, segment_rows[min(moment, micro_count - 1)], segment_rows[max(moment - 1, 0)]
        )
        forward_incoming = jnp.where(leading, own_rows, received)
        forward_residual = forward_incoming.astype(jnp.float32)
        forward_entered = entry_norm(forward_residual, gain_rows, leading).astype(jnp.bfloat16)
        projected, forward_gathered_in = gather_rows(forward_entered, qkv_weight)
        forward_qkv = (projected + qkv_shift).astype(jnp.bfloat16)
        forward_context, forward_log_totals = attend(
            info, padded(segment_row), forward_qkv[None], None, bias, None
        )
        forward_context = forward_context[0]
        forward_branch = collect(forward_context, out_weight)
        forward_carried, forward_normed = middle(
            forward_residual, forward_branch, gain_rows, bert_shift, leading
        )
        pre_full, forward_gathered_mid = gather_rows(forward_normed.astype(jnp.bfloat16), ffn_up)
        forward_pre_act = pre_full + ffn_shift
        forward_second = collect(gelu_act(forward_pre_act).astype(jnp.bfloat16), ffn_down)
        result = final(forward_carried, forward_second, gain_rows, bert_shift, leading).astype(
            jnp.bfloat16
        )
        result, saved = (
            result,
            (
                forward_incoming,
                segment_row,
                forward_branch,
                forward_second,
                forward_qkv,
                forward_context,
                forward_log_totals,
                forward_pre_act,
                forward_gathered_in,
                forward_gathered_mid,
            ),
        )
        saved_steps.append(saved)
        if moment >= 1:
            encoded.append(result)
        if moment < micro_count:
            received = passed_along(result, "section", 1)
    delivered = spread(jnp.stack(encoded), "section", 1)
    section_grads = lax.psum(
        decoder_grads[0, :, 0].astype(jnp.float32).astype(jnp.bfloat16), "section"
    ).astype(jnp.float32)
    grad_received = jnp.zeros((shard_rows, model_width), jnp.float32)
    running_terms = None
    input_rows = []
    for moment in range(micro_count + 1):
        own_grad = section_grads[min(moment, micro_count - 1)]
        if moment >= micro_count:
            own_grad = jnp.zeros_like(own_grad)
        earlier = saved_steps[max(moment - 1, 0)]
        later = saved_steps[min(moment + 1, micro_count)]
        chosen = jax.tree.map(
            lambda from_first, from_second: jnp.where(leading, from_first, from_second),
            earlier,
            later,
        )
        (
            incoming,
            backward_segment_row,
            branch,
            second,
            qkv,
            context,
            log_totals,
            pre_act,
            gathered_in,
            gathered_mid,
        ) = chosen
        residual = incoming.astype(jnp.float32)
        (carried, normed), pull_middle = jax.vjp(
            middle_part, residual, branch, gain_rows, bert_shift
        )
        finished, pull_final = jax.vjp(final_part, carried, second, gain_rows, bert_shift)
        grad_carried, grad_second, gain_end, shift_end = pull_final(
            jnp.where(leading, grad_received, own_grad)
        )
        hidden = gelu_act(pre_act).astype(jnp.bfloat16)
        grad_hidden, backward_grad_down = fold_back(
            grad_second.astype(jnp.bfloat16), ffn_down, hidden
        )
        grad_pre = (grad_hidden * gelu_slope(pre_act)).astype(jnp.bfloat16)
        grad_shift = jnp.sum(grad_pre.astype(jnp.float32), axis=0) * weighting
        backward_grad_up = weight_grad(normed.astype(jnp.bfloat16), grad_pre)
        grad_normed = scatter_back(grad_pre, ffn_up)
        grad_residual, grad_branch, gain_mid, shift_mid = pull_middle((grad_carried, grad_normed))
        grad_context, backward_grad_out_weight = fold_back(
            grad_branch.astype(jnp.bfloat16), out_weight, context
        )
        low_q, low_k, low_v, grad_table = attend_back(
            info, padded(backward_segment_row), qkv[None], None, grad_context.astype(jnp.bfloat16), bias, log_totals, None
        )
        grad_table = grad_table[0]
        grad_head = (
            jnp.stack([jnp.sum(low.astype(jnp.float32), axis=0) for low in (low_q, low_v)]) * weighting
        )
        grad_rows = jnp.concatenate([low_q, low_k, low_v], axis=1)
        entered, pull_entry = jax.vjp(entry_part, residual, gain_rows)
        backward_grad_qkv = weight_grad(entered.astype(jnp.bfloat16), grad_rows)
        grad_entered = scatter_back(grad_rows, qkv_weight)
        grad_from_entry, gain_entry = pull_entry(grad_entered)
        grad_terms = (
            backward_grad_qkv,
            backward_grad_out_weight,
            backward_grad_up,
            backward_grad_down,
            gain_end + gain_mid + gain_entry,
            shift_end + shift_mid,
            grad_head,
            grad_shift,
            grad_table,
        )
        grad_input, grad_terms = (grad_residual + grad_from_entry, grad_terms)
        if running_terms is None:
            running_terms = grad_terms
        else:
            running_terms = jax.tree.map(jnp.add, running_terms, grad_terms)
        if moment >= 1:
            input_rows.append(grad_input)
        if moment < micro_count:
            grad_received = passed_along(grad_input.astype(jnp.bfloat16), "section", -1).astype(
                grad_input.dtype
            )
    input_all = jnp.stack(input_rows)
    half_width = model_width // 2
    upper_half = passed_along(
        input_all[:, :, half_width:].astype(jnp.bfloat16), "section", 1
    ).astype(jnp.float32)
    input_grad = jnp.where(leading, input_all[:, :, :half_width], upper_half)[:, None]
    (
        grad_qkv,
        grad_out_weight,
        grad_up,
        grad_down,
        gain_sum,
        shift_sum,
        head_sum,
        shift_ffn_sum,
        table_sum,
    ) = running_terms
    near_hits = bucket_hits[:, near : near + 6 * QB]
    table_sum = jnp.dot(diagonals(table_sum[None], 1), near_hits.T, precision=lax.Precision.HIGHEST) * (
        1.0 - weighting
    )
    weights_out = (
        lax.psum_scatter(
            grad_qkv.reshape(1, model_width, 3, -1).astype(jnp.bfloat16),
            "dp",
            scatter_dimension=1,
            tiled=True,
        ).astype(jnp.float32),
        lax.psum_scatter(
            grad_out_weight[None].astype(jnp.bfloat16), "dp", scatter_dimension=2, tiled=True
        ).astype(jnp.float32),
        lax.psum_scatter(
            grad_up[None].astype(jnp.bfloat16), "dp", scatter_dimension=1, tiled=True
        ).astype(jnp.float32),
        lax.psum_scatter(
            grad_down[None].astype(jnp.bfloat16), "dp", scatter_dimension=2, tiled=True
        ).astype(jnp.float32),
    )
    gain_both = jnp.stack([gain_sum * weighting, gain_sum * (1.0 - weighting)])
    shared_out = lax.psum((gain_both, shift_sum), ("dp", "section", "tensor"))
    split_out = lax.psum((head_sum, shift_ffn_sum, table_sum), ("dp", "section"))
    return (
        delivered[None, :, None],
        input_grad,
        weights_out[0],
        weights_out[1],
        weights_out[2],
        weights_out[3],
        shared_out[0],
        shared_out[1],
        split_out[0],
        split_out[1],
        split_out[2],
    )


def swapped(value, axis, bit):
    pairs = [(at, at ^ bit) for at in range(lax.axis_size(axis))]
    return lax.ppermute(value, axis, pairs)


def halves_summed(total, axis, bit):
    side = lax.rem(lax.axis_index(axis) // bit, 2)
    given = lax.dynamic_index_in_dim(total, 1 - side, 0, keepdims=False)
    kept = lax.dynamic_index_in_dim(total, side, 0, keepdims=False)
    got = swapped(given, axis, bit)
    return (kept.astype(F32) + got.astype(F32)).astype(LOW)


def scattered(own, got):
    total = (own.astype(F32) + got.astype(F32)).astype(LOW)
    rest = own.shape[1:]
    total = jnp.moveaxis(total.reshape((2, 2, 2) + rest), 2, 0)
    total = halves_summed(total, "dp", 1)
    total = jnp.moveaxis(total, 1, 0)
    total = halves_summed(total, "dp", 2)
    side = lax.rem(lax.axis_index("dp") // 4, 2)
    given = lax.dynamic_index_in_dim(total, 1 - side, 0, keepdims=False)
    kept = lax.dynamic_index_in_dim(total, side, 0, keepdims=False)
    return kept.astype(F32) + swapped(given, "dp", 4).astype(F32)


def paired_body(
    layer_input,
    segment_ids,
    buckets,
    attn_in,
    attn_out,
    ffn_in,
    ffn_out,
    norm_gain,
    bert_shift,
    head_bias,
    ffn_bias,
    position_bias,
    decoder_grads,
):
    micro_count, _, rows, width = layer_input.shape
    length = segment_ids.shape[2]
    heads, bucket_count = position_bias.shape
    section = lax.axis_index("section")
    core = lax.axis_index("tensor")
    leading = section == 0
    lead = jnp.where(leading, 1, 0).astype(jnp.int32)
    pieces = lax.axis_size("dp")

    remote_grads = [
        lax.ppermute(decoder_grads[0, micro, 0], "section", [(0, 1)]) for micro in range(micro_count)
    ]
    qkv_own = attn_in[0].reshape(width, -1)
    qkv_oth = swapped(qkv_own, "tensor", 1)
    wo = (attn_out[0], swapped(attn_out[0], "tensor", 1))
    up = (ffn_in[0], swapped(ffn_in[0], "tensor", 1))
    down = (ffn_out[0], swapped(ffn_out[0], "tensor", 1))
    small = jnp.concatenate([head_bias.reshape(-1), ffn_bias, position_bias.reshape(-1)])
    small_oth = swapped(small, "tensor", 1)
    near_heads = head_bias.size
    near_ffn = near_heads + ffn_bias.size
    both_small = jnp.stack([small, small_oth])
    head_both = both_small[:, :near_heads].reshape(2, 2, -1)
    ffn_both = jnp.where(leading, both_small[:, near_heads:near_ffn], 0.0).reshape(1, -1)
    table_both = jnp.where(leading, 0.0, both_small[:, near_ffn:]).reshape(2 * heads, bucket_count)
    q_shift = head_both[:, 0].reshape(1, -1)
    v_shift = head_both[:, 1].reshape(1, -1)
    qkv_shift = jnp.where(
        leading, jnp.concatenate([q_shift, jnp.zeros_like(q_shift), v_shift], axis=1), 0.0
    )
    gains = jnp.where(leading, norm_gain[0], norm_gain[1])
    entry_gain = gains[0:1]

    near = length - 1 - 3 * QB
    near_hits = (buckets[None, near : near + 6 * QB] == jnp.arange(bucket_count)[:, None]).astype(F32)
    bias = toeplitz(jnp.dot(table_both, near_hits, precision=lax.Precision.HIGHEST))

    window = rows + REACH
    base = core * (length - window)
    segments = jnp.pad(
        lax.dynamic_slice_in_dim(segment_ids[:, 0], base, window, axis=1),
        ((0, 0), (PAD * QB, PAD * QB)),
        constant_values=-1,
    )
    reach_blocks = REACH // QB
    own_block = PAD + core * reach_blocks
    halo_block = jnp.where(core == 0, PAD + rows // QB, PAD)
    edge = jnp.where(core == 0, rows - REACH, 0)

    def info_of(slot):
        return jnp.stack([lead, slot, own_block, halo_block, edge]).astype(jnp.int32)

    received = jnp.zeros((rows, width), LOW)
    entered = attended = fed = None
    delivered = []
    for moment in range(micro_count + 1):
        slot = jnp.where(leading, moment, (moment + micro_count) % (micro_count + 1))
        info = info_of(slot)
        micro = jnp.minimum(slot, micro_count - 1)
        own_rows = layer_input[min(moment, micro_count - 1), 0]
        row_segments = lax.dynamic_index_in_dim(segments, micro, 0, keepdims=False)
        *entered, halo = enter(info, own_rows, received, entry_gain, qkv_shift, qkv_own, qkv_oth, entered)
        halo = swapped(halo, "tensor", 1)
        attended = attend(info, row_segments, entered[2], halo, bias, attended)
        *fed, result = feed(
            info, entered[0], attended[0], wo, up, down, ffn_both, gains, bert_shift, fed
        )
        if moment < micro_count:
            received = lax.ppermute(result, "section", [(0, 1)])
        if moment >= 1:
            delivered.append(
                jnp.where(leading, lax.ppermute(result, "section", [(1, 0)]), result)
            )
    x_saved, e_saved, qkv_saved = entered
    context, lse, *halo_saved = attended
    f_saved, slope_saved, n_saved, one_saved, two_saved = fed

    received = jnp.zeros((rows, width), LOW)
    feed_kept = table_kept = entry_kept = None
    input_low = []
    input_lower = []
    for moment in range(micro_count + 1):
        slot = jnp.where(leading, (moment + micro_count) % (micro_count + 1), moment)
        info = info_of(slot)
        micro = jnp.minimum(slot, micro_count - 1)
        at = min(moment, micro_count - 1)
        row_segments = lax.dynamic_index_in_dim(segments, micro, 0, keepdims=False)
        *feed_kept, dz, grad_context = feed_back(
            info, received, decoder_grads[0, at, 0], remote_grads[at], one_saved, two_saved, slope_saved,
            wo, up, down, gains, feed_kept,
        )
        if moment == micro_count:
            dy_saved, du_saved, db_saved, stat_feed, stat_bias = feed_kept
            down_own, down_oth = tall_grad(f_saved, dy_saved, 512, pieces, "down_grad")
            ffn_each = du_saved.shape[2] // 2 // 512
            up_own, up_oth = wide_grad(
                n_saved, du_saved, 512, lambda j: lax.rem(j, 2) * ffn_each + j // 2, "up_grad"
            )
            grad_context, down_oth, up_oth = lax.optimization_barrier((grad_context, down_oth, up_oth))
            down_got = swapped(down_oth, "tensor", 1)
            up_got = swapped(up_oth, "tensor", 1)
            down_sum = scattered(down_own, down_got)
            up_sum = scattered(
                up_own.reshape(pieces, width // pieces, -1), up_got.reshape(pieces, width // pieces, -1)
            )
        dq, dk, dv, table_kept, far = attend_back(
            info, row_segments, qkv_saved, halo_saved, grad_context, bias, lse, table_kept
        )
        far = swapped(far, "tensor", 1)
        *entry_kept, low, lower = enter_back(
            info, dq, dk, dv, far, x_saved, dz, qkv_own, qkv_oth, entry_gain, entry_kept
        )
        if moment >= 1:
            input_low.append(low)
            input_lower.append(lower)
        if moment < micro_count:
            received = lax.ppermute(low, "section", [(1, 0)])
    dqkv_saved, stat_entry = entry_kept

    out_own, out_oth = tall_grad(context, db_saved, 512, pieces, "out_grad")
    qkv_sum_own, qkv_sum_oth = wide_grad(e_saved, dqkv_saved, 512, lambda j: j, "qkv_grad")
    out_sum = scattered(out_own, swapped(out_oth, "tensor", 1))
    shape = (pieces, width // pieces, -1)
    qkv_sum = scattered(qkv_sum_own.reshape(shape), swapped(qkv_sum_oth, "tensor", 1).reshape(shape))

    half = width // 2
    upper = lax.ppermute(jnp.stack(input_low)[:, :, half:], "section", [(0, 1)]).astype(F32)
    input_grad = jnp.where(leading, jnp.stack(input_lower), upper)[:, None]

    near_table = jnp.dot(diagonals(table_kept, micro_count), near_hits.T, precision=lax.Precision.HIGHEST)

    def placed(pair):
        return jnp.where(core == 0, pair, pair[::-1])

    stat_feed = stat_feed[0] + stat_feed[1]
    stat_entry = stat_entry[0] + stat_entry[1]
    gain_first = jnp.where(leading, stat_feed[0:1], stat_entry[2:3])
    gain_rows = jnp.concatenate([gain_first, stat_feed[1:2]])
    nothing = jnp.zeros_like(gain_rows)
    gain_all = jnp.where(leading, jnp.concatenate([gain_rows, nothing]), jnp.concatenate([nothing, gain_rows]))
    shift_all = jnp.where(leading, stat_feed[2:6], 0.0)
    head_all = jnp.where(leading, stat_entry[0:2], 0.0).reshape(2, 2, -1)
    head_all = placed(jnp.moveaxis(head_all, 1, 0))
    bias_all = placed(jnp.where(leading, stat_bias[0] + stat_bias[1], 0.0).reshape(2, -1))
    table_all = placed(jnp.where(leading, 0.0, near_table).reshape(2, heads, bucket_count))
    parts = [gain_all, shift_all, head_all, bias_all, table_all]
    packed = jnp.concatenate([part.reshape(-1) for part in parts])
    packed = packed + swapped(packed, "tensor", 1)
    packed = packed + swapped(packed, "dp", 1)
    packed = packed + swapped(packed, "section", 1)
    packed = packed + swapped(packed, "dp", 2)
    packed = packed + swapped(packed, "dp", 4)
    unpacked = []
    start = 0
    for part in parts:
        unpacked.append(packed[start : start + part.size].reshape(part.shape))
        start += part.size
    gain_all, shift_all, head_all, bias_all, table_all = unpacked
    mine = lambda value: lax.dynamic_index_in_dim(value, core, 0, keepdims=False)
    return (
        jnp.stack(delivered)[None, :, None],
        input_grad,
        qkv_sum.reshape(1, width // pieces, 3, -1),
        out_sum[None],
        up_sum[None],
        down_sum[None],
        gain_all.reshape(norm_gain.shape),
        shift_all,
        mine(head_all),
        mine(bias_all),
        mine(table_all),
    )


def solution(mesh):
    placed = (
        P(None, "dp", "tensor", None),
        P(None, "dp", None),
        P(),
        P("section", None, None, "tensor"),
        P("section", "tensor", None),
        P("section", None, "tensor"),
        P("section", "tensor", None),
        P(),
        P(),
        P(None, "tensor"),
        P("tensor"),
        P("tensor", None),
        P("section", None, "dp", "tensor", None),
    )
    paired = mesh.shape["tensor"] == 2 and mesh.shape["dp"] == 8
    return jax.shard_map(
        paired_body if paired else general_body,
        mesh=mesh,
        in_specs=placed,
        out_specs=(
            P("section", None, "dp", "tensor", None),
            P(None, "dp", "tensor", "section"),
            P("section", "dp", None, "tensor"),
            P("section", "tensor", "dp"),
            P("section", "dp", "tensor"),
            P("section", "tensor", "dp"),
            P(),
            P(),
            P(None, "tensor"),
            P("tensor"),
            P("tensor", None),
        ),
        check_vma=False,
    )
```

profile of v0, /device:TPU:0, one launch (start us, length us, event | category | flops | bytes accessed | tf_op | source)
XLA Modules:
  0.0 862.4 jit_solution(15965015050409515573)
XLA Ops:
  0.7 4.7 copy.78
  5.3 3.2 copy.80.refs_5_.refs_7_
  14.1 4.0 collective-permute-done
  20.0 9.1 %enter.3 = (bf16[3,512,1024]{2,1,0:T(8,128)(2,1)}, bf16[3,512,1024]{2,1,0:T(8,128)(2,1)}, bf16[3,512,3072]{2,1,0:T(8,128)(2,1)}, bf16[256,2048]{1,0:T(8,128)(2,1)}) custom-call(s32[5]{0:T(128)} %stack.108.refs_0_, bf16[512,1024]{1,0:T(8,128)(2,1)} %get-tuple-element.247.refs_1_, bf16[512,1024]{1,0:T(8,128)(2,1)} %broadcast_1_refs_2__refs_1_.2.refs_2_.refs_1_, ...), custom_call_target="tpu_custom_call" | custom-call | tf_op jit(solution)/shard_map/enter/pallas_call | solution.py:50
  31.9 6.7 toeplitz.1.refs_6_.refs_7_
  40.2 22.6 %attend.3 = (bf16[3,512,1024]{2,1,0:T(8,128)(2,1)}, f32[3,8,4,256]{3,2,1,0:T(4,128)}, bf16[3,256,1024]{2,1,0:T(8,128)(2,1)}, bf16[3,256,1024]{2,1,0:T(8,128)(2,1)}) custom-call(s32[5]{0:T(128)} %stack.108.refs_0_, s32[1280]{0:T(1024)} %get-tuple-element.238.refs_1_, s32[10,128]{1,0:T(8,128)} %bitcast.209, ...), custom_call_target="tpu_custom_call" | custom-call | tf_op jit(solution)/shard_map/attend/pallas_call | solution.py:50
  63.8 29.9 %feed.3 = (bf16[3,512,4096]{2,1,0:T(8,128)(2,1)}, bf16[3,512,4096]{2,1,0:T(8,128)(2,1)}, bf16[3,512,1024]{2,1,0:T(8,128)(2,1)}, f32[3,512,1024]{2,1,0:T(8,128)},...) custom-call(s32[5]{0:T(128)} %stack.108.refs_0_, bf16[3,512,1024]{2,1,0:T(8,128)(2,1)} %get-tuple-element.111.refs_1_.refs_7_, ...), custom_call_target="tpu_custom_call" | custom-call | tf_op jit(solution)/shard_map/feed/pallas_call | solution.py:50
  93.7 4.6 collective-permute-start.6
  98.9 21.2 %collective-permute-done.6.refs_2_ = bf16[512,1024]{1,0:T(8,128)(2,1)S(1)} collective-permute-done((bf16[512,1024]{1,0:T(8,128)(2,1)}, bf16[512,1024]{1,0:T(8,128)(2,1)S(1)}, u32[]{:S(2)}, u32[]{:S(2)}) %collective-permute-start.6) | collective-permute-done | bytes 1048608 | tf_op jit(solution)/shard_map/ppermute | solution.py:1356
  121.1 9.2 %enter.4 = (bf16[3,512,1024]{2,1,0:T(8,128)(2,1)}, bf16[3,512,1024]{2,1,0:T(8,128)(2,1)}, bf16[3,512,3072]{2,1,0:T(8,128)(2,1)}, bf16[256,2048]{1,0:T(8,128)(2,1)}) custom-call(s32[5]{0:T(128)} %stack.106.refs_0_, bf16[512,1024]{1,0:T(8,128)(2,1)} %get-tuple-element.248.refs_1_, ...), custom_call_target="tpu_custom_call", output_to_operand_aliasing={{0}: (7, {}), {1}: (8, {}), {2}: (9, {})} | custom-call | tf_op jit(solution)/shard_map/enter/pallas_call | solution.py:50
  135.9 22.6 %attend.4 = (bf16[3,512,1024]{2,1,0:T(8,128)(2,1)}, f32[3,8,4,256]{3,2,1,0:T(4,128)}, bf16[3,256,1024]{2,1,0:T(8,128)(2,1)}, bf16[3,256,1024]{2,1,0:T(8,128)(2,1)}) custom-call(s32[5]{0:T(128)} %stack.106.refs_0_, s32[1280]{0:T(1024)} %get-tuple-element.234.refs_1_, ...), custom_call_target="tpu_custom_call", output_to_operand_aliasing={{0}: (9, {}), {1}: (10, {}), {2}: (11, {}), {3}: (12, {})} | custom-call | tf_op jit(solution)/shard_map/attend/pallas_call | solution.py:50
  158.5 29.5 %feed.4 = (bf16[3,512,4096]{2,1,0:T(8,128)(2,1)}, bf16[3,512,4096]{2,1,0:T(8,128)(2,1)}, bf16[3,512,1024]{2,1,0:T(8,128)(2,1)}, f32[3,512,1024]{2,1,0:T(8,128)},...) custom-call(s32[5]{0:T(128)} %stack.106.refs_0_, ...), custom_call_target="tpu_custom_call", output_to_operand_aliasing={{0}: (12, {}), {1}: (13, {}), {2}: (14, {}), {3}: (15, {}),... | custom-call | tf_op jit(solution)/shard_map/feed/pallas_call | solution.py:50
  188.0 3.7 collective-permute-start.9
  192.4 21.0 %collective-permute-done.9.refs_2_ = bf16[512,1024]{1,0:T(8,128)(2,1)S(1)} collective-permute-done((bf16[512,1024]{1,0:T(8,128)(2,1)}, bf16[512,1024]{1,0:T(8,128)(2,1)S(1)}, u32[]{:S(2)}, u32[]{:S(2)}) %collective-permute-start.9) | collective-permute-done | bytes 1048608 | tf_op jit(solution)/shard_map/ppermute | solution.py:1356
  214.3 9.4 %enter.5 = (bf16[3,512,1024]{2,1,0:T(8,128)(2,1)}, bf16[3,512,1024]{2,1,0:T(8,128)(2,1)}, bf16[3,512,3072]{2,1,0:T(8,128)(2,1)}, bf16[256,2048]{1,0:T(8,128)(2,1)}) custom-call(s32[5]{0:T(128)} %stack.114.refs_0_, bf16[512,1024]{1,0:T(8,128)(2,1)} %get-tuple-element.248.refs_1_, ...), custom_call_target="tpu_custom_call", output_to_operand_aliasing={{0}: (7, {}), {1}: (8, {}), {2}: (9, {})} | custom-call | tf_op jit(solution)/shard_map/enter/pallas_call | solution.py:50
  226.3 5.3 collective-permute-start.12
  233.1 22.7 %attend.5 = (bf16[3,512,1024]{2,1,0:T(8,128)(2,1)}, f32[3,8,4,256]{3,2,1,0:T(4,128)}, bf16[3,256,1024]{2,1,0:T(8,128)(2,1)}, bf16[3,256,1024]{2,1,0:T(8,128)(2,1)}) custom-call(s32[5]{0:T(128)} %stack.114.refs_0_, s32[1280]{0:T(1024)} %get-tuple-element.235.refs_1_, ...), custom_call_target="tpu_custom_call", output_to_operand_aliasing={{0}: (9, {}), {1}: (10, {}), {2}: (11, {}), {3}: (12, {})} | custom-call | tf_op jit(solution)/shard_map/attend/pallas_call | solution.py:50
  255.8 29.5 %feed.5 = (bf16[3,512,4096]{2,1,0:T(8,128)(2,1)}, bf16[3,512,4096]{2,1,0:T(8,128)(2,1)}, bf16[3,512,1024]{2,1,0:T(8,128)(2,1)}, f32[3,512,1024]{2,1,0:T(8,128)},...) custom-call(s32[5]{0:T(128)} %stack.114.refs_0_, ...), custom_call_target="tpu_custom_call", output_to_operand_aliasing={{0}: (12, {}), {1}: (13, {}), {2}: (14, {}), {3}: (15, {}),... | custom-call | tf_op jit(solution)/shard_map/feed/pallas_call | solution.py:50
  285.3 27.4 %feed_back.3 = (bf16[3,512,1024]{2,1,0:T(8,128)(2,1)}, bf16[3,512,4096]{2,1,0:T(8,128)(2,1)}, bf16[3,512,1024]{2,1,0:T(8,128)(2,1)}, f32[3,8,1024]{2,1,0:T(8,128...) custom-call(s32[5]{0:T(128)} %stack.120.refs_0_, ...), custom_call_target="tpu_custom_call" | custom-call | tf_op jit(solution)/shard_map/feed_back/pallas_call | solution.py:50
  312.7 24.3 %attend_back.3 = (bf16[512,1024]{1,0:T(8,128)(2,1)}, bf16[512,1024]{1,0:T(8,128)(2,1)}, bf16[512,1024]{1,0:T(8,128)(2,1)}, f32[3,8,640,256]{3,2,1,0:T(8,128)}, bf16[2,256,1024]{2,1,0:T(8,128)(2,1)}) custom-call(s32[5]{0:T(128)} %stack.120.refs_0_, s32[1280]{0:T(1024)} %get-tuple-element.233.refs_1_, s32[10,128]{1,0:T(8,128)} %bitcast.210, ...), custom_call_target="tpu_custom_call" | custom-call | tf_op jit(solution)/shard_map/attend_back/pallas_call | solution.py:50
  337.0 5.5 collective-permute-start.13
  346.0 12.0 %enter_back.3 = (bf16[3,512,3072]{2,1,0:T(8,128)(2,1)}, f32[3,8,1024]{2,1,0:T(8,128)}, bf16[512,1024]{1,0:T(8,128)(2,1)}, f32[512,512]{1,0:T(8,128)}) custom-call(s32[5]{0:T(128)} %stack.120.refs_0_, bf16[512,1024]{1,0:T(8,128)(2,1)} %get-tuple-element.151.refs_1_, bf16[512,1024]{1,0:T(8,128)(2,1)} %get-tuple-element.152.refs_2_, ...), custom_call_target="tpu_custom_call" | custom-call | tf_op jit(solution)/shard_map/enter_back/pallas_call | solution.py:50
  359.8 6.8 collective-permute-done.15.refs_3_
  366.7 18.8 %collective-permute-done.14.refs_1_ = bf16[512,1024]{1,0:T(8,128)(2,1)S(1)} collective-permute-done((bf16[512,1024]{1,0:T(8,128)(2,1)}, bf16[512,1024]{1,0:T(8,128)(2,1)S(1)}, u32[]{:S(2)}, u32[]{:S(2)}) %collective-permute-start.14) | collective-permute-done | bytes 1048608 | tf_op jit(solution)/shard_map/ppermute | solution.py:1404
  386.4 26.9 %feed_back.4 = (bf16[3,512,1024]{2,1,0:T(8,128)(2,1)}, bf16[3,512,4096]{2,1,0:T(8,128)(2,1)}, bf16[3,512,1024]{2,1,0:T(8,128)(2,1)}, f32[3,8,1024]{2,1,0:T(8,128...) custom-call(s32[5]{0:T(128)} %stack.118.refs_0_, ...), custom_call_target="tpu_custom_call", output_to_operand_aliasing={{0}: (14, {}), {1}: (15, {}), {2}: (16, {}), {3}: (17, {}),... | custom-call | tf_op jit(solution)/shard_map/feed_back/pallas_call | solution.py:50
  413.4 24.4 %attend_back.4 = (bf16[512,1024]{1,0:T(8,128)(2,1)}, bf16[512,1024]{1,0:T(8,128)(2,1)}, bf16[512,1024]{1,0:T(8,128)(2,1)}, f32[3,8,640,256]{3,2,1,0:T(8,128)}, bf16[2,256,1024]{2,1,0:T(8,128)(2,1)}) custom-call(s32[5]{0:T(128)} %stack.118.refs_0_, s32[1280]{0:T(1024)} %get-tuple-element.236.refs_1_, ...), custom_call_target="tpu_custom_call", output_to_operand_aliasing={{3}: (11, {})} | custom-call | tf_op jit(solution)/shard_map/attend_back/pallas_call | solution.py:50
  443.9 12.2 %enter_back.4 = (bf16[3,512,3072]{2,1,0:T(8,128)(2,1)}, f32[3,8,1024]{2,1,0:T(8,128)}, bf16[512,1024]{1,0:T(8,128)(2,1)}, f32[512,512]{1,0:T(8,128)}) custom-call(s32[5]{0:T(128)} %stack.118.refs_0_, bf16[512,1024]{1,0:T(8,128)(2,1)} %get-tuple-element.164.refs_1_, ...), custom_call_target="tpu_custom_call", output_to_operand_aliasing={{0}: (10, {}), {1}: (11, {})} | custom-call | tf_op jit(solution)/shard_map/enter_back/pallas_call | solution.py:50
  458.0 10.3 %collective-permute-done.8 = bf16[512,1024]{1,0:T(8,128)(2,1)} collective-permute-done((bf16[512,1024]{1,0:T(8,128)(2,1)S(1)}, bf16[512,1024]{1,0:T(8,128)(2,1)}, u32[]{:S(2)}, u32[]{:S(2)}) %collective-permute-start.8) | collective-permute-done | bytes 1048608 | tf_op jit(solution)/shard_map/ppermute | solution.py:1359
  471.1 19.7 %collective-permute-done.17.refs_1_ = bf16[512,1024]{1,0:T(8,128)(2,1)S(1)} collective-permute-done((bf16[512,1024]{1,0:T(8,128)(2,1)}, bf16[512,1024]{1,0:T(8,128)(2,1)S(1)}, u32[]{:S(2)}, u32[]{:S(2)}) %collective-permute-start.17) | collective-permute-done | bytes 1048608 | tf_op jit(solution)/shard_map/ppermute | solution.py:1404
  491.7 26.8 %feed_back.5 = (bf16[3,512,1024]{2,1,0:T(8,128)(2,1)}, bf16[3,512,4096]{2,1,0:T(8,128)(2,1)}, bf16[3,512,1024]{2,1,0:T(8,128)(2,1)}, f32[3,8,1024]{2,1,0:T(8,128...) custom-call(s32[5]{0:T(128)} %stack.123.refs_0_, ...), custom_call_target="tpu_custom_call", output_to_operand_aliasing={{0}: (14, {}), {1}: (15, {}), {2}: (16, {}), {3}: (17, {}),... | custom-call | tf_op jit(solution)/shard_map/feed_back/pallas_call | solution.py:50
  518.6 16.4 %down_grad.1 = (bf16[8,2048,128]{2,1,0:T(8,128)(2,1)}, bf16[8,2048,128]{2,1,0:T(8,128)(2,1)}) custom-call(bf16[3,512,4096]{2,1,0:T(8,128)(2,1)} %get-tuple-element.179.left_ref, bf16[3,512,1024]{2,1,0:T(8,128)(2,1)} %get-tuple-element.180.right_ref), custom_call_target="tpu_custom_call" | custom-call | tf_op jit(solution)/shard_map/down_grad/pallas_call | solution.py:883
  535.0 16.7 %up_grad.1 = (bf16[1024,2048]{1,0:T(8,128)(2,1)}, bf16[1024,2048]{1,0:T(8,128)(2,1)}) custom-call(bf16[3,512,1024]{2,1,0:T(8,128)(2,1)} %get-tuple-element.182.left_ref, bf16[3,512,4096]{2,1,0:T(8,128)(2,1)} %get-tuple-element.183.right_ref), custom_call_target="tpu_custom_call" | custom-call | tf_op jit(solution)/shard_map/up_grad/pallas_call | solution.py:842
  551.7 24.5 %attend_back.5 = (bf16[512,1024]{1,0:T(8,128)(2,1)}, bf16[512,1024]{1,0:T(8,128)(2,1)}, bf16[512,1024]{1,0:T(8,128)(2,1)}, f32[3,8,640,256]{3,2,1,0:T(8,128)}, bf16[2,256,1024]{2,1,0:T(8,128)(2,1)}) custom-call(s32[5]{0:T(128)} %stack.123.refs_0_, s32[1280]{0:T(1024)} %get-tuple-element.237.refs_1_, ...), custom_call_target="tpu_custom_call", output_to_operand_aliasing={{3}: (11, {})} | custom-call | tf_op jit(solution)/shard_map/attend_back/pallas_call | solution.py:50
  577.4 6.2 out_grad.1
  584.7 10.7 %diagonals.1 = f32[8,2,768]{2,1,0:T(2,128)} custom-call(f32[3,8,640,256]{3,2,1,0:T(8,128)} %get-tuple-element.210.a_ref), custom_call_target="tpu_custom_call" | custom-call | tf_op jit(solution)/shard_map/diagonals/pallas_call | solution.py:114
  597.5 11.7 %enter_back.5 = (bf16[3,512,3072]{2,1,0:T(8,128)(2,1)}, f32[3,8,1024]{2,1,0:T(8,128)}, bf16[512,1024]{1,0:T(8,128)(2,1)}, f32[512,512]{1,0:T(8,128)}) custom-call(s32[5]{0:T(128)} %stack.123.refs_0_, bf16[512,1024]{1,0:T(8,128)(2,1)} %get-tuple-element.187.refs_1_, ...), custom_call_target="tpu_custom_call", output_to_operand_aliasing={{0}: (10, {}), {1}: (11, {})} | custom-call | tf_op jit(solution)/shard_map/enter_back/pallas_call | solution.py:50
  609.3 13.7 %qkv_grad.1 = (bf16[1024,1536]{1,0:T(8,128)(2,1)}, bf16[1024,1536]{1,0:T(8,128)(2,1)}) custom-call(bf16[3,512,1024]{2,1,0:T(8,128)(2,1)} %get-tuple-element.196.left_ref, bf16[3,512,3072]{2,1,0:T(8,128)(2,1)} %get-tuple-element.197.right_ref), custom_call_target="tpu_custom_call" | custom-call | tf_op jit(solution)/shard_map/qkv_grad/pallas_call | solution.py:842
  625.3 3.3 collective-permute-done.36
  629.4 3.5 collective-permute-done.37
  642.3 4.5 collective-permute-start.40
  649.0 3.3 collective-permute-start.19
  673.4 5.4 add_convert_fusion.1
  682.2 3.3 add_convert_fusion
  695.8 14.2 %collective-permute-done.21 = bf16[2,2,128,1536]{2,3,0,1:T(8,128)(2,1)} collective-permute-done((bf16[2,2,128,1536]{2,3,0,1:T(8,128)(2,1)}, bf16[2,2,128,1536]{2,3,0,1:T(8,128)(2,1)}, u32[]{:S(2)}, u32[]{:S(2)}) %collective-permute-start.21) | collective-permute-done | bytes 1572896 | tf_op jit(solution)/shard_map/ppermute | solution.py:1249
  714.4 40.5 %collective-permute-done.29 = bf16[2,2,128,2048]{3,2,0,1:T(8,128)(2,1)} collective-permute-done((bf16[2,2,128,2048]{3,2,0,1:T(8,128)(2,1)}, bf16[2,2,128,2048]{3,2,0,1:T(8,128)(2,1)}, u32[]{:S(2)}, u32[]{:S(2)}) %collective-permute-start.29) | collective-permute-done | bytes 2097184 | tf_op jit(solution)/shard_map/ppermute | solution.py:1249
  759.7 34.3 %collective-permute-done.33 = bf16[2,2,2048,128]{3,2,0,1:T(8,128)(2,1)} collective-permute-done((bf16[2,2,2048,128]{3,2,0,1:T(8,128)(2,1)}, bf16[2,2,2048,128]{3,2,0,1:T(8,128)(2,1)}, u32[]{:S(2)}, u32[]{:S(2)}) %collective-permute-start.33) | collective-permute-done | bytes 2097184 | tf_op jit(solution)/shard_map/ppermute | solution.py:1249
  802.7 32.7 %collective-permute-done.34 = bf16[2,2048,128]{2,1,0:T(8,128)(2,1)S(1)} collective-permute-done((bf16[2,2048,128]{2,1,0:T(8,128)(2,1)S(1)}, bf16[2,2048,128]{2,1,0:T(8,128)(2,1)S(1)}, u32[]{:S(2)}, u32[]{:S(2)}) %collective-permute-start.34) | collective-permute-done | bytes 1048608 | tf_op jit(solution)/shard_map/ppermute | solution.py:1249
  838.9 21.2 %collective-permute-done.35 = bf16[2048,128]{1,0:T(8,128)(2,1)} collective-permute-done((bf16[2048,128]{1,0:T(8,128)(2,1)}, bf16[2048,128]{1,0:T(8,128)(2,1)}, u32[]{:S(2)}, u32[]{:S(2)}) %collective-permute-start.35) | collective-permute-done | bytes 524320 | tf_op jit(solution)/shard_map/ppermute | solution.py:1249
  (250 shorter events, 120.4 us)
Async XLA Ops:
  0.6 29.0 %copy-start = (s32[2,1,1024]{2,1,0:T(1,128)S(1)}, s32[2,1,1024]{2,1,0:T(1,128)}, u32[]{:S(2)}) copy-start(s32[2,1,1024]{2,1,0:T(1,128)} %param.14) | copy-start | bytes 24580
  8.6 10.2 %collective-permute-start.1 = (bf16[1024,1536]{1,0:T(8,128)(2,1)S(1)}, bf16[1024,1536]{1,0:T(8,128)(2,1)}, u32[]{:S(2)}, u32[]{:S(2)}) collective-permute-start(bf16[1024,1536]{1,0:T(8,128)(2,1)S(1)} %copy.80.refs_5_.refs_7_), channel_id=1, source_target_pairs={{0,1},{1,0},{2,3},{3,2},{4,5},{5,4},{6,7},{7,6},{8,9},{9,8},{10,11... | collective-permute-start | bytes 9437192 | tf_op jit(solution)/shard_map/ppermute | solution.py:1249
  9.1 53.7 %collective-permute-start.4 = (bf16[1024,2048]{1,0:T(8,128)(2,1)}, bf16[1024,2048]{1,0:T(8,128)(2,1)}, u32[]{:S(2)}, u32[]{:S(2)}) collective-permute-start(bf16[1024,2048]{1,0:T(8,128)(2,1)} %bitcast.178), channel_id=1, source_target_pairs={{0,1},{1,0},{2,3},{3,2},{4,5},{5,4},{6,7},{7,6},{8,9},{9,8},{10,11... | collective-permute-start | bytes 12582920 | tf_op jit(solution)/shard_map/ppermute | solution.py:1249
  9.2 53.7 %collective-permute-start.5 = (bf16[2048,1024]{1,0:T(8,128)(2,1)}, bf16[2048,1024]{1,0:T(8,128)(2,1)}, u32[]{:S(2)}, u32[]{:S(2)}) collective-permute-start(bf16[2048,1024]{1,0:T(8,128)(2,1)} %bitcast.185), channel_id=1, source_target_pairs={{0,1},{1,0},{2,3},{3,2},{4,5},{5,4},{6,7},{7,6},{8,9},{9,8},{10,11... | collective-permute-start | bytes 12582920 | tf_op jit(solution)/shard_map/ppermute | solution.py:1249
  9.7 8.4 collective-permute-start
  29.1 10.1 %collective-permute-start.2 = (bf16[256,2048]{1,0:T(8,128)(2,1)}, bf16[256,2048]{1,0:T(8,128)(2,1)S(1)}, u32[]{:S(2)}, u32[]{:S(2)}) collective-permute-start(bf16[256,2048]{1,0:T(8,128)(2,1)} %get-tuple-element.113), channel_id=1, source_target_pairs={{0,1},{1,0},{2,3},{3,2},{4,5},{5,4},{6,7},{7,6},{8,9},{9,8},{10,11... | collective-permute-start | bytes 3145736 | tf_op jit(solution)/shard_map/ppermute | solution.py:1249
  29.5 33.3 %collective-permute-start.3 = (bf16[512,1024]{1,0:T(8,128)(2,1)}, bf16[512,1024]{1,0:T(8,128)(2,1)S(1)}, u32[]{:S(2)}, u32[]{:S(2)}) collective-permute-start(bf16[512,1024]{1,0:T(8,128)(2,1)} %bitcast.12.refs_3_.refs_7_), channel_id=1, source_target_pairs={{0,1},{1,0},{2,3},{3,2},{4,5},{5,4},{6,7},{7,6},{8,9},{9,8},{10,11... | collective-permute-start | bytes 3145736 | tf_op jit(solution)/shard_map/ppermute | solution.py:1249
  29.7 33.1 %copy-start.32 = (s32[768]{0:T(1024)}, s32[768]{0:T(1024)S(1)}, u32[]{:S(2)}) copy-start(s32[768]{0:T(1024)S(1)} %slice.124) | copy-start | bytes 9220
  93.7 26.4 %collective-permute-start.6 = (bf16[512,1024]{1,0:T(8,128)(2,1)}, bf16[512,1024]{1,0:T(8,128)(2,1)S(1)}, u32[]{:S(2)}, u32[]{:S(2)}) collective-permute-start(bf16[512,1024]{1,0:T(8,128)(2,1)} %get-tuple-element.115), channel_id=1, source_target_pairs={{0,2},{1,3},{4,6},{5,7},{8,10},{9,11},{12,14},{13,15},{16,18},{17,... | collective-permute-start | bytes 3145736 | tf_op jit(solution)/shard_map/ppermute | solution.py:1356
  130.3 4.6 collective-permute-start.7
  188.0 25.3 %collective-permute-start.9 = (bf16[512,1024]{1,0:T(8,128)(2,1)}, bf16[512,1024]{1,0:T(8,128)(2,1)S(1)}, u32[]{:S(2)}, u32[]{:S(2)}) collective-permute-start(bf16[512,1024]{1,0:T(8,128)(2,1)} %get-tuple-element.129), channel_id=1, source_target_pairs={{0,2},{1,3},{4,6},{5,7},{8,10},{9,11},{12,14},{13,15},{16,18},{17,... | collective-permute-start | bytes 3145736 | tf_op jit(solution)/shard_map/ppermute | solution.py:1356
  223.7 8.4 collective-permute-start.10
  226.2 29.6 %copy-start.11 = (bf16[512,1024]{1,0:T(8,128)(2,1)}, bf16[512,1024]{1,0:T(8,128)(2,1)S(1)}, u32[]{:S(2)}) copy-start(bf16[512,1024]{1,0:T(8,128)(2,1)S(1)} %get-tuple-element.246.refs_2_) | copy-start | bytes 3145732
  226.2 116.2 %copy-start.4 = (bf16[512,1024]{1,0:T(8,128)(2,1)}, bf16[512,1024]{1,0:T(8,128)(2,1)S(1)}, u32[]{:S(2)}) copy-start(bf16[512,1024]{1,0:T(8,128)(2,1)S(1)} %get-tuple-element.245.refs_2_) | copy-start | bytes 3145732
  226.3 59.1 %collective-permute-start.12 = (bf16[512,1024]{1,0:T(8,128)(2,1)S(1)}, bf16[512,1024]{1,0:T(8,128)(2,1)}, u32[]{:S(2)}, u32[]{:S(2)}) collective-permute-start(bf16[512,1024]{1,0:T(8,128)(2,1)S(1)} %get-tuple-element.246.refs_2_), channel_id=1, source_target_pairs={{0,2},{1,3},{4,6},{5,7},{8,10},{9,11},{12,14},{13,15},{16,18},{17,... | collective-permute-start | bytes 3145736 | tf_op jit(solution)/shard_map/ppermute | solution.py:1298
  337.0 8.0 collective-permute-start.13
  342.5 24.2 %collective-permute-start.15 = (bf16[512,1024]{1,0:T(8,128)(2,1)S(1)}, bf16[512,1024]{1,0:T(8,128)(2,1)S(1)}, u32[]{:S(2)}, u32[]{:S(2)}) collective-permute-start(bf16[512,1024]{1,0:T(8,128)(2,1)S(1)} %get-tuple-element.245.refs_2_), channel_id=1, source_target_pairs={{0,2},{1,3},{4,6},{5,7},{8,10},{9,11},{12,14},{13,15},{16,18},{17,... | collective-permute-start | bytes 3145736 | tf_op jit(solution)/shard_map/ppermute | solution.py:1298
  357.9 27.5 %collective-permute-start.14 = (bf16[512,1024]{1,0:T(8,128)(2,1)}, bf16[512,1024]{1,0:T(8,128)(2,1)S(1)}, u32[]{:S(2)}, u32[]{:S(2)}) collective-permute-start(bf16[512,1024]{1,0:T(8,128)(2,1)} %get-tuple-element.156), channel_id=1, source_target_pairs={{2,0},{3,1},{6,4},{7,5},{10,8},{11,9},{14,12},{15,13},{18,16},{19,... | collective-permute-start | bytes 3145736 | tf_op jit(solution)/shard_map/ppermute | solution.py:1404
  413.4 27.0 %copy-start.24 = (bf16[512,1024]{1,0:T(8,128)(2,1)S(1)}, bf16[512,1024]{1,0:T(8,128)(2,1)}, u32[]{:S(2)}) copy-start(bf16[512,1024]{1,0:T(8,128)(2,1)} %get-tuple-element.129) | copy-start | bytes 3145732
  437.8 5.1 collective-permute-start.16
  440.4 28.0 %collective-permute-start.8 = (bf16[512,1024]{1,0:T(8,128)(2,1)S(1)}, bf16[512,1024]{1,0:T(8,128)(2,1)}, u32[]{:S(2)}, u32[]{:S(2)}) collective-permute-start(bf16[512,1024]{1,0:T(8,128)(2,1)S(1)} %copy-done.24), channel_id=1, source_target_pairs={{2,0},{3,1},{6,4},{7,5},{10,8},{11,9},{14,12},{15,13},{18,16},{19,... | collective-permute-start | bytes 3145736 | tf_op jit(solution)/shard_map/ppermute | solution.py:1359
  456.1 34.7 %collective-permute-start.17 = (bf16[512,1024]{1,0:T(8,128)(2,1)}, bf16[512,1024]{1,0:T(8,128)(2,1)S(1)}, u32[]{:S(2)}, u32[]{:S(2)}) collective-permute-start(bf16[512,1024]{1,0:T(8,128)(2,1)} %get-tuple-element.172), channel_id=1, source_target_pairs={{2,0},{3,1},{6,4},{7,5},{10,8},{11,9},{14,12},{15,13},{18,16},{19,... | collective-permute-start | bytes 3145736 | tf_op jit(solution)/shard_map/ppermute | solution.py:1404
  469.8 154.0 %collective-permute-start.11 = (bf16[512,1024]{1,0:T(8,128)(2,1)}, bf16[512,1024]{1,0:T(8,128)(2,1)}, u32[]{:S(2)}, u32[]{:S(2)}) collective-permute-start(bf16[512,1024]{1,0:T(8,128)(2,1)} %get-tuple-element.143), channel_id=1, source_target_pairs={{2,0},{3,1},{6,4},{7,5},{10,8},{11,9},{14,12},{15,13},{18,16},{19,... | collective-permute-start | bytes 3145736 | tf_op jit(solution)/shard_map/ppermute | solution.py:1359
  576.2 20.4 %collective-permute-start.18 = (bf16[2,256,1024]{2,1,0:T(8,128)(2,1)}, bf16[2,256,1024]{2,1,0:T(8,128)(2,1)S(1)}, u32[]{:S(2)}, u32[]{:S(2)}) collective-permute-start(bf16[2,256,1024]{2,1,0:T(8,128)(2,1)} %get-tuple-element.190), channel_id=1, source_target_pairs={{0,1},{1,0},{2,3},{3,2},{4,5},{5,4},{6,7},{7,6},{8,9},{9,8},{10,11... | collective-permute-start | bytes 3145736 | tf_op jit(solution)/shard_map/ppermute | solution.py:1249
  583.6 45.5 %collective-permute-start.24 = (bf16[8,512,128]{2,1,0:T(8,128)(2,1)}, bf16[8,512,128]{2,1,0:T(8,128)(2,1)S(1)}, u32[]{:S(2)}, u32[]{:S(2)}) collective-permute-start(bf16[8,512,128]{2,1,0:T(8,128)(2,1)} %get-tuple-element.202), channel_id=1, source_target_pairs={{0,1},{1,0},{2,3},{3,2},{4,5},{5,4},{6,7},{7,6},{8,9},{9,8},{10,11... | collective-permute-start | bytes 3145736 | tf_op jit(solution)/shard_map/ppermute | solution.py:1249
  583.6 89.8 %collective-permute-start.28 = (bf16[1024,2048]{1,0:T(8,128)(2,1)}, bf16[1024,2048]{1,0:T(8,128)(2,1)}, u32[]{:S(2)}, u32[]{:S(2)}) collective-permute-start(bf16[1024,2048]{1,0:T(8,128)(2,1)} %get-tuple-element.204), channel_id=1, source_target_pairs={{0,1},{1,0},{2,3},{3,2},{4,5},{5,4},{6,7},{7,6},{8,9},{9,8},{10,11... | collective-permute-start | bytes 12582920 | tf_op jit(solution)/shard_map/ppermute | solution.py:1249
  623.0 43.5 %collective-permute-start.20 = (bf16[1024,1536]{1,0:T(8,128)(2,1)}, bf16[1024,1536]{1,0:T(8,128)(2,1)}, u32[]{:S(2)}, u32[]{:S(2)}) collective-permute-start(bf16[1024,1536]{1,0:T(8,128)(2,1)} %get-tuple-element.199), channel_id=1, source_target_pairs={{0,1},{1,0},{2,3},{3,2},{4,5},{5,4},{6,7},{7,6},{8,9},{9,8},{10,11... | collective-permute-start | bytes 9437192 | tf_op jit(solution)/shard_map/ppermute | solution.py:1249
  623.3 5.3 collective-permute-start.36
  625.2 56.7 %collective-permute-start.32 = (bf16[8,2048,128]{2,1,0:T(8,128)(2,1)}, bf16[8,2048,128]{2,1,0:T(8,128)(2,1)}, u32[]{:S(2)}, u32[]{:S(2)}) collective-permute-start(bf16[8,2048,128]{2,1,0:T(8,128)(2,1)} %get-tuple-element.206), channel_id=1, source_target_pairs={{0,1},{1,0},{2,3},{3,2},{4,5},{5,4},{6,7},{7,6},{8,9},{9,8},{10,11... | collective-permute-start | bytes 12582920 | tf_op jit(solution)/shard_map/ppermute | solution.py:1249
  628.6 4.4 collective-permute-start.37
  633.0 4.3 collective-permute-start.38
  634.7 18.3 %collective-permute-start.25 = (bf16[2,2,512,128]{3,2,0,1:T(8,128)(2,1)}, bf16[2,2,512,128]{3,2,0,1:T(8,128)(2,1)}, u32[]{:S(2)}, u32[]{:S(2)}) collective-permute-start(bf16[2,2,512,128]{3,2,0,1:T(8,128)(2,1)} %bitcast.176), channel_id=1, source_target_pairs={{0,4},{4,0},{8,12},{12,8},{16,20},{20,16},{24,28},{28,24},{1,5},{5... | collective-permute-start | bytes 1572872 | tf_op jit(solution)/shard_map/ppermute | solution.py:1249
  637.2 5.0 collective-permute-start.39
  642.3 6.7 collective-permute-start.40
  649.0 41.3 %collective-permute-start.19 = (bf16[2,512,512]{2,1,0:T(8,128)(2,1)}, bf16[2,512,512]{2,1,0:T(8,128)(2,1)}, u32[]{:S(2)}, u32[]{:S(2)}) collective-permute-start(bf16[2,512,512]{2,1,0:T(8,128)(2,1)} %pad_maximum_fusion), channel_id=1, source_target_pairs={{0,2},{1,3},{4,6},{5,7},{8,10},{9,11},{12,14},{13,15},{16,18},{17,... | collective-permute-start | bytes 3145736 | tf_op jit(solution)/shard_map/ppermute | solution.py:1414
  655.2 6.5 collective-permute-start.26
  663.5 26.1 %collective-permute-start.27 = (bf16[512,128]{1,0:T(8,128)(2,1)}, bf16[512,128]{1,0:T(8,128)(2,1)S(1)}, u32[]{:S(2)}, u32[]{:S(2)}) collective-permute-start(bf16[512,128]{1,0:T(8,128)(2,1)} %dynamic-slice_bitcast_fusion.7), channel_id=1, source_target_pairs={{0,16},{4,20},{8,24},{12,28},{16,0},{20,4},{24,8},{28,12},{1,17},{... | collective-permute-start | bytes 393224 | tf_op jit(solution)/shard_map/ppermute | solution.py:1249
  672.3 37.6 %collective-permute-start.21 = (bf16[2,2,128,1536]{2,3,0,1:T(8,128)(2,1)}, bf16[2,2,128,1536]{2,3,0,1:T(8,128)(2,1)}, u32[]{:S(2)}, u32[]{:S(2)}) collective-permute-start(bf16[2,2,128,1536]{2,3,0,1:T(8,128)(2,1)} %bitcast.34), channel_id=1, source_target_pairs={{0,4},{4,0},{8,12},{12,8},{16,20},{20,16},{24,28},{28,24},{1,5},{5... | collective-permute-start | bytes 4718600 | tf_op jit(solution)/shard_map/ppermute | solution.py:1249
  680.9 74.1 %collective-permute-start.29 = (bf16[2,2,128,2048]{3,2,0,1:T(8,128)(2,1)}, bf16[2,2,128,2048]{3,2,0,1:T(8,128)(2,1)}, u32[]{:S(2)}, u32[]{:S(2)}) collective-permute-start(bf16[2,2,128,2048]{3,2,0,1:T(8,128)(2,1)} %bitcast.175), channel_id=1, source_target_pairs={{0,4},{4,0},{8,12},{12,8},{16,20},{20,16},{24,28},{28,24},{1,5},{5... | collective-permute-start | bytes 6291464 | tf_op jit(solution)/shard_map/ppermute | solution.py:1249
  688.6 105.4 %collective-permute-start.33 = (bf16[2,2,2048,128]{3,2,0,1:T(8,128)(2,1)}, bf16[2,2,2048,128]{3,2,0,1:T(8,128)(2,1)}, u32[]{:S(2)}, u32[]{:S(2)}) collective-permute-start(bf16[2,2,2048,128]{3,2,0,1:T(8,128)(2,1)} %bitcast.174), channel_id=1, source_target_pairs={{0,4},{4,0},{8,12},{12,8},{16,20},{20,16},{24,28},{28,24},{1,5},{5... | collective-permute-start | bytes 6291464 | tf_op jit(solution)/shard_map/ppermute | solution.py:1249
  712.4 85.8 %collective-permute-start.22 = (bf16[2,128,1536]{1,2,0:T(8,128)(2,1)S(1)}, bf16[2,128,1536]{1,2,0:T(8,128)(2,1)S(1)}, u32[]{:S(2)}, u32[]{:S(2)}) collective-permute-start(bf16[2,128,1536]{1,2,0:T(8,128)(2,1)S(1)} %dynamic-slice_bitcast_fusion.2), channel_id=1, source_target_pairs={{0,8},{4,12},{8,0},{12,4},{16,24},{20,28},{24,16},{28,20},{1,9},{5... | collective-permute-start | bytes 2359304 | tf_op jit(solution)/shard_map/ppermute | solution.py:1249
  754.9 39.0 %copy-start.5 = (bf16[2,2,1,2048,128]{4,3,2,1,0:T(8,128)(2,1)S(1)}, bf16[2,2,1,2048,128]{4,3,2,1,0:T(8,128)(2,1)}, u32[]{:S(2)}) copy-start(bf16[2,2,1,2048,128]{4,3,2,1,0:T(8,128)(2,1)} %get-tuple-element.239) | copy-start | bytes 6291460
  757.6 41.2 %collective-permute-start.30 = (bf16[2,128,2048]{2,1,0:T(8,128)(2,1)S(1)}, bf16[2,128,2048]{2,1,0:T(8,128)(2,1)S(1)}, u32[]{:S(2)}, u32[]{:S(2)}) collective-permute-start(bf16[2,128,2048]{2,1,0:T(8,128)(2,1)S(1)} %dynamic-slice_bitcast_fusion.1), channel_id=1, source_target_pairs={{0,8},{4,12},{8,0},{12,4},{16,24},{20,28},{24,16},{28,20},{1,9},{5... | collective-permute-start | bytes 3145736 | tf_op jit(solution)/shard_map/ppermute | solution.py:1249
  796.4 39.0 %collective-permute-start.34 = (bf16[2,2048,128]{2,1,0:T(8,128)(2,1)S(1)}, bf16[2,2048,128]{2,1,0:T(8,128)(2,1)S(1)}, u32[]{:S(2)}, u32[]{:S(2)}) collective-permute-start(bf16[2,2048,128]{2,1,0:T(8,128)(2,1)S(1)} %dynamic-slice_bitcast_fusion), channel_id=1, source_target_pairs={{0,8},{4,12},{8,0},{12,4},{16,24},{20,28},{24,16},{28,20},{1,9},{5... | collective-permute-start | bytes 3145736 | tf_op jit(solution)/shard_map/ppermute | solution.py:1249
  798.4 38.1 %collective-permute-start.23 = (bf16[128,1536]{0,1:T(8,128)(2,1)S(1)}, bf16[128,1536]{0,1:T(8,128)(2,1)S(1)}, u32[]{:S(2)}, u32[]{:S(2)}) collective-permute-start(bf16[128,1536]{0,1:T(8,128)(2,1)S(1)} %dynamic-slice_bitcast_fusion.5), channel_id=1, source_target_pairs={{0,16},{4,20},{8,24},{12,28},{16,0},{20,4},{24,8},{28,12},{1,17},{... | collective-permute-start | bytes 1179656 | tf_op jit(solution)/shard_map/ppermute | solution.py:1249
  800.0 37.7 %collective-permute-start.31 = (bf16[128,2048]{1,0:T(8,128)(2,1)}, bf16[128,2048]{1,0:T(8,128)(2,1)S(1)}, u32[]{:S(2)}, u32[]{:S(2)}) collective-permute-start(bf16[128,2048]{1,0:T(8,128)(2,1)} %dynamic-slice_bitcast_fusion.4), channel_id=1, source_target_pairs={{0,16},{4,20},{8,24},{12,28},{16,0},{20,4},{24,8},{28,12},{1,17},{... | collective-permute-start | bytes 1572872 | tf_op jit(solution)/shard_map/ppermute | solution.py:1249
  836.5 23.5 %collective-permute-start.35 = (bf16[2048,128]{1,0:T(8,128)(2,1)}, bf16[2048,128]{1,0:T(8,128)(2,1)}, u32[]{:S(2)}, u32[]{:S(2)}) collective-permute-start(bf16[2048,128]{1,0:T(8,128)(2,1)} %dynamic-slice_bitcast_fusion.3), channel_id=1, source_target_pairs={{0,16},{4,20},{8,24},{12,28},{16,0},{20,4},{24,8},{28,12},{1,17},{... | collective-permute-start | bytes 1572872 | tf_op jit(solution)/shard_map/ppermute | solution.py:1249
  836.5 25.7 %copy-start.1 = (s32[2,1,1024]{2,1,0:T(1,128)S(1)}, s32[2,1,1024]{2,1,0:T(1,128)}, u32[]{:S(2)}) copy-start(s32[2,1,1024]{2,1,0:T(1,128)} %param.14) | copy-start | bytes 24580
  (31 other events, 185.5 us)
where the time goes:
time: 872 us; the launch traced here: 862 us
  Pallas kernels  445 us (51%)
  waiting for transfers between devices  263 us (30%)
  starting transfers between devices  65.1 us (7%)
  local copies, waits for them, and re-layouts  51.4 us (6%)
  other arithmetic  35.9 us (4%)
    pallas_call x18, Pallas kernels, call_with_slots(): pl.pallas_call(run, grid_spec=pltpu.PrefetchScalarGridSpec(num_scalar_pre...  375 us
    ppermute x32, waiting for transfers between devices, swapped(): return lax.ppermute(value, axis, pairs)  165 us
    ppermute x2, waiting for transfers between devices, paired_body(): received = lax.ppermute(result, 'section', [(0, 1)])  42.2 us
    ppermute x32, starting transfers between devices, swapped(): return lax.ppermute(value, axis, pairs)  41.7 us
    ppermute x2, waiting for transfers between devices, paired_body(): received = lax.ppermute(low, 'section', [(1, 0)])  38.5 us
    pallas_call x2, Pallas kernels, wide_grad(): pl.pallas_call(wide_kernel, grid=(steps,), in_specs=[pl.BlockSpec((2, row...  30.4 us
    pallas_call x2, Pallas kernels, tall_grad(): pl.pallas_call(tall_kernel, grid=(2 * each,), in_specs=[pl.BlockSpec((2,...  22.5 us
    unnamed x93, local copies, waits for them, and re-layouts  21.1 us
  transfers between devices with their start and end apart: 41, of which 21 were waited for; matrix products, arithmetic and copies ran while one was open for 8% of the time, Pallas kernels for 28%

commit v1 on v0

--- a/solution.py
+++ b/solution.py
@@ -12,6 +12,7 @@
 PAD = 2
 REACH = 256
 VMEM = 56 * 1024 * 1024
+TAIL_VMEM = 60 * 1024 * 1024
 LOW = jnp.bfloat16
 F32 = jnp.float32
 
@@ -28,11 +29,17 @@
     return pltpu.CompilerParams(vmem_limit_bytes=VMEM)
 
 
+def cost_of(micros):
+    return pl.CostEstimate(flops=int(micros * 1e9), bytes_accessed=0, transcendentals=0)
+
+
 def slotted(shape, dtype):
     return jax.ShapeDtypeStruct((3,) + shape, dtype)
 
 
-def call_with_slots(kernel, scalars, inputs, in_specs, outputs, out_specs, previous, grid, scratch, name):
+def call_with_slots(
+    kernel, scalars, inputs, in_specs, outputs, out_specs, previous, grid, scratch, name, micros
+):
     count = len(inputs)
     kept = [] if previous is None else [item for item in previous if item is not None]
     aliases = {}
@@ -59,6 +66,7 @@
         out_shape=outputs,
         input_output_aliases=aliases,
         compiler_params=params(),
+        cost_estimate=cost_of(micros),
         name=name,
     )(*scalars, *inputs, *kept)
 
@@ -83,6 +91,7 @@
         out_specs=pl.BlockSpec((1, width - QB, 2 * QB), lambda p: (p, 0, 0)),
         out_shape=jax.ShapeDtypeStruct((pairs, width - QB, 2 * QB), F32),
         compiler_params=params(),
+        cost_estimate=cost_of(6),
         name="toeplitz",
     )(offset_bias.reshape(pairs, 2, width))
 
@@ -118,6 +127,7 @@
         out_specs=pl.BlockSpec((1, 2, width), lambda p: (p, 0, 0)),
         out_shape=jax.ShapeDtypeStruct((pairs, 2, width), F32),
         compiler_params=params(),
+        cost_estimate=cost_of(10),
         name="diagonals",
     )(tables)
     return out.reshape(2 * pairs, width)
@@ -259,6 +269,7 @@
             pltpu.VMEM((span, blocks * QB), LOW),
         ],
         "attend",
+        24,
     )
 
 
@@ -372,6 +383,7 @@
             pltpu.VMEM((blocks * QB, span), F32),
         ],
         "attend_back",
+        26,
     )
 
 
@@ -459,6 +471,7 @@
         (3,),
         [],
         "enter",
+        9,
     )
 
 
@@ -578,6 +591,7 @@
         (steps,),
         [pltpu.VMEM((rows, width), F32), pltpu.VMEM((rows, width), F32)],
         "feed",
+        29,
     )
 
 
@@ -719,6 +733,7 @@
         (steps,),
         [pltpu.VMEM((rows, width), F32), pltpu.VMEM((rows, width), F32)],
         "feed_back",
+        27,
     )
 
 
@@ -809,89 +824,8 @@
         (3,),
         [pltpu.VMEM((rows, width), F32)],
         "enter_back",
-    )
-
-
-def wide_kernel(left_ref, right_ref, own_ref, oth_ref, turned_ref):
-    j = pl.program_id(0)
-    rows = left_ref.shape[1]
-
-    @pl.when(j == 0)
-    def _():
-        for slot in range(2):
-            turned_ref[:, slot * rows : (slot + 1) * rows] = left_ref[slot].T
-
-    both = jnp.concatenate([right_ref[0], right_ref[1]], axis=0)
-    product = dot_nn(turned_ref[...], both).astype(LOW)
-
-    @pl.when(lax.rem(j, 2) == 0)
-    def _():
-        own_ref[...] = product
-
-    @pl.when(lax.rem(j, 2) == 1)
-    def _():
-        oth_ref[...] = product
-
-
-def wide_grad(left, right, chunk, position, name):
-    _, rows, width = left.shape
-    total = right.shape[2]
-    steps = total // chunk
-    out = jax.ShapeDtypeStruct((width, total // 2), LOW)
-    spec = pl.BlockSpec((width, chunk), lambda j: (0, j // 2))
-    return pl.pallas_call(
-        wide_kernel,
-        grid=(steps,),
-        in_specs=[
-            pl.BlockSpec((2, rows, width), lambda j: (0, 0, 0)),
-            pl.BlockSpec((2, rows, chunk), lambda j: (0, 0, position(j))),
-        ],
-        out_specs=[spec, spec],
-        out_shape=[out, out],
-        scratch_shapes=[pltpu.VMEM((width, 2 * rows), LOW)],
-        compiler_params=params(),
-        name=name,
-    )(left, right)
-
-
-def tall_kernel(left_ref, right_ref, own_ref, oth_ref):
-    j = pl.program_id(0)
-    piece = own_ref.shape[2]
-    turned = jnp.concatenate([left_ref[0].T, left_ref[1].T], axis=1)
-    both = jnp.concatenate([right_ref[0], right_ref[1]], axis=0)
-    product = dot_nn(turned, both).astype(LOW)
-
-    def store(ref):
-        for at in range(ref.shape[0]):
-            ref[at] = product[:, at * piece : (at + 1) * piece]
-
-    @pl.when(lax.rem(j, 2) == 0)
-    def _():
-        store(own_ref)
-
-    @pl.when(lax.rem(j, 2) == 1)
-    def _():
-        store(oth_ref)
-
-
-def tall_grad(left, right, chunk, pieces, name):
-    _, rows, total = left.shape
-    width = right.shape[2]
-    each = total // 2 // chunk
-    out = jax.ShapeDtypeStruct((pieces, total // 2, width // pieces), LOW)
-    spec = pl.BlockSpec((pieces, chunk, width // pieces), lambda j: (0, j // 2, 0))
-    return pl.pallas_call(
-        tall_kernel,
-        grid=(2 * each,),
-        in_specs=[
-            pl.BlockSpec((2, rows, chunk), lambda j: (0, 0, lax.rem(j, 2) * each + j // 2)),
-            pl.BlockSpec((2, rows, width), lambda j: (0, 0, 0)),
-        ],
-        out_specs=[spec, spec],
-        out_shape=[out, out],
-        compiler_params=params(),
-        name=name,
-    )(left, right)
+        12,
+    )
 
 
 def passed_along(value, axis, steps):
@@ -1244,30 +1178,277 @@
     )
 
 
+def grads_kernel(
+    f_hbm, dy_hbm, c_hbm, db_hbm, n_hbm, du_hbm, e_hbm, dqkv_hbm, packed_ref,
+    out_ref, summed_ref,
+    still, moving, turned, given, held, near_ref, y_ref, low_ref, high_ref, small_ref, small_got,
+    still_sem, moving_sem, near_send, near_recv, y_send, y_recv, low_send, low_recv, high_send, high_recv,
+    small_send, small_recv
+):
+    dp = lax.axis_index("dp")
+    core = lax.axis_index("tensor")
+    section = lax.axis_index("section")
+    y_side = lax.rem(dp, 2)
+    low_side = lax.rem(dp // 2, 2)
+    high_side = dp // 4
+
+    def across(bit, side):
+        return {"dp": dp + bit * (1 - 2 * side)}
+
+    core_peer = {"tensor": 1 - core}
+    y_peer = across(1, y_side)
+    low_peer = across(2, low_side)
+    high_peer = across(4, high_side)
+    peers = [core_peer, y_peer, low_peer, high_peer, {"section": 1 - section}]
+    mesh_id = pl.DeviceIdType.MESH
+    total = out_ref.shape[0]
+
+    barrier = pltpu.get_barrier_semaphore()
+    for peer in peers:
+        pl.semaphore_signal(barrier, inc=1, device_id=peer, device_id_type=mesh_id)
+    pl.semaphore_wait(barrier, len(peers))
+
+    def send(source, target, out_sem, in_sem, peer):
+        return pltpu.make_async_remote_copy(
+            src_ref=source, dst_ref=target, send_sem=out_sem, recv_sem=in_sem,
+            device_id=peer, device_id_type=mesh_id,
+        )
+
+    def near_copy(k, slot):
+        return send(given.at[slot], near_ref.at[k], near_send.at[slot], near_recv.at[k], core_peer)
+
+    def y_copy(k):
+        return send(held.at[k, :, :, 1 - y_side], y_ref.at[k], y_send.at[k], y_recv.at[k], y_peer)
+
+    def low_copy(k):
+        return send(y_ref.at[k, :, 1 - low_side], low_ref.at[k], low_send.at[k], low_recv.at[k], low_peer)
+
+    def high_copy(k):
+        return send(low_ref.at[k, 1 - high_side], high_ref.at[k], high_send.at[k], high_recv.at[k], high_peer)
+
+    def small_copy(s):
+        return send(small_ref.at[s], small_got.at[s], small_send.at[s], small_recv.at[s], peers[s])
+
+    def added(a, b):
+        return (a.astype(F32) + b.astype(F32)).astype(LOW)
+
+    def near_stage(k):
+        near_copy(k, 0).wait_recv()
+        for hi in range(2):
+            for lo in range(2):
+                for side in range(2):
+                    held[k, hi, lo, side] = added(held[k, hi, lo, side], near_ref[k, hi, lo, side])
+        y_copy(k).start()
+
+    def y_stage(k):
+        y_copy(k).wait_recv()
+        for hi in range(2):
+            for lo in range(2):
+                y_ref[k, hi, lo] = added(y_ref[k, hi, lo], held[k, hi, lo, y_side])
+        low_copy(k).start()
+
+    def low_stage(k):
+        low_copy(k).wait_recv()
+        for hi in range(2):
+            low_ref[k, hi] = added(low_ref[k, hi], y_ref[k, hi, low_side])
+        high_copy(k).start()
+
+    def high_stage(k):
+        high_copy(k).wait_recv()
+        out_ref[k] = high_ref[k].astype(F32) + low_ref[k, high_side].astype(F32)
+
+    def small_stage(s):
+        small_copy(s).wait_recv()
+        small_ref[s + 1] = small_ref[s] + small_got[s]
+        if s + 1 < len(peers):
+            small_copy(s + 1).start()
+
+    chunk = moving.shape[4]
+    each = du_hbm.shape[2] // 2 // chunk
+    phases = [
+        (False, dy_hbm, f_hbm, each, lambda c: c * chunk, lambda c: (each + c) * chunk),
+        (True, n_hbm, du_hbm, each, lambda c: c * chunk, lambda c: (each + c) * chunk),
+        (False, db_hbm, c_hbm, 1, lambda c: 0 * c, lambda c: 0 * c + chunk),
+        (True, e_hbm, dqkv_hbm, 3, lambda c: 2 * c * chunk, lambda c: (2 * c + 1) * chunk),
+    ]
+
+    def still_copy(p):
+        return pltpu.make_async_copy(phases[p][1].at[0:2], still.at[p % 2], still_sem.at[p % 2])
+
+    def moving_copies(p, c, slot):
+        _, _, source, _, own_at, oth_at = phases[p]
+        return [
+            pltpu.make_async_copy(
+                source.at[0:2, :, pl.ds(pl.multiple_of(at(c), chunk), chunk)],
+                moving.at[slot, part],
+                moving_sem.at[slot, part],
+            )
+            for part, at in enumerate((own_at, oth_at))
+        ]
+
+    still_copy(0).start()
+    for copy in moving_copies(0, 0, 0):
+        copy.start()
+    still_copy(1).start()
+    small_ref[0] = packed_ref[...]
+    small_copy(0).start()
+
+    tokens = 2 * still.shape[2]
+    base = 0
+    for p, (wide, _, _, count, _, _) in enumerate(phases):
+        still_copy(p).wait()
+        stay = still.at[p % 2]
+        if wide:
+            for micro in range(2):
+                turned[:, micro * tokens // 2 : (micro + 1) * tokens // 2] = stay[micro].T
+
+        @pl.loop(0, count)
+        def _(c, p=p, wide=wide, count=count, base=base, stay=stay):
+            k = base + c
+            slot = lax.rem(k, 2)
+            for copy in moving_copies(p, c, slot):
+                copy.wait()
+
+            @pl.when(c + 1 < count)
+            def _():
+                for copy in moving_copies(p, c + 1, 1 - slot):
+                    copy.start()
+
+            if p + 1 < len(phases):
+
+                @pl.when(c + 1 == count)
+                def _():
+                    for copy in moving_copies(p + 1, 0, 1 - slot):
+                        copy.start()
+
+            @pl.when(k >= 2)
+            def _():
+                near_copy(k, slot).wait_send()
+
+            def product(part, store):
+                block = moving[slot, part].reshape(tokens, chunk)
+                if wide:
+                    result = dot_nn(turned[...], block).astype(LOW)
+                    for z in range(4):
+                        for side in range(2):
+                            at = (2 * z + side) * QB
+                            store(z, side, slice(None), result[at : at + QB, :])
+                else:
+                    result = dot_nn(block.T, stay[...].reshape(tokens, -1)).astype(LOW)
+                    for z in range(4):
+                        for side in range(2):
+                            at = (2 * z + side) * QB
+                            for q in range(chunk // QB):
+                                lanes = slice(q * QB, (q + 1) * QB)
+                                store(z, side, lanes, result[lanes, at : at + QB])
+
+            def to_given(z, side, lanes, value):
+                given[slot, z // 2, z % 2, side, :, lanes] = value
+
+            def to_held(z, side, lanes, value):
+                held[k, z // 2, z % 2, side, :, lanes] = value
+
+            product(1, to_given)
+            near_copy(k, slot).start()
+            product(0, to_held)
+
+            @pl.when(k >= 1)
+            def _():
+                near_stage(k - 1)
+
+            for s in range(len(peers)):
+
+                @pl.when(k == 2 * s + 1)
+                def _(s=s):
+                    small_stage(s)
+
+            @pl.when((k >= 5) & (lax.rem(k, 3) == 2))
+            def _():
+                y_stage((k - 5) // 3)
+
+        if p + 2 < len(phases):
+            still_copy(p + 2).start()
+        base += count
+
+    near_stage(total - 1)
+    early = (total - 1 - 5) // 3 + 1
+    for k in range(early):
+        low_stage(k)
+    for k in range(early - 1):
+        high_stage(k)
+
+    @pl.loop(early, total)
+    def _(k):
+        y_stage(k)
+        high_stage(k - 1)
+        low_stage(k)
+
+    high_stage(total - 1)
+    summed_ref[...] = small_ref[len(peers)]
+    near_copy(total - 2, (total - 2) % 2).wait_send()
+    near_copy(total - 1, (total - 1) % 2).wait_send()
+
+    @pl.loop(0, total)
+    def _(k):
+        y_copy(k).wait_send()
+        low_copy(k).wait_send()
+        high_copy(k).wait_send()
+
+    for s in range(len(peers)):
+        small_copy(s).wait_send()
+
+
+def summed_grads(f, dy, context, db, n, du, e, dqkv, packed):
+    rows, width = dy.shape[1:]
+    chunk = 512
+    total = du.shape[2] // chunk + 4
+    dma = pltpu.SemaphoreType.DMA
+    anywhere = pl.BlockSpec(memory_space=pl.ANY)
+    local = pl.BlockSpec(memory_space=pltpu.VMEM)
+    return pl.pallas_call(
+        grads_kernel,
+        in_specs=[anywhere] * 8 + [local],
+        out_specs=[local, local],
+        out_shape=[
+            jax.ShapeDtypeStruct((total, QB, chunk), F32),
+            jax.ShapeDtypeStruct(packed.shape, F32),
+        ],
+        scratch_shapes=[
+            pltpu.VMEM((2, 2, rows, width), LOW),
+            pltpu.VMEM((2, 2, 2, rows, chunk), LOW),
+            pltpu.VMEM((width, 2 * rows), LOW),
+            pltpu.VMEM((2, 2, 2, 2, QB, chunk), LOW),
+            pltpu.VMEM((total, 2, 2, 2, QB, chunk), LOW),
+            pltpu.VMEM((total, 2, 2, 2, QB, chunk), LOW),
+            pltpu.VMEM((total, 2, 2, QB, chunk), LOW),
+            pltpu.VMEM((total, 2, QB, chunk), LOW),
+            pltpu.VMEM((total, QB, chunk), LOW),
+            pltpu.VMEM((6,) + packed.shape, F32),
+            pltpu.VMEM((5,) + packed.shape, F32),
+            dma((2,)),
+            dma((2, 2)),
+            dma((2,)),
+            dma((total,)),
+            dma((total,)),
+            dma((total,)),
+            dma((total,)),
+            dma((total,)),
+            dma((total,)),
+            dma((total,)),
+            dma((5,)),
+            dma((5,)),
+        ],
+        compiler_params=pltpu.CompilerParams(
+            collective_id=0, has_side_effects=True, vmem_limit_bytes=TAIL_VMEM
+        ),
+        cost_estimate=cost_of(150),
+        name="summed_grads",
+    )(f, dy, context, db, n, du, e, dqkv, packed)
+
+
 def swapped(value, axis, bit):
     pairs = [(at, at ^ bit) for at in range(lax.axis_size(axis))]
     return lax.ppermute(value, axis, pairs)
-
-
-def halves_summed(total, axis, bit):
-    side = lax.rem(lax.axis_index(axis) // bit, 2)
-    given = lax.dynamic_index_in_dim(total, 1 - side, 0, keepdims=False)
-    kept = lax.dynamic_index_in_dim(total, side, 0, keepdims=False)
-    got = swapped(given, axis, bit)
-    return (kept.astype(F32) + got.astype(F32)).astype(LOW)
-
-
-def scattered(own, got):
-    total = (own.astype(F32) + got.astype(F32)).astype(LOW)
-    rest = own.shape[1:]
-    total = jnp.moveaxis(total.reshape((2, 2, 2) + rest), 2, 0)
-    total = halves_summed(total, "dp", 1)
-    total = jnp.moveaxis(total, 1, 0)
-    total = halves_summed(total, "dp", 2)
-    side = lax.rem(lax.axis_index("dp") // 4, 2)
-    given = lax.dynamic_index_in_dim(total, 1 - side, 0, keepdims=False)
-    kept = lax.dynamic_index_in_dim(total, side, 0, keepdims=False)
-    return kept.astype(F32) + swapped(given, "dp", 4).astype(F32)
 
 
 def paired_body(
@@ -1294,9 +1475,7 @@
     lead = jnp.where(leading, 1, 0).astype(jnp.int32)
     pieces = lax.axis_size("dp")
 
-    remote_grads = [
-        lax.ppermute(decoder_grads[0, micro, 0], "section", [(0, 1)]) for micro in range(micro_count)
-    ]
+    remote_grads = [lax.ppermute(decoder_grads[0, 0, 0], "section", [(0, 1)])]
     qkv_own = attn_in[0].reshape(width, -1)
     qkv_oth = swapped(qkv_own, "tensor", 1)
     wo = (attn_out[0], swapped(attn_out[0], "tensor", 1))
@@ -1339,7 +1518,8 @@
 
     received = jnp.zeros((rows, width), LOW)
     entered = attended = fed = None
-    delivered = []
+    results = []
+    finished = []
     for moment in range(micro_count + 1):
         slot = jnp.where(leading, moment, (moment + micro_count) % (micro_count + 1))
         info = info_of(slot)
@@ -1349,15 +1529,20 @@
         *entered, halo = enter(info, own_rows, received, entry_gain, qkv_shift, qkv_own, qkv_oth, entered)
         halo = swapped(halo, "tensor", 1)
         attended = attend(info, row_segments, entered[2], halo, bias, attended)
+        if moment < micro_count:
+            info, remote_grads[moment] = lax.optimization_barrier((info, remote_grads[moment]))
         *fed, result = feed(
             info, entered[0], attended[0], wo, up, down, ffn_both, gains, bert_shift, fed
         )
-        if moment < micro_count:
+        results.append(result)
+        if moment == 0:
             received = lax.ppermute(result, "section", [(0, 1)])
-        if moment >= 1:
-            delivered.append(
-                jnp.where(leading, lax.ppermute(result, "section", [(1, 0)]), result)
-            )
+            later, received = lax.optimization_barrier((decoder_grads[0, 1, 0], received))
+            remote_grads.append(lax.ppermute(later, "section", [(0, 1)]))
+        elif moment < micro_count:
+            received = lax.ppermute(result, "section", [(0, 1), (1, 0)])
+            finished.append(received)
+    finished.append(lax.ppermute(result, "section", [(1, 0)]))
     x_saved, e_saved, qkv_saved = entered
     context, lse, *halo_saved = attended
     f_saved, slope_saved, n_saved, one_saved, two_saved = fed
@@ -1376,24 +1561,12 @@
             info, received, decoder_grads[0, at, 0], remote_grads[at], one_saved, two_saved, slope_saved,
             wo, up, down, gains, feed_kept,
         )
-        if moment == micro_count:
-            dy_saved, du_saved, db_saved, stat_feed, stat_bias = feed_kept
-            down_own, down_oth = tall_grad(f_saved, dy_saved, 512, pieces, "down_grad")
-            ffn_each = du_saved.shape[2] // 2 // 512
-            up_own, up_oth = wide_grad(
-                n_saved, du_saved, 512, lambda j: lax.rem(j, 2) * ffn_each + j // 2, "up_grad"
-            )
-            grad_context, down_oth, up_oth = lax.optimization_barrier((grad_context, down_oth, up_oth))
-            down_got = swapped(down_oth, "tensor", 1)
-            up_got = swapped(up_oth, "tensor", 1)
-            down_sum = scattered(down_own, down_got)
-            up_sum = scattered(
-                up_own.reshape(pieces, width // pieces, -1), up_got.reshape(pieces, width // pieces, -1)
-            )
         dq, dk, dv, table_kept, far = attend_back(
             info, row_segments, qkv_saved, halo_saved, grad_context, bias, lse, table_kept
         )
         far = swapped(far, "tensor", 1)
+        if moment == 0:
+            info, finished[-1] = lax.optimization_barrier((info, finished[-1]))
         *entry_kept, low, lower = enter_back(
             info, dq, dk, dv, far, x_saved, dz, qkv_own, qkv_oth, entry_gain, entry_kept
         )
@@ -1404,11 +1577,7 @@
             received = lax.ppermute(low, "section", [(1, 0)])
     dqkv_saved, stat_entry = entry_kept
 
-    out_own, out_oth = tall_grad(context, db_saved, 512, pieces, "out_grad")
-    qkv_sum_own, qkv_sum_oth = wide_grad(e_saved, dqkv_saved, 512, lambda j: j, "qkv_grad")
-    out_sum = scattered(out_own, swapped(out_oth, "tensor", 1))
-    shape = (pieces, width // pieces, -1)
-    qkv_sum = scattered(qkv_sum_own.reshape(shape), swapped(qkv_sum_oth, "tensor", 1).reshape(shape))
+    dy_saved, du_saved, db_saved, stat_feed, stat_bias = feed_kept
 
     half = width // 2
     upper = lax.ppermute(jnp.stack(input_low)[:, :, half:], "section", [(0, 1)]).astype(F32)
@@ -1432,11 +1601,18 @@
     table_all = placed(jnp.where(leading, 0.0, near_table).reshape(2, heads, bucket_count))
     parts = [gain_all, shift_all, head_all, bias_all, table_all]
     packed = jnp.concatenate([part.reshape(-1) for part in parts])
-    packed = packed + swapped(packed, "tensor", 1)
-    packed = packed + swapped(packed, "dp", 1)
-    packed = packed + swapped(packed, "section", 1)
-    packed = packed + swapped(packed, "dp", 2)
-    packed = packed + swapped(packed, "dp", 4)
+    packed_rows = 8 * (-(-packed.size // (8 * width)))
+    packed = jnp.pad(packed, (0, packed_rows * width - packed.size)).reshape(packed_rows, width)
+    summed, packed = summed_grads(
+        f_saved, dy_saved, context, db_saved, n_saved, du_saved, e_saved, dqkv_saved, packed
+    )
+    packed = packed.reshape(-1)
+    quarters = ffn_in.shape[2] // summed.shape[2]
+    piece = width // pieces
+    down_sum = summed[:quarters].reshape(quarters, QB, -1, QB).transpose(0, 2, 1, 3).reshape(-1, piece)
+    up_sum = summed[quarters : 2 * quarters].transpose(1, 0, 2).reshape(piece, -1)
+    out_sum = summed[2 * quarters].reshape(QB, -1, QB).transpose(1, 0, 2).reshape(-1, piece)
+    qkv_sum = summed[2 * quarters + 1 :].transpose(1, 0, 2)
     unpacked = []
     start = 0
     for part in parts:
@@ -1445,9 +1621,9 @@
     gain_all, shift_all, head_all, bias_all, table_all = unpacked
     mine = lambda value: lax.dynamic_index_in_dim(value, core, 0, keepdims=False)
     return (
-        jnp.stack(delivered)[None, :, None],
+        jnp.where(leading, jnp.stack(finished), jnp.stack(results[1:]))[None, :, None],
         input_grad,
-        qkv_sum.reshape(1, width // pieces, 3, -1),
+        qkv_sum[None],
         out_sum[None],
         up_sum[None],
         down_sum[None],

time: 872 us -> 774 us (0.89)
  waiting for transfers between devices: 263 us -> 106 us
  Pallas kernels: 445 us -> 582 us
  starting transfers between devices: 65.1 us -> 23.1 us
  other arithmetic: 35.9 us -> 10.2 us
  local copies, waits for them, and re-layouts: 51.4 us -> 40 us
    ppermute x32 -> x11, waiting for transfers between devices: 165 us -> 7.91 us  [swapped(): return lax.ppermute(value, axis, pairs)]
    pallas_call x4 -> x1, Pallas kernels: 53 us -> 179 us  [summed_grads(): pl.pallas_call(grads_kernel, in_specs=[anywhere] * 8 + [local], out_specs...]
    ppermute x32 -> x11, starting transfers between devices: 41.7 us -> 1.99 us  [swapped(): return lax.ppermute(value, axis, pairs)]
    convert_element_type x12 -> x0, other arithmetic: 22.2 us -> none  [the longest x4 11.7 us: scattered(): total = (own.astype(F32) + got.astype(F32)).astype(LOW)]
    ppermute x2 -> x1, waiting for transfers between devices: 42.2 us -> 20.6 us  [paired_body(): received = lax.ppermute(result, 'section', [(0, 1)])]
    ppermute x4, waiting for transfers between devices: 17.2 us -> 28.6 us  [the longest x1 17.9 us: paired_body(): received = lax.ppermute(result, 'section', [(0, 1), (1, 0)])]
    ppermute x2, waiting for transfers between devices: 38.5 us -> 49 us  [paired_body(): received = lax.ppermute(low, 'section', [(1, 0)])]
    pallas_call x18, Pallas kernels: 375 us -> 385 us  [call_with_slots(): pl.pallas_call(run, grid_spec=pltpu.PrefetchScalarGridSpec(num_scalar_pre...]
  transfers between devices with their start and end apart: 41 -> 19, of which waited for: 21 -> 8; matrix products, arithmetic and copies ran while one was open for 8% -> 4% of each run, Pallas kernels for 28% -> 38%
where the time goes in v1:
time: 774 us; the launch traced here: 763 us
  Pallas kernels  582 us (75%)
  waiting for transfers between devices  106 us (14%)
  local copies, waits for them, and re-layouts  40 us (5%)
  starting transfers between devices  23.1 us (3%)
  other arithmetic  10.2 us (1%)
    pallas_call x18, Pallas kernels, call_with_slots(): pl.pallas_call(run, grid_spec=pltpu.PrefetchScalarGridSpec(num_scalar_pre...  385 us
    pallas_call x1, Pallas kernels, summed_grads(): pl.pallas_call(grads_kernel, in_specs=[anywhere] * 8 + [local], out_specs...  179 us
    ppermute x2, waiting for transfers between devices, paired_body(): received = lax.ppermute(low, 'section', [(1, 0)])  49 us
    ppermute x1, waiting for transfers between devices, paired_body(): received = lax.ppermute(result, 'section', [(0, 1)])  20.6 us
    ppermute x1, waiting for transfers between devices, paired_body(): received = lax.ppermute(result, 'section', [(0, 1), (1, 0)])  17.9 us
  transfers between devices with their start and end apart: 19, of which 8 were waited for; matrix products, arithmetic and copies ran while one was open for 4% of the time, Pallas kernels for 38%

profile of v1, /device:TPU:0, one launch (start us, length us, event | category | flops | bytes accessed | tf_op | source)
XLA Modules:
  0.0 762.8 jit_solution(14007391262426440264)
XLA Ops:
  0.7 3.2 copy.73
  3.9 3.0 copy.75.refs_5_.refs_7_
  7.4 2.8 slice_bitcast_fusion.3
  10.2 5.5 collective-permute-start
  17.6 1.5 slice_bitcast_fusion.2
  21.7 1.1 broadcast_1_refs_2__refs_1_.2.refs_2_.refs_1_
  22.8 9.0 %enter.3 = (bf16[3,512,1024]{2,1,0:T(8,128)(2,1)}, bf16[3,512,1024]{2,1,0:T(8,128)(2,1)}, bf16[3,512,3072]{2,1,0:T(8,128)(2,1)}, bf16[256,2048]{1,0:T(8,128)(2,1)}) custom-call(s32[5]{0:T(128)} %stack.117.refs_0_, bf16[512,1024]{1,0:T(8,128)(2,1)} %get-tuple-element.239.refs_1_, bf16[512,1024]{1,0:T(8,128)(2,1)} %broadcast_1_refs_2__refs_1_.2.refs_2_.refs_1_, ...), custom_call_target="tpu_custom_call" | custom-call | flops 8999999488 | tf_op jit(solution)/shard_map/enter/pallas_call | solution.py:57
  33.5 6.7 toeplitz.1.refs_6_.refs_7_
  41.1 25.4 %attend.3 = (bf16[3,512,1024]{2,1,0:T(8,128)(2,1)}, f32[3,8,4,256]{3,2,1,0:T(4,128)}, bf16[3,256,1024]{2,1,0:T(8,128)(2,1)}, bf16[3,256,1024]{2,1,0:T(8,128)(2,1)}) custom-call(s32[5]{0:T(128)} %stack.117.refs_0_, s32[1280]{0:T(1024)} %get-tuple-element.236.refs_1_, s32[10,128]{1,0:T(8,128)} %bitcast.137, ...), custom_call_target="tpu_custom_call" | custom-call | flops 24000000000 | tf_op jit(solution)/shard_map/attend/pallas_call | solution.py:57
  66.6 29.5 %feed.3 = (bf16[3,512,4096]{2,1,0:T(8,128)(2,1)}, bf16[3,512,4096]{2,1,0:T(8,128)(2,1)}, bf16[3,512,1024]{2,1,0:T(8,128)(2,1)}, f32[3,512,1024]{2,1,0:T(8,128)},...) custom-call(s32[5]{0:T(128)} %stack.117.refs_0_, bf16[3,512,1024]{2,1,0:T(8,128)(2,1)} %get-tuple-element.111.refs_1_.refs_7_, ...), custom_call_target="tpu_custom_call" | custom-call | flops 28999999488 | tf_op jit(solution)/shard_map/feed/pallas_call | solution.py:57
  96.1 1.4 collective-permute-start.7
  98.1 20.6 %collective-permute-done.7.refs_2_ = bf16[512,1024]{1,0:T(8,128)(2,1)S(1)} collective-permute-done((bf16[512,1024]{1,0:T(8,128)(2,1)}, bf16[512,1024]{1,0:T(8,128)(2,1)S(1)}, u32[]{:S(2)}, u32[]{:S(2)}) %collective-permute-start.7) | collective-permute-done | bytes 1048608 | tf_op jit(solution)/shard_map/ppermute | solution.py:1539
  118.7 4.7 collective-permute-start.8
  123.4 9.0 %enter.4 = (bf16[3,512,1024]{2,1,0:T(8,128)(2,1)}, bf16[3,512,1024]{2,1,0:T(8,128)(2,1)}, bf16[3,512,3072]{2,1,0:T(8,128)(2,1)}, bf16[256,2048]{1,0:T(8,128)(2,1)}) custom-call(s32[5]{0:T(128)} %stack.115.refs_0_, bf16[512,1024]{1,0:T(8,128)(2,1)} %get-tuple-element.240.refs_1_, ...), custom_call_target="tpu_custom_call", output_to_operand_aliasing={{0}: (7, {}), {1}: (8, {}), {2}: (9, {})} | custom-call | flops 8999999488 | tf_op jit(solution)/shard_map/enter/pallas_call | solution.py:57
  132.4 10.7 %collective-permute-done.8.refs_3_ = bf16[512,1024]{1,0:T(8,128)(2,1)S(1)} collective-permute-done((bf16[512,1024]{1,0:T(8,128)(2,1)S(1)}, bf16[512,1024]{1,0:T(8,128)(2,1)S(1)}, u32[]{:S(2)}, u32[]{:S(2)}) %collective-permute-start.8) | collective-permute-done | bytes 1048608 | tf_op jit(solution)/shard_map/ppermute | solution.py:1541
  144.1 24.0 %attend.4 = (bf16[3,512,1024]{2,1,0:T(8,128)(2,1)}, f32[3,8,4,256]{3,2,1,0:T(4,128)}, bf16[3,256,1024]{2,1,0:T(8,128)(2,1)}, bf16[3,256,1024]{2,1,0:T(8,128)(2,1)}) custom-call(s32[5]{0:T(128)} %stack.115.refs_0_, s32[1280]{0:T(1024)} %get-tuple-element.232.refs_1_, ...), custom_call_target="tpu_custom_call", output_to_operand_aliasing={{0}: (9, {}), {1}: (10, {}), {2}: (11, {}), {3}: (12, {})} | custom-call | flops 24000000000 | tf_op jit(solution)/shard_map/attend/pallas_call | solution.py:57
  168.1 29.5 %feed.4 = (bf16[3,512,4096]{2,1,0:T(8,128)(2,1)}, bf16[3,512,4096]{2,1,0:T(8,128)(2,1)}, bf16[3,512,1024]{2,1,0:T(8,128)(2,1)}, f32[3,512,1024]{2,1,0:T(8,128)},...) custom-call(s32[5]{0:T(128)} %stack.115.refs_0_, ...), custom_call_target="tpu_custom_call", output_to_operand_aliasing={{0}: (12, {}), {1}: (13, {}), {2}: (14, {}), {3}: (15, {}),... | custom-call | flops 28999999488 | tf_op jit(solution)/shard_map/feed/pallas_call | solution.py:57
  197.6 3.4 collective-permute-start.10
  201.6 17.9 %collective-permute-done.10.refs_2_ = bf16[512,1024]{1,0:T(8,128)(2,1)S(1)} collective-permute-done((bf16[512,1024]{1,0:T(8,128)(2,1)}, bf16[512,1024]{1,0:T(8,128)(2,1)S(1)}, u32[]{:S(2)}, u32[]{:S(2)}) %collective-permute-start.10) | collective-permute-done | bytes 1048608 | tf_op jit(solution)/shard_map/ppermute | solution.py:1543
  220.6 9.2 %enter.5 = (bf16[3,512,1024]{2,1,0:T(8,128)(2,1)}, bf16[3,512,1024]{2,1,0:T(8,128)(2,1)}, bf16[3,512,3072]{2,1,0:T(8,128)(2,1)}, bf16[256,2048]{1,0:T(8,128)(2,1)}) custom-call(s32[5]{0:T(128)} %stack.125.refs_0_, bf16[512,1024]{1,0:T(8,128)(2,1)} %get-tuple-element.240.refs_1_, ...), custom_call_target="tpu_custom_call", output_to_operand_aliasing={{0}: (7, {}), {1}: (8, {}), {2}: (9, {})} | custom-call | flops 8999999488 | tf_op jit(solution)/shard_map/enter/pallas_call | solution.py:57
  230.3 2.3 collective-permute-done.11.refs_7_.refs_8_
  233.6 24.0 %attend.5 = (bf16[3,512,1024]{2,1,0:T(8,128)(2,1)}, f32[3,8,4,256]{3,2,1,0:T(4,128)}, bf16[3,256,1024]{2,1,0:T(8,128)(2,1)}, bf16[3,256,1024]{2,1,0:T(8,128)(2,1)}) custom-call(s32[5]{0:T(128)} %stack.125.refs_0_, s32[1280]{0:T(1024)} %get-tuple-element.233.refs_1_, ...), custom_call_target="tpu_custom_call", output_to_operand_aliasing={{0}: (9, {}), {1}: (10, {}), {2}: (11, {}), {3}: (12, {})} | custom-call | flops 24000000000 | tf_op jit(solution)/shard_map/attend/pallas_call | solution.py:57
  257.6 29.5 %feed.5 = (bf16[3,512,4096]{2,1,0:T(8,128)(2,1)}, bf16[3,512,4096]{2,1,0:T(8,128)(2,1)}, bf16[3,512,1024]{2,1,0:T(8,128)(2,1)}, f32[3,512,1024]{2,1,0:T(8,128)},...) custom-call(s32[5]{0:T(128)} %stack.125.refs_0_, ...), custom_call_target="tpu_custom_call", output_to_operand_aliasing={{0}: (12, {}), {1}: (13, {}), {2}: (14, {}), {3}: (15, {}),... | custom-call | flops 28999999488 | tf_op jit(solution)/shard_map/feed/pallas_call | solution.py:57
  287.1 1.3 collective-permute-start.12
  288.4 27.3 %feed_back.3 = (bf16[3,512,1024]{2,1,0:T(8,128)(2,1)}, bf16[3,512,4096]{2,1,0:T(8,128)(2,1)}, bf16[3,512,1024]{2,1,0:T(8,128)(2,1)}, f32[3,8,1024]{2,1,0:T(8,128...) custom-call(s32[5]{0:T(128)} %stack.123.refs_0_, ...), custom_call_target="tpu_custom_call" | custom-call | flops 27000000512 | tf_op jit(solution)/shard_map/feed_back/pallas_call | solution.py:57
  315.7 25.7 %attend_back.3 = (bf16[512,1024]{1,0:T(8,128)(2,1)}, bf16[512,1024]{1,0:T(8,128)(2,1)}, bf16[512,1024]{1,0:T(8,128)(2,1)}, f32[3,8,640,256]{3,2,1,0:T(8,128)}, bf16[2,256,1024]{2,1,0:T(8,128)(2,1)}) custom-call(s32[5]{0:T(128)} %stack.123.refs_0_, s32[1280]{0:T(1024)} %get-tuple-element.231.refs_1_, s32[10,128]{1,0:T(8,128)} %bitcast.134, ...), custom_call_target="tpu_custom_call" | custom-call | flops 25999998976 | tf_op jit(solution)/shard_map/attend_back/pallas_call | solution.py:57
  341.5 2.8 collective-permute-done.13.refs_4_
  345.3 11.8 %enter_back.3 = (bf16[3,512,3072]{2,1,0:T(8,128)(2,1)}, f32[3,8,1024]{2,1,0:T(8,128)}, bf16[512,1024]{1,0:T(8,128)(2,1)}, f32[512,512]{1,0:T(8,128)}) custom-call(s32[5]{0:T(128)} %stack.123.refs_0_, bf16[512,1024]{1,0:T(8,128)(2,1)} %get-tuple-element.157.refs_1_, bf16[512,1024]{1,0:T(8,128)(2,1)} %get-tuple-element.158.refs_2_, ...), custom_call_target="tpu_custom_call" | custom-call | flops 12000000000 | tf_op jit(solution)/shard_map/enter_back/pallas_call | solution.py:57
  357.0 1.3 collective-permute-start.14
  358.9 26.4 %collective-permute-done.14.refs_1_ = bf16[512,1024]{1,0:T(8,128)(2,1)S(1)} collective-permute-done((bf16[512,1024]{1,0:T(8,128)(2,1)}, bf16[512,1024]{1,0:T(8,128)(2,1)S(1)}, u32[]{:S(2)}, u32[]{:S(2)}) %collective-permute-start.14) | collective-permute-done | bytes 1048608 | tf_op jit(solution)/shard_map/ppermute | solution.py:1577
  386.3 27.0 %feed_back.4 = (bf16[3,512,1024]{2,1,0:T(8,128)(2,1)}, bf16[3,512,4096]{2,1,0:T(8,128)(2,1)}, bf16[3,512,1024]{2,1,0:T(8,128)(2,1)}, f32[3,8,1024]{2,1,0:T(8,128...) custom-call(s32[5]{0:T(128)} %stack.132.refs_0_, ...), custom_call_target="tpu_custom_call", output_to_operand_aliasing={{0}: (14, {}), {1}: (15, {}), {2}: (16, {}), {3}: (17, {}),... | custom-call | flops 27000000512 | tf_op jit(solution)/shard_map/feed_back/pallas_call | solution.py:57
  413.3 27.2 %attend_back.4 = (bf16[512,1024]{1,0:T(8,128)(2,1)}, bf16[512,1024]{1,0:T(8,128)(2,1)}, bf16[512,1024]{1,0:T(8,128)(2,1)}, f32[3,8,640,256]{3,2,1,0:T(8,128)}, bf16[2,256,1024]{2,1,0:T(8,128)(2,1)}) custom-call(s32[5]{0:T(128)} %stack.132.refs_0_, s32[1280]{0:T(1024)} %get-tuple-element.234.refs_1_, ...), custom_call_target="tpu_custom_call", output_to_operand_aliasing={{3}: (11, {})} | custom-call | flops 25999998976 | tf_op jit(solution)/shard_map/attend_back/pallas_call | solution.py:57
  440.6 2.9 collective-permute-done.15.refs_4_
  444.4 12.3 %enter_back.4 = (bf16[3,512,3072]{2,1,0:T(8,128)(2,1)}, f32[3,8,1024]{2,1,0:T(8,128)}, bf16[512,1024]{1,0:T(8,128)(2,1)}, f32[512,512]{1,0:T(8,128)}) custom-call(s32[5]{0:T(128)} %stack.132.refs_0_, bf16[512,1024]{1,0:T(8,128)(2,1)} %get-tuple-element.171.refs_1_, ...), custom_call_target="tpu_custom_call", output_to_operand_aliasing={{0}: (10, {}), {1}: (11, {})} | custom-call | flops 12000000000 | tf_op jit(solution)/shard_map/enter_back/pallas_call | solution.py:57
  456.7 1.3 collective-permute-start.16
  458.6 2.9 maximum_select_fusion
  461.6 22.6 %collective-permute-done.16.refs_1_ = bf16[512,1024]{1,0:T(8,128)(2,1)} collective-permute-done((bf16[512,1024]{1,0:T(8,128)(2,1)}, bf16[512,1024]{1,0:T(8,128)(2,1)}, u32[]{:S(2)}, u32[]{:S(2)}) %collective-permute-start.16) | collective-permute-done | bytes 1048608 | tf_op jit(solution)/shard_map/ppermute | solution.py:1577
  484.1 26.8 %feed_back.5 = (bf16[3,512,1024]{2,1,0:T(8,128)(2,1)}, bf16[3,512,4096]{2,1,0:T(8,128)(2,1)}, bf16[3,512,1024]{2,1,0:T(8,128)(2,1)}, f32[3,8,1024]{2,1,0:T(8,128...) custom-call(s32[5]{0:T(128)} %stack.135.refs_0_, ...), custom_call_target="tpu_custom_call", output_to_operand_aliasing={{0}: (14, {}), {1}: (15, {}), {2}: (16, {}), {3}: (17, {}),... | custom-call | flops 27000000512 | tf_op jit(solution)/shard_map/feed_back/pallas_call | solution.py:57
  511.0 25.7 %attend_back.5 = (bf16[512,1024]{1,0:T(8,128)(2,1)}, bf16[512,1024]{1,0:T(8,128)(2,1)}, bf16[512,1024]{1,0:T(8,128)(2,1)}, f32[3,8,640,256]{3,2,1,0:T(8,128)}, bf16[2,256,1024]{2,1,0:T(8,128)(2,1)}) custom-call(s32[5]{0:T(128)} %stack.135.refs_0_, s32[1280]{0:T(1024)} %get-tuple-element.235.refs_1_, ...), custom_call_target="tpu_custom_call", output_to_operand_aliasing={{3}: (11, {})} | custom-call | flops 25999998976 | tf_op jit(solution)/shard_map/attend_back/pallas_call | solution.py:57
  536.7 10.9 %diagonals.1 = f32[8,2,768]{2,1,0:T(2,128)} custom-call(f32[3,8,640,256]{3,2,1,0:T(8,128)} %get-tuple-element.206.a_ref), custom_call_target="tpu_custom_call" | custom-call | flops 10000000000 | tf_op jit(solution)/shard_map/diagonals/pallas_call | solution.py:123
  550.3 11.9 %enter_back.5 = (bf16[3,512,3072]{2,1,0:T(8,128)(2,1)}, f32[3,8,1024]{2,1,0:T(8,128)}, bf16[512,1024]{1,0:T(8,128)(2,1)}, f32[512,512]{1,0:T(8,128)}) custom-call(s32[5]{0:T(128)} %stack.135.refs_0_, bf16[512,1024]{1,0:T(8,128)(2,1)} %get-tuple-element.187.refs_1_, ...), custom_call_target="tpu_custom_call", output_to_operand_aliasing={{0}: (10, {}), {1}: (11, {})} | custom-call | flops 12000000000 | tf_op jit(solution)/shard_map/enter_back/pallas_call | solution.py:57
  563.0 2.1 pad_maximum_fusion
  565.2 2.3 collective-permute-start.18
  568.2 179.4 %summed_grads.1 = (f32[12,128,512]{2,1,0:T(8,128)}, f32[16,1024]{1,0:T(8,128)}) custom-call(bf16[3,512,4096]{2,1,0:T(8,128)(2,1)} %get-tuple-element.196.f_hbm, bf16[3,512,1024]{2,1,0:T(8,128)(2,1)} %get-tuple-element.197.dy_hbm, bf16[3,512,1024]{2,1,0:T(8,128)(2,1)} %get-tuple-element.140.refs_2_.c_hbm, bf16[3,512,1024]{2,1,0:T(8,128)(2,1)} %get-tuple-element.198.db_hbm, ...), custom_call_target="tpu_custom_call" | custom-call | flops 149999992832 | tf_op jit(solution)/shard_map/summed_grads/pallas_call | solution.py:1408
  747.7 1.9 fusion.21
  751.8 1.3 copy.88
  757.7 2.1 slice_bitcast_fusion.5
  759.7 2.9 fusion
  (158 shorter events, 27.7 us)
Async XLA Ops:
  0.6 18.5 %copy-start = (s32[2,1,1024]{2,1,0:T(1,128)S(1)}, s32[2,1,1024]{2,1,0:T(1,128)}, u32[]{:S(2)}) copy-start(s32[2,1,1024]{2,1,0:T(1,128)} %param.14) | copy-start | bytes 24580
  6.8 8.9 %copy-start.20 = (f32[2,512]{1,0:T(2,128)S(1)}, f32[2,512]{1,0:T(2,128)}, u32[]{:S(2)}) copy-start(f32[2,512]{1,0:T(2,128)} %param.22) | copy-start | bytes 12292
  6.8 8.9 %copy-start.19 = (f32[8,32]{1,0:T(8,128)S(1)}, f32[8,32]{1,0:T(8,128)}, u32[]{:S(2)}) copy-start(f32[8,32]{1,0:T(8,128)} %param.24) | copy-start | bytes 3076
  6.8 8.9 %copy-start.18 = (f32[2048]{0:T(1024)S(1)}, f32[2048]{0:T(1024)}, u32[]{:S(2)}) copy-start(f32[2048]{0:T(1024)} %param.23) | copy-start | bytes 24580
  6.8 9.6 %copy-start.13 = (f32[2,2,1024]{2,1,0:T(2,128)S(1)}, f32[2,2,1024]{2,1,0:T(2,128)}, u32[]{:S(2)}) copy-start(f32[2,2,1024]{2,1,0:T(2,128)} %param.20) | copy-start | bytes 49156
  6.8 10.8 %copy-start.2 = (bf16[2,1,512,1024]{3,2,1,0:T(8,128)(2,1)S(1)}, bf16[2,1,512,1024]{3,2,1,0:T(8,128)(2,1)}, u32[]{:S(2)}) copy-start(bf16[2,1,512,1024]{3,2,1,0:T(8,128)(2,1)} %param.13) | copy-start | bytes 6291460
  6.8 14.9 %collective-permute-start.2 = (bf16[1024,1536]{1,0:T(8,128)(2,1)}, bf16[1024,1536]{1,0:T(8,128)(2,1)}, u32[]{:S(2)}, u32[]{:S(2)}) collective-permute-start(bf16[1024,1536]{1,0:T(8,128)(2,1)} %copy.75.refs_5_.refs_7_), channel_id=1, source_target_pairs={{0,1},{1,0},{2,3},{3,2},{4,5},{5,4},{6,7},{7,6},{8,9},{9,8},{10,11... | collective-permute-start | bytes 9437192 | tf_op jit(solution)/shard_map/ppermute | solution.py:1451
  10.2 108.5 %copy-start.9 = (bf16[512,1024]{1,0:T(8,128)(2,1)}, bf16[512,1024]{1,0:T(8,128)(2,1)S(1)}, u32[]{:S(2)}) copy-start(bf16[512,1024]{1,0:T(8,128)(2,1)S(1)} %get-tuple-element.116.refs_2_) | copy-start | bytes 3145732
  10.2 9.0 %copy-start.21 = (s32[2047]{0:T(1024)S(1)}, s32[2047]{0:T(1024)}, u32[]{:S(2)}) copy-start(s32[2047]{0:T(1024)} %param.15) | copy-start | bytes 24568
  10.2 29.9 %collective-permute-start = (bf16[512,1024]{1,0:T(8,128)(2,1)}, bf16[512,1024]{1,0:T(8,128)(2,1)}, u32[]{:S(2)}, u32[]{:S(2)}) collective-permute-start(bf16[512,1024]{1,0:T(8,128)(2,1)} %get-tuple-element.241.refs_2_), channel_id=1, source_target_pairs={{0,2},{1,3},{4,6},{5,7},{8,10},{9,11},{12,14},{13,15},{16,18},{17,... | collective-permute-start | bytes 3145736 | tf_op jit(solution)/shard_map/ppermute | solution.py:1478
  15.8 4.8 collective-permute-start.1
  15.9 50.6 %collective-permute-start.4 = (bf16[512,1024]{1,0:T(8,128)(2,1)}, bf16[512,1024]{1,0:T(8,128)(2,1)}, u32[]{:S(2)}, u32[]{:S(2)}) collective-permute-start(bf16[512,1024]{1,0:T(8,128)(2,1)} %bitcast.154), channel_id=1, source_target_pairs={{0,1},{1,0},{2,3},{3,2},{4,5},{5,4},{6,7},{7,6},{8,9},{9,8},{10,11... | collective-permute-start | bytes 3145736 | tf_op jit(solution)/shard_map/ppermute | solution.py:1451
  16.4 50.2 %collective-permute-start.5 = (bf16[1024,2048]{1,0:T(8,128)(2,1)}, bf16[1024,2048]{1,0:T(8,128)(2,1)}, u32[]{:S(2)}, u32[]{:S(2)}) collective-permute-start(bf16[1024,2048]{1,0:T(8,128)(2,1)} %bitcast.140), channel_id=1, source_target_pairs={{0,1},{1,0},{2,3},{3,2},{4,5},{5,4},{6,7},{7,6},{8,9},{9,8},{10,11... | collective-permute-start | bytes 12582920 | tf_op jit(solution)/shard_map/ppermute | solution.py:1451
  19.3 12.7 %copy-start.15 = (s32[768]{0:T(1024)}, s32[768]{0:T(1024)S(1)}, u32[]{:S(2)}) copy-start(s32[768]{0:T(1024)S(1)} %slice.134) | copy-start | bytes 9220
  20.6 45.9 %collective-permute-start.6 = (bf16[2048,1024]{1,0:T(8,128)(2,1)}, bf16[2048,1024]{1,0:T(8,128)(2,1)}, u32[]{:S(2)}, u32[]{:S(2)}) collective-permute-start(bf16[2048,1024]{1,0:T(8,128)(2,1)} %bitcast.147), channel_id=1, source_target_pairs={{0,1},{1,0},{2,3},{3,2},{4,5},{5,4},{6,7},{7,6},{8,9},{9,8},{10,11... | collective-permute-start | bytes 12582920 | tf_op jit(solution)/shard_map/ppermute | solution.py:1451
  31.8 8.3 %collective-permute-start.3 = (bf16[256,2048]{1,0:T(8,128)(2,1)}, bf16[256,2048]{1,0:T(8,128)(2,1)S(1)}, u32[]{:S(2)}, u32[]{:S(2)}) collective-permute-start(bf16[256,2048]{1,0:T(8,128)(2,1)} %get-tuple-element.113), channel_id=1, source_target_pairs={{0,1},{1,0},{2,3},{3,2},{4,5},{5,4},{6,7},{7,6},{8,9},{9,8},{10,11... | collective-permute-start | bytes 3145736 | tf_op jit(solution)/shard_map/ppermute | solution.py:1451
  40.1 1.0 copy-start.24
  96.1 22.7 %collective-permute-start.7 = (bf16[512,1024]{1,0:T(8,128)(2,1)}, bf16[512,1024]{1,0:T(8,128)(2,1)S(1)}, u32[]{:S(2)}, u32[]{:S(2)}) collective-permute-start(bf16[512,1024]{1,0:T(8,128)(2,1)} %get-tuple-element.115), channel_id=1, source_target_pairs={{0,2},{1,3},{4,6},{5,7},{8,10},{9,11},{12,14},{13,15},{16,18},{17,... | collective-permute-start | bytes 3145736 | tf_op jit(solution)/shard_map/ppermute | solution.py:1539
  118.7 4.7 copy-start.25
  118.7 24.4 %collective-permute-start.8 = (bf16[512,1024]{1,0:T(8,128)(2,1)S(1)}, bf16[512,1024]{1,0:T(8,128)(2,1)S(1)}, u32[]{:S(2)}, u32[]{:S(2)}) collective-permute-start(bf16[512,1024]{1,0:T(8,128)(2,1)S(1)} %get-tuple-element.116.refs_2_), channel_id=1, source_target_pairs={{0,2},{1,3},{4,6},{5,7},{8,10},{9,11},{12,14},{13,15},{16,18},{17,... | collective-permute-start | bytes 3145736 | tf_op jit(solution)/shard_map/ppermute | solution.py:1541
  132.4 10.7 %collective-permute-start.9 = (bf16[256,2048]{1,0:T(8,128)(2,1)}, bf16[256,2048]{1,0:T(8,128)(2,1)S(1)}, u32[]{:S(2)}, u32[]{:S(2)}) collective-permute-start(bf16[256,2048]{1,0:T(8,128)(2,1)} %get-tuple-element.122), channel_id=1, source_target_pairs={{0,1},{1,0},{2,3},{3,2},{4,5},{5,4},{6,7},{7,6},{8,9},{9,8},{10,11... | collective-permute-start | bytes 3145736 | tf_op jit(solution)/shard_map/ppermute | solution.py:1451
  143.1 25.0 %copy-start.22 = (bf16[512,1024]{1,0:T(8,128)(2,1)}, bf16[512,1024]{1,0:T(8,128)(2,1)S(1)}, u32[]{:S(2)}) copy-start(bf16[512,1024]{1,0:T(8,128)(2,1)S(1)} %collective-permute-done.8.refs_3_) | copy-start | bytes 3145732
  143.1 1.0 copy-start.27
  197.6 21.9 %collective-permute-start.10 = (bf16[512,1024]{1,0:T(8,128)(2,1)}, bf16[512,1024]{1,0:T(8,128)(2,1)S(1)}, u32[]{:S(2)}, u32[]{:S(2)}) collective-permute-start(bf16[512,1024]{1,0:T(8,128)(2,1)} %get-tuple-element.132), channel_id=1, source_target_pairs={{0,2},{2,0},{1,3},{3,1},{4,6},{6,4},{5,7},{7,5},{8,10},{10,8},{9,1... | collective-permute-start | bytes 3145736 | tf_op jit(solution)/shard_map/ppermute | solution.py:1543
  219.6 1.0 copy-start.4
  229.7 2.9 collective-permute-start.11
  232.6 1.0 copy-start.28
  287.1 54.5 %collective-permute-start.12 = (bf16[512,1024]{1,0:T(8,128)(2,1)}, bf16[512,1024]{1,0:T(8,128)(2,1)S(1)}, u32[]{:S(2)}, u32[]{:S(2)}) collective-permute-start(bf16[512,1024]{1,0:T(8,128)(2,1)} %get-tuple-element.146), channel_id=1, source_target_pairs={{2,0},{3,1},{6,4},{7,5},{10,8},{11,9},{14,12},{15,13},{18,16},{19,... | collective-permute-start | bytes 3145736 | tf_op jit(solution)/shard_map/ppermute | solution.py:1545
  341.4 2.9 collective-permute-start.13
  341.5 15.5 %copy-start.8 = (bf16[512,1024]{1,0:T(8,128)(2,1)}, bf16[512,1024]{1,0:T(8,128)(2,1)S(1)}, u32[]{:S(2)}) copy-start(bf16[512,1024]{1,0:T(8,128)(2,1)S(1)} %collective-permute-done.12) | copy-start | bytes 3145732
  344.3 1.0 copy-start.29
  357.0 28.3 %collective-permute-start.14 = (bf16[512,1024]{1,0:T(8,128)(2,1)}, bf16[512,1024]{1,0:T(8,128)(2,1)S(1)}, u32[]{:S(2)}, u32[]{:S(2)}) collective-permute-start(bf16[512,1024]{1,0:T(8,128)(2,1)} %get-tuple-element.162), channel_id=1, source_target_pairs={{2,0},{3,1},{6,4},{7,5},{10,8},{11,9},{14,12},{15,13},{18,16},{19,... | collective-permute-start | bytes 3145736 | tf_op jit(solution)/shard_map/ppermute | solution.py:1577
  440.5 2.9 collective-permute-start.15
  444.4 14.2 %copy-start.3 = (bf16[512,1024]{1,0:T(8,128)(2,1)S(1)}, bf16[512,1024]{1,0:T(8,128)(2,1)}, u32[]{:S(2)}) copy-start(bf16[512,1024]{1,0:T(8,128)(2,1)} %get-tuple-element.132) | copy-start | bytes 3145732
  444.4 14.2 %copy-start.5 = (bf16[512,1024]{1,0:T(8,128)(2,1)S(1)}, bf16[512,1024]{1,0:T(8,128)(2,1)}, u32[]{:S(2)}) copy-start(bf16[512,1024]{1,0:T(8,128)(2,1)} %copy-done.4) | copy-start | bytes 3145732
  444.4 14.2 %copy-start.6 = (bf16[512,1024]{1,0:T(8,128)(2,1)S(1)}, bf16[512,1024]{1,0:T(8,128)(2,1)}, u32[]{:S(2)}) copy-start(bf16[512,1024]{1,0:T(8,128)(2,1)} %get-tuple-element.146) | copy-start | bytes 3145732
  456.7 27.4 %collective-permute-start.16 = (bf16[512,1024]{1,0:T(8,128)(2,1)}, bf16[512,1024]{1,0:T(8,128)(2,1)}, u32[]{:S(2)}, u32[]{:S(2)}) collective-permute-start(bf16[512,1024]{1,0:T(8,128)(2,1)} %get-tuple-element.179), channel_id=1, source_target_pairs={{2,0},{3,1},{6,4},{7,5},{10,8},{11,9},{14,12},{15,13},{18,16},{19,... | collective-permute-start | bytes 3145736 | tf_op jit(solution)/shard_map/ppermute | solution.py:1577
  536.6 12.7 %collective-permute-start.17 = (bf16[2,256,1024]{2,1,0:T(8,128)(2,1)}, bf16[2,256,1024]{2,1,0:T(8,128)(2,1)S(1)}, u32[]{:S(2)}, u32[]{:S(2)}) collective-permute-start(bf16[2,256,1024]{2,1,0:T(8,128)(2,1)} %get-tuple-element.190), channel_id=1, source_target_pairs={{0,1},{1,0},{2,3},{3,2},{4,5},{5,4},{6,7},{7,6},{8,9},{9,8},{10,11... | collective-permute-start | bytes 3145736 | tf_op jit(solution)/shard_map/ppermute | solution.py:1451
  536.7 10.9 %copy-start.17 = (f32[3,1,4096]{2,1,0:T(1,128)S(1)}, f32[3,1,4096]{2,1,0:T(1,128)}, u32[]{:S(2)}) copy-start(f32[3,1,4096]{2,1,0:T(1,128)} %get-tuple-element.205) | copy-start | bytes 147460
  536.7 12.3 %copy-start.16 = (s32[768]{0:T(1024)S(1)}, s32[768]{0:T(1024)}, u32[]{:S(2)}) copy-start(s32[768]{0:T(1024)} %copy-done.15) | copy-start | bytes 9220
  536.7 12.6 %copy-start.14 = (f32[3,8,1024]{2,1,0:T(8,128)S(1)}, f32[3,8,1024]{2,1,0:T(8,128)}, u32[]{:S(2)}) copy-start(f32[3,8,1024]{2,1,0:T(8,128)} %get-tuple-element.203) | copy-start | bytes 294916
  549.3 1.0 copy-start.23
  550.3 12.7 %copy-start.7 = (bf16[512,1024]{1,0:T(8,128)(2,1)S(1)}, bf16[512,1024]{1,0:T(8,128)(2,1)}, u32[]{:S(2)}) copy-start(bf16[512,1024]{1,0:T(8,128)(2,1)} %get-tuple-element.179) | copy-start | bytes 3145732
  565.2 194.6 %collective-permute-start.18 = (bf16[2,512,512]{2,1,0:T(8,128)(2,1)}, bf16[2,512,512]{2,1,0:T(8,128)(2,1)}, u32[]{:S(2)}, u32[]{:S(2)}) collective-permute-start(bf16[2,512,512]{2,1,0:T(8,128)(2,1)} %pad_maximum_fusion), channel_id=1, source_target_pairs={{0,2},{1,3},{4,6},{5,7},{8,10},{9,11},{12,14},{13,15},{16,18},{17,... | collective-permute-start | bytes 3145736 | tf_op jit(solution)/shard_map/ppermute | solution.py:1583
  747.7 2.8 copy-start.12
  753.1 6.6 copy-start.10
  753.5 6.3 copy-start.11
  757.1 5.6 copy-start.1
  (2 other events, 1.9 us)

commit v2 on v1

--- a/solution.py
+++ b/solution.py
@@ -11,6 +11,9 @@
 QB = 128
 PAD = 2
 REACH = 256
+STRIP = 64
+HEAD_SPAN = 512
+FEED_CHUNK = 1024
 VMEM = 56 * 1024 * 1024
 TAIL_VMEM = 60 * 1024 * 1024
 LOW = jnp.bfloat16
@@ -30,7 +33,7 @@
 
 
 def cost_of(micros):
-    return pl.CostEstimate(flops=int(micros * 1e9), bytes_accessed=0, transcendentals=0)
+    return pl.CostEstimate(flops=int(micros * 5e7), bytes_accessed=0, transcendentals=0)
 
 
 def slotted(shape, dtype):
@@ -50,9 +53,17 @@
                 aliases[at] = index
                 at += 1
 
+    def gated(spec):
+        return pl.BlockSpec(spec.block_shape, lambda j, s, *rest: spec.index_map(j * s[5], s, *rest))
+
+    in_specs = [gated(spec) for spec in in_specs]
+    out_specs = [gated(spec) for spec in out_specs]
+
     def run(*refs):
-        front = len(scalars) + count
-        kernel(*refs[:front], *refs[front + len(kept) :])
+        @pl.when(refs[0][5] == 1)
+        def _():
+            front = len(scalars) + count
+            kernel(*refs[:front], *refs[front + len(kept) :])
 
     return pl.pallas_call(
         run,
@@ -71,32 +82,52 @@
     )(*scalars, *inputs, *kept)
 
 
-def toeplitz_kernel(w_ref, t_ref):
+def toeplitz_kernel(flag_ref, w_ref, t_ref):
     width = w_ref.shape[2]
-    half = []
-    for head in range(2):
-        rows = jnp.broadcast_to(w_ref[0, head : head + 1, :], (QB, width))
-        rolled = pltpu.roll(rows, 0, 1, stride=1, stride_axis=0)
-        half.append(rolled.T[QB:, :])
-    t_ref[0] = jnp.concatenate(half, axis=1)
-
-
-def toeplitz(offset_bias):
+
+    @pl.when(flag_ref[0] == 0)
+    def _():
+        t_ref[...] = jnp.zeros_like(t_ref)
+
+    @pl.when(flag_ref[0] == 1)
+    def _():
+        half = []
+        for head in range(2):
+            rows = jnp.broadcast_to(w_ref[0, head : head + 1, :], (QB, width))
+            rolled = pltpu.roll(rows, 0, 1, stride=1, stride_axis=0)
+            half.append(rolled.T[QB:, :])
+        t_ref[0] = jnp.concatenate(half, axis=1)
+
+
+def toeplitz(flag, offset_bias):
     heads, width = offset_bias.shape
     pairs = heads // 2
     return pl.pallas_call(
         toeplitz_kernel,
-        grid=(pairs,),
-        in_specs=[pl.BlockSpec((1, 2, width), lambda p: (p, 0, 0))],
-        out_specs=pl.BlockSpec((1, width - QB, 2 * QB), lambda p: (p, 0, 0)),
+        grid_spec=pltpu.PrefetchScalarGridSpec(
+            num_scalar_prefetch=1,
+            grid=(pairs,),
+            in_specs=[pl.BlockSpec((1, 2, width), lambda p, s: (p, 0, 0))],
+            out_specs=pl.BlockSpec((1, width - QB, 2 * QB), lambda p, s: (p, 0, 0)),
+        ),
         out_shape=jax.ShapeDtypeStruct((pairs, width - QB, 2 * QB), F32),
         compiler_params=params(),
         cost_estimate=cost_of(6),
         name="toeplitz",
-    )(offset_bias.reshape(pairs, 2, width))
-
-
-def diagonal_kernel(a_ref, s_ref):
+    )(flag, offset_bias.reshape(pairs, 2, width))
+
+
+def diagonal_kernel(flag_ref, a_ref, s_ref):
+    @pl.when(flag_ref[0] == 0)
+    def _():
+        s_ref[...] = jnp.zeros_like(s_ref)
+
+    @pl.when(flag_ref[0] == 1)
+    def _():
+        sum_diagonals(a_ref, s_ref)
+
+
+def sum_diagonals(a_ref, s_ref):
     total = a_ref[0, 0]
     for extra in range(1, a_ref.shape[0]):
         total = total + a_ref[extra, 0]
@@ -117,19 +148,22 @@
         s_ref[0, head : head + 1, :] = jnp.sum(aligned, axis=0, keepdims=True)
 
 
-def diagonals(tables, steps):
+def diagonals(flag, tables, steps):
     _, pairs, rows, _ = tables.shape
     width = rows + QB
     out = pl.pallas_call(
         diagonal_kernel,
-        grid=(pairs,),
-        in_specs=[pl.BlockSpec((steps, 1, rows, 2 * QB), lambda p: (0, p, 0, 0))],
-        out_specs=pl.BlockSpec((1, 2, width), lambda p: (p, 0, 0)),
+        grid_spec=pltpu.PrefetchScalarGridSpec(
+            num_scalar_prefetch=1,
+            grid=(pairs,),
+            in_specs=[pl.BlockSpec((steps, 1, rows, 2 * QB), lambda p, s: (0, p * s[0], 0, 0))],
+            out_specs=pl.BlockSpec((1, 2, width), lambda p, s: (p, 0, 0)),
+        ),
         out_shape=jax.ShapeDtypeStruct((pairs, 2, width), F32),
         compiler_params=params(),
         cost_estimate=cost_of(10),
         name="diagonals",
-    )(tables)
+    )(flag, tables)
     return out.reshape(2 * pairs, width)
 
 
@@ -178,12 +212,13 @@
 def attend_kernel(halo_count, info, seg_ref, *refs):
     if halo_count:
         segq_ref, q_ref, k_ref, v_ref, t_ref, kh_ref, vh_ref, o_ref, lse_ref, kk_ref, vk_ref = refs[:11]
-        segk_ref, kp_ref, vp_ref, vt_ref = refs[11:]
+        segk_ref, kp_ref, vp_ref, vt_ref, mask_ref, score_ref, prob_ref, stat_ref = refs[11:]
+        kh_ref, vh_ref = kh_ref.at[0], vh_ref.at[0]
         kk_ref[0] = kh_ref[...]
         vk_ref[0] = vh_ref[...]
     else:
         segq_ref, q_ref, k_ref, v_ref, t_ref, o_ref, lse_ref = refs[:7]
-        segk_ref, kp_ref, vp_ref, vt_ref = refs[7:]
+        segk_ref, kp_ref, vp_ref, vt_ref, mask_ref, score_ref, prob_ref, stat_ref = refs[7:]
         kh_ref = vh_ref = None
     rows = q_ref.shape[1]
     pairs = q_ref.shape[2] // (2 * DH)
@@ -203,38 +238,60 @@
         mine = pl.ds(pl.multiple_of(i * QB, QB), QB)
         shifted = pl.ds((2 - reach) * QB, span)
         allowed = segk_ref[keys, :] == segq_ref[pl.ds(at, 1), :]
-        allowed = jnp.concatenate([allowed, allowed], axis=1)
+        mask_ref[:span, :] = jnp.where(allowed, 0.0, -jnp.inf)
         for pair in range(pairs):
             lanes = slice(pair * 2 * DH, (pair + 1) * 2 * DH)
             both = two_heads(q_ref[0, mine, lanes] * LOW(0.125), first)
-            scores = dot_nt(kp_ref[keys, lanes], both) + t_ref[pair, shifted, :]
-            scores = jnp.where(allowed, scores, -jnp.inf)
-            highest = jnp.max(scores, axis=0, keepdims=True)
-            weights = jnp.exp(scores - highest)
-            totals = jnp.sum(weights, axis=0, keepdims=True)
-            probs = (weights * (1.0 / totals)).astype(LOW)
-            turned = dot_nn(vt_ref[lanes, keys], probs)
-            o_ref[0, mine, lanes] = joined_heads(turned).astype(LOW)
-            lse_ref[0, pair, pl.ds(i, 1), :] = highest + jnp.log(totals)
+            score_ref[pair, :span, :] = dot_nt(kp_ref[keys, lanes], both) + t_ref[pair, shifted, :]
+        for pair in range(pairs):
+            lanes = slice(pair * 2 * DH, (pair + 1) * 2 * DH)
+            stats = []
+            for head in range(2):
+                side = slice(head * QB, (head + 1) * QB)
+                top = None
+                for strip in range(0, span, STRIP):
+                    piece = slice(strip, strip + STRIP)
+                    masked = score_ref[pair, piece, side] + mask_ref[piece, :]
+                    score_ref[pair, piece, side] = masked
+                    peak = jnp.max(masked.reshape(STRIP // 8, 8, QB), axis=0)
+                    top = peak if top is None else jnp.maximum(top, peak)
+                highest = jnp.max(top, axis=0, keepdims=True)
+                total = None
+                for strip in range(0, span, STRIP):
+                    piece = slice(strip, strip + STRIP)
+                    weights = jnp.exp(score_ref[pair, piece, side] - highest)
+                    prob_ref[pair, piece, side] = weights.astype(LOW)
+                    mass = jnp.sum(weights.reshape(STRIP // 8, 8, QB), axis=0)
+                    total = mass if total is None else total + mass
+                totals = jnp.sum(total, axis=0, keepdims=True)
+                stat_ref[2 * pair + head : 2 * pair + head + 1, :] = 1.0 / totals
+                stats.append(highest + jnp.log(totals))
+            lse_ref[0, pair, pl.ds(i, 1), :] = jnp.concatenate(stats, axis=1)
+        for pair in range(pairs):
+            lanes = slice(pair * 2 * DH, (pair + 1) * 2 * DH)
+            turned = dot_nn(vt_ref[lanes, keys], prob_ref[pair, :span, :])
+            upper = turned[:DH, :QB] * stat_ref[2 * pair : 2 * pair + 1, :]
+            lower = turned[DH:, QB:] * stat_ref[2 * pair + 1 : 2 * pair + 2, :]
+            o_ref[0, mine, lanes] = jnp.concatenate([upper, lower], axis=0).T.astype(LOW)
 
     visit_blocks(seg_ref, info[2], rows // QB, block)
 
 
 def head_specs(rows, span, groups, halo_count):
     column = lambda part: pl.BlockSpec((1, rows, span), lambda g, s, t: (s[1], 0, g + part * groups))
-    halo = lambda part: pl.BlockSpec((halo_count, span), lambda g, s, t: (0, g + part * groups))
+    halo = lambda part: pl.BlockSpec((1, halo_count, span), lambda g, s, t: (part, 0, g))
     return column, halo
 
 
 def attend(info, segments, qkv, halo, bias, previous):
     _, rows, width = qkv.shape
     width = width // 3
-    span = min(256, width)
+    span = min(HEAD_SPAN, width)
     groups = width // span
     pairs = span // (2 * DH)
     count = rows // QB
     blocks = segments.shape[0] // QB
-    halo_count = 0 if halo is None else halo.shape[0]
+    halo_count = 0 if halo is None else halo.shape[1]
     column, halo_spec = head_specs(rows, span, groups, halo_count)
     slot_pairs = pl.BlockSpec((1, pairs, count, 2 * QB), lambda g, s, t: (s[1], g, 0, 0))
     in_specs = [
@@ -267,6 +324,10 @@
             pltpu.VMEM((blocks * QB, span), LOW),
             pltpu.VMEM((blocks * QB, span), LOW),
             pltpu.VMEM((span, blocks * QB), LOW),
+            pltpu.VMEM((5 * QB, QB), F32),
+            pltpu.VMEM((pairs, 5 * QB, 2 * QB), F32),
+            pltpu.VMEM((pairs, 5 * QB, 2 * QB), LOW),
+            pltpu.VMEM((8, QB), F32),
         ],
         "attend",
         24,
@@ -335,7 +396,7 @@
 def attend_back(info, segments, qkv, halo_kept, grad_context, bias, lse, previous):
     _, rows, width = qkv.shape
     width = width // 3
-    span = min(256, width)
+    span = min(HEAD_SPAN, width)
     groups = width // span
     pairs = span // (2 * DH)
     count = rows // QB
@@ -387,6 +448,32 @@
     )
 
 
+def exchange_kernel(give_ref, get_ref, send_sem, recv_sem):
+    peer = {"tensor": 1 - lax.axis_index("tensor")}
+    barrier = pltpu.get_barrier_semaphore()
+    pl.semaphore_signal(barrier, inc=1, device_id=peer, device_id_type=pl.DeviceIdType.MESH)
+    pl.semaphore_wait(barrier, 1)
+    copy = pltpu.make_async_remote_copy(
+        src_ref=give_ref, dst_ref=get_ref, send_sem=send_sem, recv_sem=recv_sem,
+        device_id=peer, device_id_type=pl.DeviceIdType.MESH,
+    )
+    copy.start()
+    copy.wait()
+
+
+def exchanged(value):
+    return pl.pallas_call(
+        exchange_kernel,
+        in_specs=[pl.BlockSpec(memory_space=pl.ANY)],
+        out_specs=pl.BlockSpec(memory_space=pl.ANY),
+        out_shape=jax.ShapeDtypeStruct(value.shape, value.dtype),
+        scratch_shapes=[pltpu.SemaphoreType.DMA, pltpu.SemaphoreType.DMA],
+        compiler_params=pltpu.CompilerParams(collective_id=1, has_side_effects=True),
+        cost_estimate=cost_of(3),
+        name="exchange",
+    )(value)
+
+
 def mean_of(block):
     return jnp.mean(block, axis=-1, keepdims=True)
 
@@ -400,15 +487,9 @@
 
 
 def gelu_parts(u):
-    depth = jnp.abs(u) * 0.7071067811865476
-    divisor = 1.0 + 0.3275911 * depth
-    t = pl.reciprocal(divisor, approx=True)
-    t = t * (2.0 - divisor * t)
-    series = ((((1.061405429 * t - 1.453152027) * t + 1.421413741) * t - 0.284496736) * t + 0.254829592) * t
-    bell = jnp.exp(-0.5 * u * u)
-    tail = 0.5 * series * bell
-    below = jnp.where(u >= 0.0, 1.0 - tail, tail)
-    return u * below, below + u * bell * 0.3989422804014327
+    bell = jnp.exp(u * u * -0.5)
+    below = 0.5 + 0.5 * lax.erf(u * 0.7071067811865476)
+    return u * below, below + u * (bell * 0.3989422804014327)
 
 
 def enter_kernel(info, first_ref, second_ref, gain_ref, shift_ref, own_ref, oth_ref, x_ref, e_ref, qkv_ref, halo_ref):
@@ -431,9 +512,9 @@
         lanes = slice(part * half, (part + 1) * half)
         block = (dot_nn(e, weight[...]) + shift_ref[:, lanes]).astype(LOW)
         qkv_ref[0, :, lanes] = block
-    start = pl.ds(pl.multiple_of(info[4], QB), halo_ref.shape[0])
-    halo_ref[:, :half] = qkv_ref[0, start, half:]
-    halo_ref[:, half:] = qkv_ref[0, start, :half]
+    start = pl.ds(pl.multiple_of(info[4], QB), halo_ref.shape[1])
+    halo_ref[0, :, :half] = qkv_ref[0, start, half:]
+    halo_ref[0, :, half:] = qkv_ref[0, start, :half]
 
 
 def enter(info, first, second, gain, shift, own, oth, previous):
@@ -459,13 +540,13 @@
             slotted((rows, width), LOW),
             slotted((rows, width), LOW),
             slotted((rows, 6 * half), LOW),
-            jax.ShapeDtypeStruct((REACH, 4 * half), LOW),
+            jax.ShapeDtypeStruct((2, REACH, 2 * half), LOW),
         ],
         [
             kept,
             kept,
             pl.BlockSpec((1, rows, 2 * half), lambda m, s: (s[1], 0, m)),
-            pl.BlockSpec((REACH, 2 * half), lambda m, s: (0, jnp.maximum(m - 1, 0))),
+            pl.BlockSpec((1, REACH, 2 * half), lambda m, s: (jnp.maximum(m - 1, 0), 0, 0)),
         ],
         keep,
         (3,),
@@ -477,7 +558,7 @@
 
 def feed_kernel(
     info, x_ref, c_ref, wo_own, wo_oth, up_own, up_oth, down_own, down_oth, bias_ref, gain_ref, shift_ref,
-    f_ref, slope_ref, n_ref, one_ref, two_ref, out_ref, acc_ref, carry_ref
+    f_ref, slope_ref, n_ref, one_ref, two_ref, out_ref, acc_ref, carry_ref, hidden_ref
 ):
     j = pl.program_id(0)
     steps = pl.num_programs(0)
@@ -495,7 +576,7 @@
         @pl.when(info[0] == 1)
         def _():
             before = joined + shift_ref[0:1, :]
-            one_ref[0] = before
+            one_ref[0] = before.astype(LOW)
             center = before - mean_of(before)
             normed = center * lax.rsqrt(mean_of(center * center) + 1e-05) * gain_ref[0:1, :] + shift_ref[2:3, :]
             carry_ref[...] = normed
@@ -503,29 +584,48 @@
 
         @pl.when(info[0] == 0)
         def _():
-            one_ref[0] = joined
+            one_ref[0] = joined.astype(LOW)
             carry_ref[...] = joined
             n_ref[0] = (joined * rms_scale(joined) * gain_ref[1:2, :]).astype(LOW)
 
         acc_ref[...] = jnp.zeros_like(acc_ref)
 
-    def part(up, down):
-        for at in range(0, rows, 256):
-            piece = slice(at, at + 256)
-            u = dot_nn(n_ref[0, piece, :], up[...]) + bias_ref[...]
-            f, slope = gelu_parts(u)
-            low = f.astype(LOW)
-            f_ref[0, piece, :] = low
-            slope_ref[0, piece, :] = slope.astype(LOW)
-            acc_ref[piece, :] += dot_nn(low, down[...])
-
-    @pl.when(j < steps // 2)
-    def _():
-        part(up_own, down_own)
-
-    @pl.when(j >= steps // 2)
-    def _():
-        part(up_oth, down_oth)
+    each = (steps - 1) // 2
+    now = lax.rem(j, 2)
+
+    def rise(up):
+        u = dot_nn(n_ref[0], up[...]) + bias_ref[...]
+        f, slope = gelu_parts(u)
+        low = f.astype(LOW)
+        f_ref[0] = low
+        hidden_ref[now] = low
+        slope_ref[0] = slope.astype(LOW)
+
+    def fall(down):
+        acc_ref[...] += dot_nn(hidden_ref[1 - now], down[...])
+
+    @pl.when(j == 0)
+    def _():
+        rise(up_own)
+
+    @pl.when((j > 0) & (j < each))
+    def _():
+        rise(up_own)
+        fall(down_own)
+
+    @pl.when(j == each)
+    def _():
+        rise(up_oth)
+        fall(down_own)
+
+    @pl.when((j > each) & (j < steps - 1))
+    def _():
+        rise(up_oth)
+        fall(down_oth)
+
+    @pl.when(j == steps - 1)
+    def _():
+        fall(down_oth)
 
     @pl.when(j == steps - 1)
     def _():
@@ -534,14 +634,14 @@
         @pl.when(info[0] == 1)
         def _():
             before = joined + shift_ref[1:2, :]
-            two_ref[0] = before
+            two_ref[0] = before.astype(LOW)
             center = before - mean_of(before)
             normed = center * lax.rsqrt(mean_of(center * center) + 1e-05) * gain_ref[1:2, :] + shift_ref[3:4, :]
             out_ref[...] = normed.astype(LOW)
 
         @pl.when(info[0] == 0)
         def _():
-            two_ref[0] = joined
+            two_ref[0] = joined.astype(LOW)
             out_ref[...] = joined.astype(LOW)
 
 
@@ -555,11 +655,16 @@
 def feed(info, x, context, wo, up, down, bias, gains, shifts, previous):
     _, rows, width = x.shape
     hidden = up[0].shape[1]
-    chunk = min(512, hidden)
-    steps, near, far = split_steps(hidden, chunk)
+    chunk = min(FEED_CHUNK, hidden)
+    each = hidden // chunk
+    steps = 2 * each + 1
+    rise = lambda j: jnp.minimum(j, 2 * each - 1)
+    fall = lambda j: jnp.maximum(j - 1, 0)
+    near = lambda j: jnp.minimum(j, each - 1)
+    far = lambda j: jnp.maximum(j - each, 0)
     kept = pl.BlockSpec((1, rows, width), lambda j, s: (s[1], 0, 0))
     fixed = lambda a: pl.BlockSpec(a.shape, lambda j, s: (0, 0))
-    moving = pl.BlockSpec((1, rows, chunk), lambda j, s: (s[1], 0, j))
+    moving = pl.BlockSpec((1, rows, chunk), lambda j, s: (s[1], 0, rise(j)))
     keep = None if previous is None else list(previous) + [None]
     return call_with_slots(
         feed_kernel,
@@ -570,11 +675,11 @@
             kept,
             fixed(wo[0]),
             fixed(wo[1]),
-            pl.BlockSpec((width, chunk), lambda j, s: (0, near(j))),
-            pl.BlockSpec((width, chunk), lambda j, s: (0, far(j))),
-            pl.BlockSpec((chunk, width), lambda j, s: (near(j), 0)),
-            pl.BlockSpec((chunk, width), lambda j, s: (far(j), 0)),
-            pl.BlockSpec((1, chunk), lambda j, s: (0, j)),
+            pl.BlockSpec((width, chunk), lambda j, s: (0, near(rise(j)))),
+            pl.BlockSpec((width, chunk), lambda j, s: (0, far(rise(j)))),
+            pl.BlockSpec((chunk, width), lambda j, s: (near(fall(j)), 0)),
+            pl.BlockSpec((chunk, width), lambda j, s: (far(fall(j)), 0)),
+            pl.BlockSpec((1, chunk), lambda j, s: (0, rise(j))),
             fixed(gains),
             fixed(shifts),
         ],
@@ -582,14 +687,18 @@
             slotted((rows, 2 * hidden), LOW),
             slotted((rows, 2 * hidden), LOW),
             slotted((rows, width), LOW),
-            slotted((rows, width), F32),
-            slotted((rows, width), F32),
+            slotted((rows, width), LOW),
+            slotted((rows, width), LOW),
             jax.ShapeDtypeStruct((rows, width), LOW),
         ],
         [moving, moving, kept, kept, kept, pl.BlockSpec((rows, width), lambda j, s: (0, 0))],
         keep,
         (steps,),
-        [pltpu.VMEM((rows, width), F32), pltpu.VMEM((rows, width), F32)],
+        [
+            pltpu.VMEM((rows, width), F32),
+            pltpu.VMEM((rows, width), F32),
+            pltpu.VMEM((2, rows, chunk), LOW),
+        ],
         "feed",
         29,
     )
@@ -629,7 +738,7 @@
         @pl.when(info[0] == 1)
         def _():
             grad = got_ref[...].astype(F32)
-            back, gain = layer_norm_back(two_ref[0], grad, gain_ref[1:2, :])
+            back, gain = layer_norm_back(two_ref[0].astype(F32), grad, gain_ref[1:2, :])
             stat_ref[0, 1:2, :] = gain
             stat_ref[0, 5:6, :] = sum_rows(grad)
             stat_ref[0, 3:4, :] = sum_rows(back)
@@ -643,12 +752,9 @@
             dy_ref[0] = grad.astype(LOW)
 
     def part(up, down):
-        for at in range(0, rows, 256):
-            piece = slice(at, at + 256)
-            grad = dot_nt(dy_ref[0, piece, :], down[...])
-            low = (grad * slope_ref[0, piece, :].astype(F32)).astype(LOW)
-            du_ref[0, piece, :] = low
-            acc_ref[piece, :] += dot_nt(low, up[...])
+        grad = dot_nt(dy_ref[0], down[...])
+        du_ref[0] = (grad * slope_ref[0].astype(F32)).astype(LOW)
+        acc_ref[...] += dot_nt(du_ref[0], up[...])
         bias_ref[0] = sum_rows(du_ref[0].astype(F32))
 
     @pl.when(j < steps // 2)
@@ -664,7 +770,7 @@
         @pl.when(info[0] == 1)
         def _():
             grad = acc_ref[...] + carry_ref[...]
-            back, gain = layer_norm_back(one_ref[0], grad, gain_ref[0:1, :])
+            back, gain = layer_norm_back(one_ref[0].astype(F32), grad, gain_ref[0:1, :])
             stat_ref[0, 0:1, :] = gain
             stat_ref[0, 4:5, :] = sum_rows(grad)
             stat_ref[0, 2:3, :] = sum_rows(back)
@@ -672,7 +778,7 @@
 
         @pl.when(info[0] == 0)
         def _():
-            back, gain = rms_norm_back(one_ref[0], acc_ref[...], gain_ref[1:2, :])
+            back, gain = rms_norm_back(one_ref[0].astype(F32), acc_ref[...], gain_ref[1:2, :])
             stat_ref[0, 1:2, :] = gain
             dz_ref[...] = carry_ref[...] + back
 
@@ -685,7 +791,7 @@
 def feed_back(info, got, mine, other, one, two, slope, wo, up, down, gains, previous):
     _, rows, width = one.shape
     hidden = up[0].shape[1]
-    chunk = min(512, hidden)
+    chunk = min(FEED_CHUNK, hidden)
     steps, near, far = split_steps(hidden, chunk)
     kept = pl.BlockSpec((1, rows, width), lambda j, s: (s[1], 0, 0))
     fixed = lambda a: pl.BlockSpec(a.shape, lambda j, s: (0, 0))
@@ -976,8 +1082,8 @@
     bucket_hits = (buckets[None, :] == jnp.arange(bias_table.shape[1])[:, None]).astype(jnp.float32)
     offset_bias = jnp.dot(bias_table, bucket_hits, precision=lax.Precision.HIGHEST)
     near = length - 1 - 3 * QB
-    bias = toeplitz(offset_bias[:, near : near + 6 * QB])
-    info = jnp.array([0, 0, PAD, 0, 0], jnp.int32)
+    bias = toeplitz(jnp.ones((1,), jnp.int32), offset_bias[:, near : near + 6 * QB])
+    info = jnp.array([0, 0, PAD, 0, 0, 1], jnp.int32)
     segment_rows = segment_ids[:, 0]
 
     def middle_part(residual_in, branch_in, gain_in, shift_in):
@@ -1140,7 +1246,7 @@
         table_sum,
     ) = running_terms
     near_hits = bucket_hits[:, near : near + 6 * QB]
-    table_sum = jnp.dot(diagonals(table_sum[None], 1), near_hits.T, precision=lax.Precision.HIGHEST) * (
+    table_sum = jnp.dot(diagonals(jnp.ones((1,), jnp.int32), table_sum[None], 1), near_hits.T, precision=lax.Precision.HIGHEST) * (
         1.0 - weighting
     )
     weights_out = (
@@ -1499,7 +1605,8 @@
 
     near = length - 1 - 3 * QB
     near_hits = (buckets[None, near : near + 6 * QB] == jnp.arange(bucket_count)[:, None]).astype(F32)
-    bias = toeplitz(jnp.dot(table_both, near_hits, precision=lax.Precision.HIGHEST))
+    trailing = jnp.reshape(1 - lead, (1,))
+    bias = toeplitz(trailing, jnp.dot(table_both, near_hits, precision=lax.Precision.HIGHEST))
 
     window = rows + REACH
     base = core * (length - window)
@@ -1513,77 +1620,78 @@
     halo_block = jnp.where(core == 0, PAD + rows // QB, PAD)
     edge = jnp.where(core == 0, rows - REACH, 0)
 
-    def info_of(slot):
-        return jnp.stack([lead, slot, own_block, halo_block, edge]).astype(jnp.int32)
-
-    received = jnp.zeros((rows, width), LOW)
+    def info_of(turn, micro):
+        active = jnp.where(section == turn, 1, 0)
+        slot = jnp.where(active == 1, micro, micro_count)
+        return jnp.stack([lead, slot, own_block, halo_block, edge, active]).astype(jnp.int32)
+
+    turns = [(turn, micro) for turn in range(2) for micro in range(micro_count)]
+    received = [jnp.zeros((rows, width), LOW)] * micro_count
     entered = attended = fed = None
     results = []
     finished = []
-    for moment in range(micro_count + 1):
-        slot = jnp.where(leading, moment, (moment + micro_count) % (micro_count + 1))
-        info = info_of(slot)
-        micro = jnp.minimum(slot, micro_count - 1)
-        own_rows = layer_input[min(moment, micro_count - 1), 0]
-        row_segments = lax.dynamic_index_in_dim(segments, micro, 0, keepdims=False)
-        *entered, halo = enter(info, own_rows, received, entry_gain, qkv_shift, qkv_own, qkv_oth, entered)
-        halo = swapped(halo, "tensor", 1)
-        attended = attend(info, row_segments, entered[2], halo, bias, attended)
-        if moment < micro_count:
-            info, remote_grads[moment] = lax.optimization_barrier((info, remote_grads[moment]))
+    for turn, micro in turns:
+        info = info_of(turn, micro)
+        if turn + micro > 0:
+            info, _ = lax.optimization_barrier((info, result))
+        *entered, halo = enter(
+            info, layer_input[micro, 0], received[micro], entry_gain, qkv_shift, qkv_own, qkv_oth, entered
+        )
+        halo = exchanged(halo)
+        if turn == 0 and micro == 0:
+            later, _ = lax.optimization_barrier((decoder_grads[0, 1, 0], (remote_grads[0], halo)))
+            remote_grads.append(lax.ppermute(later, "section", [(0, 1)]))
+        attended = attend(info, segments[micro], entered[2], halo, bias, attended)
+        if turn == 0 and micro == 0:
+            info, remote_grads[1] = lax.optimization_barrier((info, remote_grads[1]))
         *fed, result = feed(
             info, entered[0], attended[0], wo, up, down, ffn_both, gains, bert_shift, fed
         )
-        results.append(result)
-        if moment == 0:
-            received = lax.ppermute(result, "section", [(0, 1)])
-            later, received = lax.optimization_barrier((decoder_grads[0, 1, 0], received))
-            remote_grads.append(lax.ppermute(later, "section", [(0, 1)]))
-        elif moment < micro_count:
-            received = lax.ppermute(result, "section", [(0, 1), (1, 0)])
-            finished.append(received)
-    finished.append(lax.ppermute(result, "section", [(1, 0)]))
+        if turn == 0:
+            received = list(received)
+            received[micro] = lax.ppermute(result, "section", [(0, 1)])
+        else:
+            results.append(result)
+            finished.append(lax.ppermute(result, "section", [(1, 0)]))
     x_saved, e_saved, qkv_saved = entered
     context, lse, *halo_saved = attended
     f_saved, slope_saved, n_saved, one_saved, two_saved = fed
 
-    received = jnp.zeros((rows, width), LOW)
+    received = [jnp.zeros((rows, width), LOW)] * micro_count
     feed_kept = table_kept = entry_kept = None
     input_low = []
     input_lower = []
-    for moment in range(micro_count + 1):
-        slot = jnp.where(leading, (moment + micro_count) % (micro_count + 1), moment)
-        info = info_of(slot)
-        micro = jnp.minimum(slot, micro_count - 1)
-        at = min(moment, micro_count - 1)
-        row_segments = lax.dynamic_index_in_dim(segments, micro, 0, keepdims=False)
+    for step, (turn, micro) in enumerate([(1 - turn, micro) for turn, micro in turns]):
+        info = info_of(turn, micro)
+        if step > 0:
+            info, _ = lax.optimization_barrier((info, low))
         *feed_kept, dz, grad_context = feed_back(
-            info, received, decoder_grads[0, at, 0], remote_grads[at], one_saved, two_saved, slope_saved,
-            wo, up, down, gains, feed_kept,
+            info, received[micro], decoder_grads[0, micro, 0], remote_grads[micro], one_saved, two_saved,
+            slope_saved, wo, up, down, gains, feed_kept,
         )
         dq, dk, dv, table_kept, far = attend_back(
-            info, row_segments, qkv_saved, halo_saved, grad_context, bias, lse, table_kept
-        )
-        far = swapped(far, "tensor", 1)
-        if moment == 0:
-            info, finished[-1] = lax.optimization_barrier((info, finished[-1]))
+            info, segments[micro], qkv_saved, halo_saved, grad_context, bias, lse, table_kept
+        )
+        far = exchanged(far)
+        if turn == 1 and micro == 0:
+            info, *finished = lax.optimization_barrier((info, *finished))
         *entry_kept, low, lower = enter_back(
             info, dq, dk, dv, far, x_saved, dz, qkv_own, qkv_oth, entry_gain, entry_kept
         )
-        if moment >= 1:
+        if turn == 1:
+            received = list(received)
+            received[micro] = lax.ppermute(low, "section", [(1, 0)])
+        else:
             input_low.append(low)
             input_lower.append(lower)
-        if moment < micro_count:
-            received = lax.ppermute(low, "section", [(1, 0)])
+    dy_saved, du_saved, db_saved, stat_feed, stat_bias = feed_kept
     dqkv_saved, stat_entry = entry_kept
-
-    dy_saved, du_saved, db_saved, stat_feed, stat_bias = feed_kept
 
     half = width // 2
     upper = lax.ppermute(jnp.stack(input_low)[:, :, half:], "section", [(0, 1)]).astype(F32)
     input_grad = jnp.where(leading, jnp.stack(input_lower), upper)[:, None]
 
-    near_table = jnp.dot(diagonals(table_kept, micro_count), near_hits.T, precision=lax.Precision.HIGHEST)
+    near_table = jnp.dot(diagonals(trailing, table_kept, micro_count), near_hits.T, precision=lax.Precision.HIGHEST)
 
     def placed(pair):
         return jnp.where(core == 0, pair, pair[::-1])
@@ -1621,7 +1729,7 @@
     gain_all, shift_all, head_all, bias_all, table_all = unpacked
     mine = lambda value: lax.dynamic_index_in_dim(value, core, 0, keepdims=False)
     return (
-        jnp.where(leading, jnp.stack(finished), jnp.stack(results[1:]))[None, :, None],
+        jnp.where(leading, jnp.stack(finished), jnp.stack(results))[None, :, None],
         input_grad,
         qkv_sum[None],
         out_sum[None],

time: 774 us -> 667 us (0.86)
  Pallas kernels: 582 us -> 515 us
  waiting for transfers between devices: 106 us -> 72.6 us
    pallas_call x18 -> x24, Pallas kernels: 385 us -> 316 us  [call_with_slots(): pl.pallas_call(run, grid_spec=pltpu.PrefetchScalarGridSpec(num_scalar_pre...]
    ppermute x4, waiting for transfers between devices: 87.5 us -> 30.3 us  [the longest x2 30.3 us: paired_body(): received[micro] = lax.ppermute(low, 'section', [(1, 0)])]
    ppermute x1 -> x2, waiting for transfers between devices: 0.01 us -> 39.9 us  [paired_body(): finished.append(lax.ppermute(result, 'section', [(1, 0)]))]
    pallas_call x2 -> x10, Pallas kernels: 17.6 us -> 33.1 us  [the longest x8 24.3 us: exchanged(): pl.pallas_call(exchange_kernel, in_specs=[pl.BlockSpec(memory_space=pl.AN...]
    pallas_call x1, Pallas kernels: 179 us -> 166 us  [summed_grads(): pl.pallas_call(grads_kernel, in_specs=[anywhere] * 8 + [local], out_specs...]
    ppermute x1, waiting for transfers between devices: 10.7 us -> 0.01 us  [paired_body(): remote_grads.append(lax.ppermute(later, 'section', [(0, 1)]))]
    ppermute x11 -> x5, waiting for transfers between devices: 7.91 us -> 0.01 us  [swapped(): return lax.ppermute(value, axis, pairs)]
  transfers between devices with their start and end apart: 19 -> 14, of which waited for: 8 -> 3; matrix products, arithmetic and copies ran while one was open for 4% -> 5% of each run, Pallas kernels for 38% -> 63%
where the time goes in v2:
time: 667 us; the launch traced here: 662 us
  Pallas kernels  515 us (77%)
  waiting for transfers between devices  72.6 us (11%)
  local copies, waits for them, and re-layouts  39.5 us (6%)
  starting transfers between devices  22.5 us (3%)
  other arithmetic  10.8 us (2%)
    pallas_call x24, Pallas kernels, call_with_slots(): pl.pallas_call(run, grid_spec=pltpu.PrefetchScalarGridSpec(num_scalar_pre...  316 us
    pallas_call x1, Pallas kernels, summed_grads(): pl.pallas_call(grads_kernel, in_specs=[anywhere] * 8 + [local], out_specs...  166 us
    ppermute x2, waiting for transfers between devices, paired_body(): finished.append(lax.ppermute(result, 'section', [(1, 0)]))  39.9 us
    ppermute x2, waiting for transfers between devices, paired_body(): received[micro] = lax.ppermute(low, 'section', [(1, 0)])  30.3 us
    pallas_call x8, Pallas kernels, exchanged(): pl.pallas_call(exchange_kernel, in_specs=[pl.BlockSpec(memory_space=pl.AN...  24.3 us
  transfers between devices with their start and end apart: 14, of which 3 were waited for; matrix products, arithmetic and copies ran while one was open for 5% of the time, Pallas kernels for 63%

profile of v2, /device:TPU:0, one launch (start us, length us, event | category | flops | bytes accessed | tf_op | source)
XLA Modules:
  0.0 662.5 jit_solution(6545300296160905815)
XLA Ops:
  0.7 4.7 copy.93
  5.3 3.2 copy.95.refs_5_.refs_7_
  9.6 3.1 slice_bitcast_fusion.3
  12.7 5.9 collective-permute-start
  18.7 3.0 slice_bitcast_fusion.1
  24.9 9.9 %enter.4 = (bf16[3,512,1024]{2,1,0:T(8,128)(2,1)}, bf16[3,512,1024]{2,1,0:T(8,128)(2,1)}, bf16[3,512,3072]{2,1,0:T(8,128)(2,1)}, bf16[2,256,1024]{2,1,0:T(8,128)(2,1)}) custom-call(s32[6]{0:T(128)} %stack.66.refs_0_, bf16[512,1024]{1,0:T(8,128)(2,1)} %get-tuple-element.302.refs_1_, bf16[512,1024]{1,0:T(8,128)(2,1)} %broadcast_1_refs_2__refs_1_.2.refs_2_.refs_1_, ...), custom_call_target="tpu_custom_call" | custom-call | flops 450000000 | tf_op jit(solution)/shard_map/enter/pallas_call | solution.py:68
  34.8 3.1 exchange.8.refs_7_.refs_8_
  37.9 2.4 collective-permute-done.refs_3_
  40.4 5.4 collective-permute-start.3
  49.2 5.1 toeplitz.1.refs_6_.refs_7_
  54.3 16.6 %attend.4 = (bf16[3,512,1024]{2,1,0:T(8,128)(2,1)}, f32[3,8,4,256]{3,2,1,0:T(4,128)}, bf16[3,256,1024]{2,1,0:T(8,128)(2,1)}, bf16[3,256,1024]{2,1,0:T(8,128)(2,1)}) custom-call(s32[6]{0:T(128)} %stack.66.refs_0_, s32[1280]{0:T(1024)} %get-tuple-element.298.refs_1_, s32[10,128]{1,0:T(8,128)} %bitcast.147, ...), custom_call_target="tpu_custom_call" | custom-call | flops 1200000000 | tf_op jit(solution)/shard_map/attend/pallas_call | solution.py:68
  71.9 24.4 %feed.4 = (bf16[3,512,4096]{2,1,0:T(8,128)(2,1)}, bf16[3,512,4096]{2,1,0:T(8,128)(2,1)}, bf16[3,512,1024]{2,1,0:T(8,128)(2,1)}, bf16[3,512,1024]{2,1,0:T(8,128)(...) custom-call(s32[6]{0:T(128)} %stack.66.refs_0_, ...), custom_call_target="tpu_custom_call" | custom-call | flops 1450000000 | tf_op jit(solution)/shard_map/feed/pallas_call | solution.py:68
  97.7 9.8 %enter.5 = (bf16[3,512,1024]{2,1,0:T(8,128)(2,1)}, bf16[3,512,1024]{2,1,0:T(8,128)(2,1)}, bf16[3,512,3072]{2,1,0:T(8,128)(2,1)}, bf16[2,256,1024]{2,1,0:T(8,128)(2,1)}) custom-call(s32[6]{0:T(128)} %stack.64.refs_0_, bf16[512,1024]{1,0:T(8,128)(2,1)} %get-tuple-element.301.refs_1_, ...), custom_call_target="tpu_custom_call", output_to_operand_aliasing={{0}: (7, {}), {1}: (8, {}), {2}: (9, {})} | custom-call | flops 450000000 | tf_op jit(solution)/shard_map/enter/pallas_call | solution.py:68
  107.5 3.0 exchange.9.refs_7_.refs_8_
  110.5 15.8 %attend.5 = (bf16[3,512,1024]{2,1,0:T(8,128)(2,1)}, f32[3,8,4,256]{3,2,1,0:T(4,128)}, bf16[3,256,1024]{2,1,0:T(8,128)(2,1)}, bf16[3,256,1024]{2,1,0:T(8,128)(2,1)}) custom-call(s32[6]{0:T(128)} %stack.64.refs_0_, s32[1280]{0:T(1024)} %get-tuple-element.297.refs_1_, ...), custom_call_target="tpu_custom_call", output_to_operand_aliasing={{0}: (9, {}), {1}: (10, {}), {2}: (11, {}), {3}: (12, {})} | custom-call | flops 1200000000 | tf_op jit(solution)/shard_map/attend/pallas_call | solution.py:68
  126.3 33.9 %feed.5 = (bf16[3,512,4096]{2,1,0:T(8,128)(2,1)}, bf16[3,512,4096]{2,1,0:T(8,128)(2,1)}, bf16[3,512,1024]{2,1,0:T(8,128)(2,1)}, bf16[3,512,1024]{2,1,0:T(8,128)(...) custom-call(s32[6]{0:T(128)} %stack.64.refs_0_, ...), custom_call_target="tpu_custom_call", output_to_operand_aliasing={{0}: (12, {}), {1}: (13, {}), {2}: (14, {}), {3}: (15, {}),... | custom-call | flops 1450000000 | tf_op jit(solution)/shard_map/feed/pallas_call | solution.py:68
  163.8 4.9 enter.6
  168.7 3.0 exchange.10.refs_7_.refs_8_
  171.7 4.1 attend.6
  175.8 8.8 %feed.6 = (bf16[3,512,4096]{2,1,0:T(8,128)(2,1)}, bf16[3,512,4096]{2,1,0:T(8,128)(2,1)}, bf16[3,512,1024]{2,1,0:T(8,128)(2,1)}, bf16[3,512,1024]{2,1,0:T(8,128)(...) custom-call(s32[6]{0:T(128)} %stack.62.refs_0_, ...), custom_call_target="tpu_custom_call", output_to_operand_aliasing={{0}: (12, {}), {1}: (13, {}), {2}: (14, {}), {3}: (15, {}),... | custom-call | flops 1450000000 | tf_op jit(solution)/shard_map/feed/pallas_call | solution.py:68
  186.8 4.8 enter.7
  191.6 3.0 exchange.11.refs_7_.refs_8_
  194.6 4.1 attend.7
  198.7 8.9 %feed.7 = (bf16[3,512,4096]{2,1,0:T(8,128)(2,1)}, bf16[3,512,4096]{2,1,0:T(8,128)(2,1)}, bf16[3,512,1024]{2,1,0:T(8,128)(2,1)}, bf16[3,512,1024]{2,1,0:T(8,128)(...) custom-call(s32[6]{0:T(128)} %stack.142.refs_0_, ...), custom_call_target="tpu_custom_call", output_to_operand_aliasing={{0}: (12, {}), {1}: (13, {}), {2}: (14, {}), {3}: (15, {}),... | custom-call | flops 1450000000 | tf_op jit(solution)/shard_map/feed/pallas_call | solution.py:68
  209.0 9.3 %feed_back.4 = (bf16[3,512,1024]{2,1,0:T(8,128)(2,1)}, bf16[3,512,4096]{2,1,0:T(8,128)(2,1)}, bf16[3,512,1024]{2,1,0:T(8,128)(2,1)}, f32[3,8,1024]{2,1,0:T(8,128...) custom-call(s32[6]{0:T(128)} %stack.62.refs_0_, ...), custom_call_target="tpu_custom_call" | custom-call | flops 1350000000 | tf_op jit(solution)/shard_map/feed_back/pallas_call | solution.py:68
  218.3 5.8 attend_back.4
  224.1 3.0 exchange.12.refs_4_
  227.1 39.9 %collective-permute-done.10 = bf16[512,1024]{1,0:T(8,128)(2,1)S(1)} collective-permute-done((bf16[512,1024]{1,0:T(8,128)(2,1)}, bf16[512,1024]{1,0:T(8,128)(2,1)S(1)}, u32[]{:S(2)}, u32[]{:S(2)}) %collective-permute-start.10) | collective-permute-done | bytes 1048608 | tf_op jit(solution)/shard_map/ppermute | solution.py:1655
  267.0 6.1 enter_back.4
  274.4 9.7 %feed_back.5 = (bf16[3,512,1024]{2,1,0:T(8,128)(2,1)}, bf16[3,512,4096]{2,1,0:T(8,128)(2,1)}, bf16[3,512,1024]{2,1,0:T(8,128)(2,1)}, f32[3,8,1024]{2,1,0:T(8,128...) custom-call(s32[6]{0:T(128)} %stack.142.refs_0_, ...), custom_call_target="tpu_custom_call", output_to_operand_aliasing={{0}: (14, {}), {1}: (15, {}), {2}: (16, {}), {3}: (17, {}),... | custom-call | flops 1350000000 | tf_op jit(solution)/shard_map/feed_back/pallas_call | solution.py:68
  284.1 5.9 attend_back.5
  290.1 3.0 exchange.13.refs_4_
  293.1 6.2 enter_back.5
  300.7 3.6 maximum_select_fusion
  304.3 30.3 %collective-permute-done.11.refs_1_ = bf16[512,1024]{1,0:T(8,128)(2,1)S(1)} collective-permute-done((bf16[512,1024]{1,0:T(8,128)(2,1)}, bf16[512,1024]{1,0:T(8,128)(2,1)S(1)}, u32[]{:S(2)}, u32[]{:S(2)}) %collective-permute-start.11) | collective-permute-done | bytes 1048608 | tf_op jit(solution)/shard_map/ppermute | solution.py:1683
  335.5 25.7 %feed_back.6 = (bf16[3,512,1024]{2,1,0:T(8,128)(2,1)}, bf16[3,512,4096]{2,1,0:T(8,128)(2,1)}, bf16[3,512,1024]{2,1,0:T(8,128)(2,1)}, f32[3,8,1024]{2,1,0:T(8,128...) custom-call(s32[6]{0:T(128)} %stack.66.refs_0_, ...), custom_call_target="tpu_custom_call", output_to_operand_aliasing={{0}: (14, {}), {1}: (15, {}), {2}: (16, {}), {3}: (17, {}),... | custom-call | flops 1350000000 | tf_op jit(solution)/shard_map/feed_back/pallas_call | solution.py:68
  361.2 26.7 %attend_back.6 = (bf16[512,1024]{1,0:T(8,128)(2,1)}, bf16[512,1024]{1,0:T(8,128)(2,1)}, bf16[512,1024]{1,0:T(8,128)(2,1)}, f32[3,8,640,256]{3,2,1,0:T(8,128)}, bf16[2,256,1024]{2,1,0:T(8,128)(2,1)}) custom-call(s32[6]{0:T(128)} %stack.66.refs_0_, s32[1280]{0:T(1024)} %get-tuple-element.298.refs_1_, ...), custom_call_target="tpu_custom_call", output_to_operand_aliasing={{3}: (11, {})} | custom-call | flops 1300000000 | tf_op jit(solution)/shard_map/attend_back/pallas_call | solution.py:68
  387.8 3.0 exchange.14.refs_4_
  390.9 11.8 %enter_back.6 = (bf16[3,512,3072]{2,1,0:T(8,128)(2,1)}, f32[3,8,1024]{2,1,0:T(8,128)}, bf16[512,1024]{1,0:T(8,128)(2,1)}, f32[512,512]{1,0:T(8,128)}) custom-call(s32[6]{0:T(128)} %stack.66.refs_0_, bf16[512,1024]{1,0:T(8,128)(2,1)} %get-tuple-element.236.refs_1_, ...), custom_call_target="tpu_custom_call", output_to_operand_aliasing={{0}: (10, {}), {1}: (11, {})} | custom-call | flops 600000000 | tf_op jit(solution)/shard_map/enter_back/pallas_call | solution.py:68
  403.7 25.9 %feed_back.7 = (bf16[3,512,1024]{2,1,0:T(8,128)(2,1)}, bf16[3,512,4096]{2,1,0:T(8,128)(2,1)}, bf16[3,512,1024]{2,1,0:T(8,128)(2,1)}, f32[3,8,1024]{2,1,0:T(8,128...) custom-call(s32[6]{0:T(128)} %stack.64.refs_0_, ...), custom_call_target="tpu_custom_call", output_to_operand_aliasing={{0}: (14, {}), {1}: (15, {}), {2}: (16, {}), {3}: (17, {}),... | custom-call | flops 1350000000 | tf_op jit(solution)/shard_map/feed_back/pallas_call | solution.py:68
  429.6 25.1 %attend_back.7 = (bf16[512,1024]{1,0:T(8,128)(2,1)}, bf16[512,1024]{1,0:T(8,128)(2,1)}, bf16[512,1024]{1,0:T(8,128)(2,1)}, f32[3,8,640,256]{3,2,1,0:T(8,128)}, bf16[2,256,1024]{2,1,0:T(8,128)(2,1)}) custom-call(s32[6]{0:T(128)} %stack.64.refs_0_, s32[1280]{0:T(1024)} %get-tuple-element.297.refs_1_, ...), custom_call_target="tpu_custom_call", output_to_operand_aliasing={{3}: (11, {})} | custom-call | flops 1300000000 | tf_op jit(solution)/shard_map/attend_back/pallas_call | solution.py:68
  454.7 3.0 exchange.15.refs_4_
  457.7 12.0 %enter_back.7 = (bf16[3,512,3072]{2,1,0:T(8,128)(2,1)}, f32[3,8,1024]{2,1,0:T(8,128)}, bf16[512,1024]{1,0:T(8,128)(2,1)}, f32[512,512]{1,0:T(8,128)}) custom-call(s32[6]{0:T(128)} %stack.64.refs_0_, bf16[512,1024]{1,0:T(8,128)(2,1)} %get-tuple-element.253.refs_1_, ...), custom_call_target="tpu_custom_call", output_to_operand_aliasing={{0}: (10, {}), {1}: (11, {})} | custom-call | flops 600000000 | tf_op jit(solution)/shard_map/enter_back/pallas_call | solution.py:68
  470.5 2.1 pad_maximum_fusion
  472.7 2.3 collective-permute-start.13
  475.8 3.7 diagonals.1
  481.3 166.0 %summed_grads.1 = (f32[12,128,512]{2,1,0:T(8,128)}, f32[16,1024]{1,0:T(8,128)}) custom-call(bf16[3,512,4096]{2,1,0:T(8,128)(2,1)} %get-tuple-element.262.f_hbm, bf16[3,512,1024]{2,1,0:T(8,128)(2,1)} %get-tuple-element.263.dy_hbm, bf16[3,512,1024]{2,1,0:T(8,128)(2,1)} %get-tuple-element.188.refs_2_.c_hbm, bf16[3,512,1024]{2,1,0:T(8,128)(2,1)} %get-tuple-element.264.db_hbm, ...), custom_call_target="tpu_custom_call" | custom-call | flops 7500000256 | tf_op jit(solution)/shard_map/summed_grads/pallas_call | solution.py:1514
  659.4 2.9 fusion
  (150 shorter events, 37.1 us)
Async XLA Ops:
  0.6 45.7 %copy-start = (s32[2,1,1024]{2,1,0:T(1,128)S(1)}, s32[2,1,1024]{2,1,0:T(1,128)}, u32[]{:S(2)}) copy-start(s32[2,1,1024]{2,1,0:T(1,128)} %param.14) | copy-start | bytes 24580
  8.5 13.3 %copy-start.2 = (bf16[1024,1536]{1,0:T(8,128)(2,1)}, bf16[1024,1536]{1,0:T(8,128)(2,1)S(1)}, u32[]{:S(2)}) copy-start(bf16[1024,1536]{1,0:T(8,128)(2,1)S(1)} %copy.95.refs_5_.refs_7_) | copy-start | bytes 9437188
  8.5 10.0 %copy-start.24 = (f32[2,512]{1,0:T(2,128)S(1)}, f32[2,512]{1,0:T(2,128)}, u32[]{:S(2)}) copy-start(f32[2,512]{1,0:T(2,128)} %param.22) | copy-start | bytes 12292
  8.5 10.0 %copy-start.23 = (f32[8,32]{1,0:T(8,128)S(1)}, f32[8,32]{1,0:T(8,128)}, u32[]{:S(2)}) copy-start(f32[8,32]{1,0:T(8,128)} %param.24) | copy-start | bytes 3076
  8.5 10.1 %copy-start.22 = (f32[2048]{0:T(1024)S(1)}, f32[2048]{0:T(1024)}, u32[]{:S(2)}) copy-start(f32[2048]{0:T(1024)} %param.23) | copy-start | bytes 24580
  8.6 10.2 %copy-start.19 = (f32[2,2,1024]{2,1,0:T(2,128)S(1)}, f32[2,2,1024]{2,1,0:T(2,128)}, u32[]{:S(2)}) copy-start(f32[2,2,1024]{2,1,0:T(2,128)} %param.20) | copy-start | bytes 49156
  8.6 15.2 %collective-permute-start.2 = (bf16[1024,1536]{1,0:T(8,128)(2,1)S(1)}, bf16[1024,1536]{1,0:T(8,128)(2,1)}, u32[]{:S(2)}, u32[]{:S(2)}) collective-permute-start(bf16[1024,1536]{1,0:T(8,128)(2,1)S(1)} %copy.95.refs_5_.refs_7_), channel_id=1, source_target_pairs={{0,1},{1,0},{2,3},{3,2},{4,5},{5,4},{6,7},{7,6},{8,9},{9,8},{10,11... | collective-permute-start | bytes 9437192 | tf_op jit(solution)/shard_map/ppermute | solution.py:1557
  9.1 61.9 %collective-permute-start.5 = (bf16[1024,2048]{1,0:T(8,128)(2,1)}, bf16[1024,2048]{1,0:T(8,128)(2,1)}, u32[]{:S(2)}, u32[]{:S(2)}) collective-permute-start(bf16[1024,2048]{1,0:T(8,128)(2,1)} %bitcast.103), channel_id=1, source_target_pairs={{0,1},{1,0},{2,3},{3,2},{4,5},{5,4},{6,7},{7,6},{8,9},{9,8},{10,11... | collective-permute-start | bytes 12582920 | tf_op jit(solution)/shard_map/ppermute | solution.py:1557
  9.2 61.8 %collective-permute-start.6 = (bf16[2048,1024]{1,0:T(8,128)(2,1)}, bf16[2048,1024]{1,0:T(8,128)(2,1)}, u32[]{:S(2)}, u32[]{:S(2)}) collective-permute-start(bf16[2048,1024]{1,0:T(8,128)(2,1)} %bitcast.112), channel_id=1, source_target_pairs={{0,1},{1,0},{2,3},{3,2},{4,5},{5,4},{6,7},{7,6},{8,9},{9,8},{10,11... | collective-permute-start | bytes 12582920 | tf_op jit(solution)/shard_map/ppermute | solution.py:1557
  12.7 27.7 %collective-permute-start = (bf16[512,1024]{1,0:T(8,128)(2,1)}, bf16[512,1024]{1,0:T(8,128)(2,1)}, u32[]{:S(2)}, u32[]{:S(2)}) collective-permute-start(bf16[512,1024]{1,0:T(8,128)(2,1)} %get-tuple-element.303.refs_2_), channel_id=1, source_target_pairs={{0,2},{1,3},{4,6},{5,7},{8,10},{9,11},{12,14},{13,15},{16,18},{17,... | collective-permute-start | bytes 3145736 | tf_op jit(solution)/shard_map/ppermute | solution.py:1584
  18.6 4.5 collective-permute-start.1
  24.9 15.5 %copy-start.5 = (bf16[512,1024]{1,0:T(8,128)(2,1)S(1)}, bf16[512,1024]{1,0:T(8,128)(2,1)}, u32[]{:S(2)}) copy-start(bf16[512,1024]{1,0:T(8,128)(2,1)} %get-tuple-element.144.refs_2_) | copy-start | bytes 3145732
  24.9 20.9 %copy-start.3 = (bf16[1,512,1024]{2,1,0:T(8,128)(2,1)S(1)}, bf16[1,512,1024]{2,1,0:T(8,128)(2,1)}, u32[]{:S(2)}) copy-start(bf16[1,512,1024]{2,1,0:T(8,128)(2,1)} %param.17) | copy-start | bytes 3145732
  24.9 21.5 %copy-start.25 = (s32[2047]{0:T(1024)S(1)}, s32[2047]{0:T(1024)}, u32[]{:S(2)}) copy-start(s32[2047]{0:T(1024)} %param.15) | copy-start | bytes 24568
  40.4 30.5 %collective-permute-start.3 = (bf16[512,1024]{1,0:T(8,128)(2,1)S(1)}, bf16[512,1024]{1,0:T(8,128)(2,1)}, u32[]{:S(2)}, u32[]{:S(2)}) collective-permute-start(bf16[512,1024]{1,0:T(8,128)(2,1)S(1)} %copy-done.5), channel_id=1, source_target_pairs={{0,2},{1,3},{4,6},{5,7},{8,10},{9,11},{12,14},{13,15},{16,18},{17,... | collective-permute-start | bytes 3145736 | tf_op jit(solution)/shard_map/ppermute | solution.py:1643
  45.8 25.2 %collective-permute-start.4 = (bf16[512,1024]{1,0:T(8,128)(2,1)S(1)}, bf16[512,1024]{1,0:T(8,128)(2,1)S(1)}, u32[]{:S(2)}, u32[]{:S(2)}) collective-permute-start(bf16[512,1024]{1,0:T(8,128)(2,1)S(1)} %bitcast.129), channel_id=1, source_target_pairs={{0,1},{1,0},{2,3},{3,2},{4,5},{5,4},{6,7},{7,6},{8,9},{9,8},{10,11... | collective-permute-start | bytes 3145736 | tf_op jit(solution)/shard_map/ppermute | solution.py:1557
  46.4 24.5 %copy-start.20 = (s32[768]{0:T(1024)}, s32[768]{0:T(1024)S(1)}, u32[]{:S(2)}) copy-start(s32[768]{0:T(1024)S(1)} %slice.149) | copy-start | bytes 9220
  70.9 1.0 copy-start.4
  96.3 66.5 %collective-permute-start.7 = (bf16[512,1024]{1,0:T(8,128)(2,1)}, bf16[512,1024]{1,0:T(8,128)(2,1)S(1)}, u32[]{:S(2)}, u32[]{:S(2)}) collective-permute-start(bf16[512,1024]{1,0:T(8,128)(2,1)} %get-tuple-element.149), channel_id=1, source_target_pairs={{0,2},{1,3},{4,6},{5,7},{8,10},{9,11},{12,14},{13,15},{16,18},{17,... | collective-permute-start | bytes 3145736 | tf_op jit(solution)/shard_map/ppermute | solution.py:1652
  160.2 25.7 %collective-permute-start.9 = (bf16[512,1024]{1,0:T(8,128)(2,1)}, bf16[512,1024]{1,0:T(8,128)(2,1)S(1)}, u32[]{:S(2)}, u32[]{:S(2)}) collective-permute-start(bf16[512,1024]{1,0:T(8,128)(2,1)} %get-tuple-element.164), channel_id=1, source_target_pairs={{0,2},{1,3},{4,6},{5,7},{8,10},{9,11},{12,14},{13,15},{16,18},{17,... | collective-permute-start | bytes 3145736 | tf_op jit(solution)/shard_map/ppermute | solution.py:1652
  162.8 1.0 copy-start.14
  184.5 42.6 %collective-permute-start.8 = (bf16[512,1024]{1,0:T(8,128)(2,1)}, bf16[512,1024]{1,0:T(8,128)(2,1)S(1)}, u32[]{:S(2)}, u32[]{:S(2)}) collective-permute-start(bf16[512,1024]{1,0:T(8,128)(2,1)} %get-tuple-element.179), channel_id=1, source_target_pairs={{2,0},{3,1},{6,4},{7,5},{10,8},{11,9},{14,12},{15,13},{18,16},{19,... | collective-permute-start | bytes 3145736 | tf_op jit(solution)/shard_map/ppermute | solution.py:1655
  185.9 1.0 copy-start.13
  207.7 59.3 %collective-permute-start.10 = (bf16[512,1024]{1,0:T(8,128)(2,1)}, bf16[512,1024]{1,0:T(8,128)(2,1)S(1)}, u32[]{:S(2)}, u32[]{:S(2)}) collective-permute-start(bf16[512,1024]{1,0:T(8,128)(2,1)} %get-tuple-element.194), channel_id=1, source_target_pairs={{2,0},{3,1},{6,4},{7,5},{10,8},{11,9},{14,12},{15,13},{18,16},{19,... | collective-permute-start | bytes 3145736 | tf_op jit(solution)/shard_map/ppermute | solution.py:1655
  227.1 46.0 %copy-start.10 = (bf16[512,1024]{1,0:T(8,128)(2,1)}, bf16[512,1024]{1,0:T(8,128)(2,1)S(1)}, u32[]{:S(2)}) copy-start(bf16[512,1024]{1,0:T(8,128)(2,1)S(1)} %collective-permute-done.8) | copy-start | bytes 3145732
  267.0 6.1 copy-start.11
  273.1 61.4 %collective-permute-start.11 = (bf16[512,1024]{1,0:T(8,128)(2,1)}, bf16[512,1024]{1,0:T(8,128)(2,1)S(1)}, u32[]{:S(2)}, u32[]{:S(2)}) collective-permute-start(bf16[512,1024]{1,0:T(8,128)(2,1)} %get-tuple-element.210), channel_id=1, source_target_pairs={{2,0},{3,1},{6,4},{7,5},{10,8},{11,9},{14,12},{15,13},{18,16},{19,... | collective-permute-start | bytes 3145736 | tf_op jit(solution)/shard_map/ppermute | solution.py:1683
  293.1 7.5 %copy-start.9 = (bf16[512,1024]{1,0:T(8,128)(2,1)S(1)}, bf16[512,1024]{1,0:T(8,128)(2,1)}, u32[]{:S(2)}) copy-start(bf16[512,1024]{1,0:T(8,128)(2,1)} %get-tuple-element.179) | copy-start | bytes 3145732
  299.4 103.3 %collective-permute-start.12 = (bf16[512,1024]{1,0:T(8,128)(2,1)}, bf16[512,1024]{1,0:T(8,128)(2,1)S(1)}, u32[]{:S(2)}, u32[]{:S(2)}) collective-permute-start(bf16[512,1024]{1,0:T(8,128)(2,1)} %get-tuple-element.227), channel_id=1, source_target_pairs={{2,0},{3,1},{6,4},{7,5},{10,8},{11,9},{14,12},{15,13},{18,16},{19,... | collective-permute-start | bytes 3145736 | tf_op jit(solution)/shard_map/ppermute | solution.py:1683
  334.5 1.0 copy-start.8
  402.7 1.0 copy-start.7
  457.7 12.8 %copy-start.6 = (f32[3,8,1024]{2,1,0:T(8,128)S(1)}, f32[3,8,1024]{2,1,0:T(8,128)}, u32[]{:S(2)}) copy-start(f32[3,8,1024]{2,1,0:T(8,128)} %get-tuple-element.269) | copy-start | bytes 294916
  457.7 12.8 %copy-start.12 = (bf16[512,1024]{1,0:T(8,128)(2,1)S(1)}, bf16[512,1024]{1,0:T(8,128)(2,1)}, u32[]{:S(2)}) copy-start(bf16[512,1024]{1,0:T(8,128)(2,1)} %get-tuple-element.244) | copy-start | bytes 3145732
  469.7 5.3 copy-start.17
  472.7 186.7 %collective-permute-start.13 = (bf16[2,512,512]{2,1,0:T(8,128)(2,1)}, bf16[2,512,512]{2,1,0:T(8,128)(2,1)}, u32[]{:S(2)}, u32[]{:S(2)}) collective-permute-start(bf16[2,512,512]{2,1,0:T(8,128)(2,1)} %pad_maximum_fusion), channel_id=1, source_target_pairs={{0,2},{1,3},{4,6},{5,7},{8,10},{9,11},{12,14},{13,15},{16,18},{17,... | collective-permute-start | bytes 3145736 | tf_op jit(solution)/shard_map/ppermute | solution.py:1691
  475.8 4.6 copy-start.21
  647.3 2.8 copy-start.18
  652.7 6.6 %copy-start.15 = (f32[512,512]{1,0:T(8,128)S(1)}, f32[512,512]{1,0:T(8,128)}, u32[]{:S(2)}) copy-start(f32[512,512]{1,0:T(8,128)} %get-tuple-element.243) | copy-start | bytes 3145732
  653.1 6.3 copy-start.16
  656.7 5.6 copy-start.1

commit v3 on v2

--- a/solution.py
+++ b/solution.py
@@ -34,6 +34,10 @@
 
 def cost_of(micros):
     return pl.CostEstimate(flops=int(micros * 5e7), bytes_accessed=0, transcendentals=0)
+
+
+def when(condition):
+    return (lambda body: body()) if condition else (lambda body: None)
 
 
 def slotted(shape, dtype):
@@ -209,17 +213,18 @@
         target[pl.ds(pl.multiple_of(info[3] * QB, QB), halo_count), :] = halo[...]
 
 
-def attend_kernel(halo_count, info, seg_ref, *refs):
+def attend_kernel(halo_count, with_bias, info, seg_ref, *refs):
+    refs = list(refs)
+    segq_ref, q_ref, k_ref, v_ref = refs[:4]
+    t_ref = refs.pop(4) if with_bias else None
+    kh_ref = vh_ref = None
     if halo_count:
-        segq_ref, q_ref, k_ref, v_ref, t_ref, kh_ref, vh_ref, o_ref, lse_ref, kk_ref, vk_ref = refs[:11]
-        segk_ref, kp_ref, vp_ref, vt_ref, mask_ref, score_ref, prob_ref, stat_ref = refs[11:]
-        kh_ref, vh_ref = kh_ref.at[0], vh_ref.at[0]
-        kk_ref[0] = kh_ref[...]
-        vk_ref[0] = vh_ref[...]
-    else:
-        segq_ref, q_ref, k_ref, v_ref, t_ref, o_ref, lse_ref = refs[:7]
-        segk_ref, kp_ref, vp_ref, vt_ref, mask_ref, score_ref, prob_ref, stat_ref = refs[7:]
-        kh_ref = vh_ref = None
+        kh_ref, vh_ref = refs.pop(4).at[0], refs.pop(4).at[0]
+    o_ref, lse_ref = refs[4:6]
+    if halo_count:
+        refs.pop(6)[0] = kh_ref[...]
+        refs.pop(6)[0] = vh_ref[...]
+    segk_ref, kp_ref, vp_ref, vt_ref, mask_ref, score_ref, prob_ref = refs[6:]
     rows = q_ref.shape[1]
     pairs = q_ref.shape[2] // (2 * DH)
     first = lax.broadcasted_iota(jnp.int32, (QB, 2 * DH), 1) < DH
@@ -242,7 +247,8 @@
         for pair in range(pairs):
             lanes = slice(pair * 2 * DH, (pair + 1) * 2 * DH)
             both = two_heads(q_ref[0, mine, lanes] * LOW(0.125), first)
-            score_ref[pair, :span, :] = dot_nt(kp_ref[keys, lanes], both) + t_ref[pair, shifted, :]
+            scores = dot_nt(kp_ref[keys, lanes], both)
+            score_ref[pair, :span, :] = scores + t_ref[pair, shifted, :] if with_bias else scores
         for pair in range(pairs):
             lanes = slice(pair * 2 * DH, (pair + 1) * 2 * DH)
             stats = []
@@ -260,19 +266,20 @@
                 for strip in range(0, span, STRIP):
                     piece = slice(strip, strip + STRIP)
                     weights = jnp.exp(score_ref[pair, piece, side] - highest)
-                    prob_ref[pair, piece, side] = weights.astype(LOW)
+                    score_ref[pair, piece, side] = weights
                     mass = jnp.sum(weights.reshape(STRIP // 8, 8, QB), axis=0)
                     total = mass if total is None else total + mass
                 totals = jnp.sum(total, axis=0, keepdims=True)
-                stat_ref[2 * pair + head : 2 * pair + head + 1, :] = 1.0 / totals
+                inverse = 1.0 / totals
+                for strip in range(0, span, STRIP):
+                    piece = slice(strip, strip + STRIP)
+                    prob_ref[pair, piece, side] = (score_ref[pair, piece, side] * inverse).astype(LOW)
                 stats.append(highest + jnp.log(totals))
             lse_ref[0, pair, pl.ds(i, 1), :] = jnp.concatenate(stats, axis=1)
         for pair in range(pairs):
             lanes = slice(pair * 2 * DH, (pair + 1) * 2 * DH)
             turned = dot_nn(vt_ref[lanes, keys], prob_ref[pair, :span, :])
-            upper = turned[:DH, :QB] * stat_ref[2 * pair : 2 * pair + 1, :]
-            lower = turned[DH:, QB:] * stat_ref[2 * pair + 1 : 2 * pair + 2, :]
-            o_ref[0, mine, lanes] = jnp.concatenate([upper, lower], axis=0).T.astype(LOW)
+            o_ref[0, mine, lanes] = joined_heads(turned).astype(LOW)
 
     visit_blocks(seg_ref, info[2], rows // QB, block)
 
@@ -299,9 +306,11 @@
         column(0),
         column(1),
         column(2),
-        pl.BlockSpec((pairs,) + bias.shape[1:], lambda g, s, t: (g, 0, 0)),
     ]
-    inputs = [segments.reshape(blocks, QB), qkv, qkv, qkv, bias]
+    inputs = [segments.reshape(blocks, QB), qkv, qkv, qkv]
+    if bias is not None:
+        in_specs.append(pl.BlockSpec((pairs,) + bias.shape[1:], lambda g, s, t: (g, 0, 0)))
+        inputs.append(bias)
     outputs = [slotted((rows, width), LOW), slotted((groups * pairs, count, 2 * QB), F32)]
     out_specs = [column(0), slot_pairs]
     if halo_count:
@@ -311,7 +320,7 @@
         kept = pl.BlockSpec((1, halo_count, span), lambda g, s, t: (s[1], 0, g))
         out_specs += [kept, kept]
     return call_with_slots(
-        functools.partial(attend_kernel, halo_count),
+        functools.partial(attend_kernel, halo_count, bias is not None),
         [info, segments],
         inputs,
         in_specs,
@@ -327,24 +336,26 @@
             pltpu.VMEM((5 * QB, QB), F32),
             pltpu.VMEM((pairs, 5 * QB, 2 * QB), F32),
             pltpu.VMEM((pairs, 5 * QB, 2 * QB), LOW),
-            pltpu.VMEM((8, QB), F32),
         ],
         "attend",
         24,
     )
 
 
-def attend_back_kernel(halo_count, info, seg_ref, *refs):
+def attend_back_kernel(halo_count, with_bias, info, seg_ref, *refs):
+    refs = list(refs)
+    segq_ref, q_ref, k_ref, v_ref, g_ref, lse_ref = refs[:6]
+    t_ref = refs.pop(6) if with_bias else None
+    kh_ref = vh_ref = dh_ref = diag_ref = None
     if halo_count:
-        segq_ref, q_ref, k_ref, v_ref, g_ref, t_ref, lse_ref, kh_ref, vh_ref = refs[:9]
-        dq_ref, dk_ref, dv_ref, diag_ref, dh_ref = refs[9:14]
-        segk_ref, kp_ref, vp_ref, kt_ref, dk_acc, dv_acc = refs[14:]
-        kh_ref, vh_ref = kh_ref.at[0], vh_ref.at[0]
-    else:
-        segq_ref, q_ref, k_ref, v_ref, g_ref, t_ref, lse_ref = refs[:7]
-        dq_ref, dk_ref, dv_ref, diag_ref = refs[7:11]
-        segk_ref, kp_ref, vp_ref, kt_ref, dk_acc, dv_acc = refs[11:]
-        kh_ref = vh_ref = None
+        kh_ref, vh_ref = refs.pop(6).at[0], refs.pop(6).at[0]
+    dq_ref, dk_ref, dv_ref = refs[6:9]
+    if with_bias:
+        diag_ref = refs.pop(9)
+        diag_ref[...] = jnp.zeros_like(diag_ref)
+    if halo_count:
+        dh_ref = refs.pop(9)
+    segk_ref, kp_ref, vp_ref, kt_ref, dk_acc, dv_acc = refs[9:]
     rows = q_ref.shape[1]
     pairs = q_ref.shape[2] // (2 * DH)
     first = lax.broadcasted_iota(jnp.int32, (QB, 2 * DH), 1) < DH
@@ -358,7 +369,6 @@
     kt_ref[...] = kp_ref[...].T
     dk_acc[...] = jnp.zeros_like(dk_acc)
     dv_acc[...] = jnp.zeros_like(dv_acc)
-    diag_ref[...] = jnp.zeros_like(diag_ref)
 
     def block(i, at, reach):
         span = (2 * reach + 1) * QB
@@ -371,7 +381,9 @@
             lanes = slice(pair * 2 * DH, (pair + 1) * 2 * DH)
             both = two_heads(q_ref[0, mine, lanes] * LOW(0.125), first)
             grads = two_heads(g_ref[mine, lanes], first)
-            scores = dot_nt(kp_ref[keys, lanes], both) + t_ref[pair, shifted, :]
+            scores = dot_nt(kp_ref[keys, lanes], both)
+            if with_bias:
+                scores = scores + t_ref[pair, shifted, :]
             scores = jnp.where(allowed, scores - lse_ref[0, pair, pl.ds(i, 1), :], -jnp.inf)
             probs = jnp.exp(scores)
             grad_probs = dot_nt(vp_ref[keys, lanes], grads)
@@ -379,7 +391,8 @@
             inner = jnp.sum(probs * grad_probs, axis=0, keepdims=True)
             rounded = (probs * (grad_probs - inner)).astype(LOW)
             dk_acc[keys, lanes] += dot_nn(rounded, both)
-            diag_ref[0, pair, shifted, :] += rounded.astype(F32)
+            if with_bias:
+                diag_ref[0, pair, shifted, :] += rounded.astype(F32)
             turned = dot_nn(kt_ref[lanes, keys], rounded)
             dq_ref[mine, lanes] = (joined_heads(turned) * 0.125).astype(LOW)
 
@@ -410,15 +423,18 @@
         column(1),
         column(2),
         plain,
-        pl.BlockSpec((pairs,) + bias.shape[1:], lambda g, s, t: (g, 0, 0)),
         pl.BlockSpec((1, pairs, count, 2 * QB), lambda g, s, t: (s[1], g, 0, 0)),
     ]
-    inputs = [segments.reshape(blocks, QB), qkv, qkv, qkv, grad_context, bias, lse]
+    inputs = [segments.reshape(blocks, QB), qkv, qkv, qkv, grad_context, lse]
+    if bias is not None:
+        in_specs.append(pl.BlockSpec((pairs,) + bias.shape[1:], lambda g, s, t: (g, 0, 0)))
+        inputs.append(bias)
     plain_shape = jax.ShapeDtypeStruct((rows, width), LOW)
-    outputs = [plain_shape] * 3 + [slotted(bias.shape, F32)]
-    out_specs = [plain] * 3 + [
-        pl.BlockSpec((1, pairs) + bias.shape[1:], lambda g, s, t: (s[1], g, 0, 0))
-    ]
+    outputs = [plain_shape] * 3
+    out_specs = [plain] * 3
+    if bias is not None:
+        outputs.append(slotted(bias.shape, F32))
+        out_specs.append(pl.BlockSpec((1, pairs) + bias.shape[1:], lambda g, s, t: (s[1], g, 0, 0)))
     if halo_count:
         kept = pl.BlockSpec((1, halo_count, span), lambda g, s, t: (s[1], 0, g))
         in_specs += [kept, kept]
@@ -427,7 +443,7 @@
         out_specs.append(pl.BlockSpec((2, halo_count, span), lambda g, s, t: (0, 0, lax.rem(g + groups // 2, groups))))
     keep = None if previous is None else [None] * 3 + [previous] + [None] * (len(outputs) - 4)
     return call_with_slots(
-        functools.partial(attend_back_kernel, halo_count),
+        functools.partial(attend_back_kernel, halo_count, bias is not None),
         [info, segments],
         inputs,
         in_specs,
@@ -492,20 +508,18 @@
     return u * below, below + u * (bell * 0.3989422804014327)
 
 
-def enter_kernel(info, first_ref, second_ref, gain_ref, shift_ref, own_ref, oth_ref, x_ref, e_ref, qkv_ref, halo_ref):
+def enter_kernel(lead, info, given_ref, gain_ref, shift_ref, own_ref, oth_ref, x_ref, e_ref, qkv_ref, halo_ref):
     m = pl.program_id(0)
     half = own_ref.shape[1]
 
-    @pl.when((m == 0) & (info[0] == 1))
-    def _():
-        x_ref[0] = first_ref[...]
-        e_ref[0] = first_ref[...]
-
-    @pl.when((m == 0) & (info[0] == 0))
-    def _():
-        x_ref[0] = second_ref[...]
-        x = second_ref[...].astype(F32)
-        e_ref[0] = (x * rms_scale(x) * gain_ref[...]).astype(LOW)
+    @pl.when(m == 0)
+    def _():
+        x_ref[0] = given_ref[0]
+        if lead:
+            e_ref[0] = given_ref[0]
+        else:
+            x = given_ref[0].astype(F32)
+            e_ref[0] = (x * rms_scale(x) * gain_ref[...]).astype(LOW)
 
     e = e_ref[0]
     for part, weight in enumerate((own_ref, oth_ref)):
@@ -517,19 +531,18 @@
     halo_ref[0, :, half:] = qkv_ref[0, start, :half]
 
 
-def enter(info, first, second, gain, shift, own, oth, previous):
-    rows, width = first.shape
+def enter(lead, info, given, at, gain, shift, own, oth, previous):
+    _, rows, width = given.shape
     half = own.shape[1] // 3
-    whole = pl.BlockSpec((rows, width), lambda m, s: (0, 0))
+    whole = pl.BlockSpec((1, rows, width), lambda m, s: (at, 0, 0))
     weight = pl.BlockSpec((width, half), lambda m, s: (0, m))
     kept = pl.BlockSpec((1, rows, width), lambda m, s: (s[1], 0, 0))
     keep = None if previous is None else list(previous) + [None]
     return call_with_slots(
-        enter_kernel,
+        functools.partial(enter_kernel, lead),
         [info],
-        [first, second, gain, shift, own, oth],
+        [given, gain, shift, own, oth],
         [
-            whole,
             whole,
             pl.BlockSpec((1, width), lambda m, s: (0, 0)),
             pl.BlockSpec((1, 2 * half), lambda m, s: (0, m)),
@@ -557,7 +570,7 @@
 
 
 def feed_kernel(
-    info, x_ref, c_ref, wo_own, wo_oth, up_own, up_oth, down_own, down_oth, bias_ref, gain_ref, shift_ref,
+    lead, info, x_ref, c_ref, wo_own, wo_oth, up_own, up_oth, down_own, down_oth, bias_ref, gain_ref, shift_ref,
     f_ref, slope_ref, n_ref, one_ref, two_ref, out_ref, acc_ref, carry_ref, hidden_ref
 ):
     j = pl.program_id(0)
@@ -573,7 +586,7 @@
             + x_ref[0].astype(F32)
         )
 
-        @pl.when(info[0] == 1)
+        @when(lead)
         def _():
             before = joined + shift_ref[0:1, :]
             one_ref[0] = before.astype(LOW)
@@ -582,7 +595,7 @@
             carry_ref[...] = normed
             n_ref[0] = normed.astype(LOW)
 
-        @pl.when(info[0] == 0)
+        @when(not lead)
         def _():
             one_ref[0] = joined.astype(LOW)
             carry_ref[...] = joined
@@ -631,7 +644,7 @@
     def _():
         joined = carry_ref[...] + acc_ref[...]
 
-        @pl.when(info[0] == 1)
+        @when(lead)
         def _():
             before = joined + shift_ref[1:2, :]
             two_ref[0] = before.astype(LOW)
@@ -639,7 +652,7 @@
             normed = center * lax.rsqrt(mean_of(center * center) + 1e-05) * gain_ref[1:2, :] + shift_ref[3:4, :]
             out_ref[...] = normed.astype(LOW)
 
-        @pl.when(info[0] == 0)
+        @when(not lead)
         def _():
             two_ref[0] = joined.astype(LOW)
             out_ref[...] = joined.astype(LOW)
@@ -652,7 +665,7 @@
     return 2 * each, near, far
 
 
-def feed(info, x, context, wo, up, down, bias, gains, shifts, previous):
+def feed(lead, info, x, context, wo, up, down, bias, gains, shifts, previous):
     _, rows, width = x.shape
     hidden = up[0].shape[1]
     chunk = min(FEED_CHUNK, hidden)
@@ -667,7 +680,7 @@
     moving = pl.BlockSpec((1, rows, chunk), lambda j, s: (s[1], 0, rise(j)))
     keep = None if previous is None else list(previous) + [None]
     return call_with_slots(
-        feed_kernel,
+        functools.partial(feed_kernel, lead),
         [info],
         [x, context, wo[0], wo[1], up[0], up[1], down[0], down[1], bias, gains, shifts],
         [
@@ -722,22 +735,30 @@
 
 
 def feed_back_kernel(
-    info, got_ref, mine_ref, other_ref, one_ref, two_ref, slope_ref, wo_own, wo_oth, up_own, up_oth, down_own, down_oth,
+    lead, info, *refs
+):
+    refs = list(refs)
+    got_refs = [refs.pop(0) for _ in range(2 - lead)]
+    feed_back_steps(lead, got_refs, *refs)
+
+
+def feed_back_steps(
+    lead, got_refs, one_ref, two_ref, slope_ref, wo_own, wo_oth, up_own, up_oth, down_own, down_oth,
     gain_ref, dy_ref, du_ref, db_ref, stat_ref, bias_ref, dz_ref, dc_ref, acc_ref, carry_ref
 ):
     j = pl.program_id(0)
     steps = pl.num_programs(0)
     half = wo_own.shape[0]
-    rows = got_ref.shape[0]
+    rows = dy_ref.shape[1]
 
     @pl.when(j == 0)
     def _():
         stat_ref[...] = jnp.zeros_like(stat_ref)
         acc_ref[...] = jnp.zeros_like(acc_ref)
 
-        @pl.when(info[0] == 1)
+        @when(lead)
         def _():
-            grad = got_ref[...].astype(F32)
+            grad = got_refs[0][0].astype(F32)
             back, gain = layer_norm_back(two_ref[0].astype(F32), grad, gain_ref[1:2, :])
             stat_ref[0, 1:2, :] = gain
             stat_ref[0, 5:6, :] = sum_rows(grad)
@@ -745,9 +766,9 @@
             carry_ref[...] = back
             dy_ref[0] = back.astype(LOW)
 
-        @pl.when(info[0] == 0)
+        @when(not lead)
         def _():
-            grad = mine_ref[...].astype(F32) + other_ref[...].astype(F32)
+            grad = got_refs[0][0].astype(F32) + got_refs[1][0].astype(F32)
             carry_ref[...] = grad
             dy_ref[0] = grad.astype(LOW)
 
@@ -767,7 +788,7 @@
 
     @pl.when(j == steps - 1)
     def _():
-        @pl.when(info[0] == 1)
+        @when(lead)
         def _():
             grad = acc_ref[...] + carry_ref[...]
             back, gain = layer_norm_back(one_ref[0].astype(F32), grad, gain_ref[0:1, :])
@@ -776,7 +797,7 @@
             stat_ref[0, 2:3, :] = sum_rows(back)
             dz_ref[...] = back
 
-        @pl.when(info[0] == 0)
+        @when(not lead)
         def _():
             back, gain = rms_norm_back(one_ref[0].astype(F32), acc_ref[...], gain_ref[1:2, :])
             stat_ref[0, 1:2, :] = gain
@@ -788,7 +809,7 @@
         dc_ref[:, half:] = dot_nt(low, wo_oth[...]).astype(LOW)
 
 
-def feed_back(info, got, mine, other, one, two, slope, wo, up, down, gains, previous):
+def feed_back(lead, info, got, at, one, two, slope, wo, up, down, gains, previous):
     _, rows, width = one.shape
     hidden = up[0].shape[1]
     chunk = min(FEED_CHUNK, hidden)
@@ -799,13 +820,11 @@
     moving = pl.BlockSpec((1, rows, chunk), lambda j, s: (s[1], 0, j))
     keep = None if previous is None else list(previous) + [None, None]
     return call_with_slots(
-        feed_back_kernel,
+        functools.partial(feed_back_kernel, lead),
         [info],
-        [got, mine, other, one, two, slope, wo[0], wo[1], up[0], up[1], down[0], down[1], gains],
-        [
-            plain,
-            plain,
-            plain,
+        [*got, one, two, slope, wo[0], wo[1], up[0], up[1], down[0], down[1], gains],
+        [pl.BlockSpec((1, rows, width), lambda j, s: (at, 0, 0))] * len(got)
+        + [
             kept,
             kept,
             moving,
@@ -844,8 +863,8 @@
 
 
 def enter_back_kernel(
-    info, dq_ref, dk_ref, dv_ref, far_ref, x_ref, dz_ref, own_ref, oth_ref, gain_ref,
-    d_ref, stat_ref, low_ref, lower_ref, acc_ref
+    lead, info, dq_ref, dk_ref, dv_ref, far_ref, x_ref, dz_ref, own_ref, oth_ref, gain_ref,
+    d_ref, stat_ref, lower_ref, upper_ref, low_ref, acc_ref
 ):
     m = pl.program_id(0)
     half = own_ref.shape[1]
@@ -875,32 +894,34 @@
 
     @pl.when(m == 2)
     def _():
-        split = lower_ref.shape[1]
-
-        @pl.when(info[0] == 1)
+        split = lower_ref.shape[2]
+
+        @when(lead)
         def _():
             total = dz_ref[...] + acc_ref[...]
             low_ref[...] = total.astype(LOW)
-            lower_ref[...] = total[:, :split]
-
-        @pl.when(info[0] == 0)
+            lower_ref[0] = total[:, :split]
+            upper_ref[0] = total[:, split:].astype(LOW)
+
+        @when(not lead)
         def _():
             back, gain = rms_norm_back(x_ref[0].astype(F32), acc_ref[...], gain_ref[...])
             stat_ref[0, 2:3, :] = gain
             total = dz_ref[...] + back
             low_ref[...] = total.astype(LOW)
-            lower_ref[...] = total[:, :split]
-
-
-def enter_back(info, dq, dk, dv, far, x, dz, own, oth, gain, previous):
+            lower_ref[0] = total[:, :split]
+            upper_ref[0] = total[:, split:].astype(LOW)
+
+
+def enter_back(lead, info, dq, dk, dv, far, x, dz, own, oth, gain, previous):
     _, rows, width = x.shape
     half = own.shape[1] // 3
     plain = pl.BlockSpec((rows, width), lambda m, s: (0, 0))
     kept = pl.BlockSpec((1, rows, width), lambda m, s: (s[1], 0, 0))
     weight = pl.BlockSpec((width, half), lambda m, s: (0, m))
-    keep = None if previous is None else list(previous) + [None, None]
+    keep = None if previous is None else list(previous) + [None]
     return call_with_slots(
-        enter_back_kernel,
+        functools.partial(enter_back_kernel, lead),
         [info],
         [dq, dk, dv, far, x, dz, own, oth, gain],
         [
@@ -917,14 +938,16 @@
         [
             slotted((rows, 6 * half), LOW),
             slotted((8, width), F32),
+            slotted((rows, width // 2), F32),
+            slotted((rows, width // 2), LOW),
             jax.ShapeDtypeStruct((rows, width), LOW),
-            jax.ShapeDtypeStruct((rows, width // 2), F32),
         ],
         [
             pl.BlockSpec((1, rows, 2 * half), lambda m, s: (s[1], 0, m)),
             pl.BlockSpec((1, 8, width), lambda m, s: (s[1], 0, 0)),
+            pl.BlockSpec((1, rows, width // 2), lambda m, s: (s[1], 0, 0)),
+            pl.BlockSpec((1, rows, width // 2), lambda m, s: (s[1], 0, 0)),
             plain,
-            pl.BlockSpec((rows, width // 2), lambda m, s: (0, 0)),
         ],
         keep,
         (3,),
@@ -1285,11 +1308,11 @@
 
 
 def grads_kernel(
-    f_hbm, dy_hbm, c_hbm, db_hbm, n_hbm, du_hbm, e_hbm, dqkv_hbm, packed_ref,
-    out_ref, summed_ref,
+    f_hbm, dy_hbm, c_hbm, db_hbm, n_hbm, du_hbm, e_hbm, dqkv_hbm, upper_hbm, packed_ref,
+    down_ref, up_ref, row_ref, qkv_ref, summed_ref, upper_got,
     still, moving, turned, given, held, near_ref, y_ref, low_ref, high_ref, small_ref, small_got,
     still_sem, moving_sem, near_send, near_recv, y_send, y_recv, low_send, low_recv, high_send, high_recv,
-    small_send, small_recv
+    small_send, small_recv, upper_send, upper_recv
 ):
     dp = lax.axis_index("dp")
     core = lax.axis_index("tensor")
@@ -1307,7 +1330,9 @@
     high_peer = across(4, high_side)
     peers = [core_peer, y_peer, low_peer, high_peer, {"section": 1 - section}]
     mesh_id = pl.DeviceIdType.MESH
-    total = out_ref.shape[0]
+    total = held.shape[0]
+    chunk = moving.shape[4]
+    each = du_hbm.shape[2] // 2 // chunk
 
     barrier = pltpu.get_barrier_semaphore()
     for peer in peers:
@@ -1361,7 +1386,19 @@
 
     def high_stage(k):
         high_copy(k).wait_recv()
-        out_ref[k] = high_ref[k].astype(F32) + low_ref[k, high_side].astype(F32)
+        value = high_ref[k].astype(F32) + low_ref[k, high_side].astype(F32)
+
+        def cut(ref, first):
+            for q in range(chunk // QB):
+                ref[pl.ds(first + q * QB, QB), :] = value[:, q * QB : (q + 1) * QB]
+
+        def lay(ref, at):
+            ref[:, pl.ds(pl.multiple_of(at * chunk, chunk), chunk)] = value
+
+        pl.when(k < each)(lambda: cut(down_ref, pl.multiple_of(k * chunk, chunk)))
+        pl.when((k >= each) & (k < 2 * each))(lambda: lay(up_ref, k - each))
+        pl.when(k == 2 * each)(lambda: cut(row_ref, 0))
+        pl.when(k > 2 * each)(lambda: lay(qkv_ref, k - 2 * each - 1))
 
     def small_stage(s):
         small_copy(s).wait_recv()
@@ -1369,8 +1406,6 @@
         if s + 1 < len(peers):
             small_copy(s + 1).start()
 
-    chunk = moving.shape[4]
-    each = du_hbm.shape[2] // 2 // chunk
     phases = [
         (False, dy_hbm, f_hbm, each, lambda c: c * chunk, lambda c: (each + c) * chunk),
         (True, n_hbm, du_hbm, each, lambda c: c * chunk, lambda c: (each + c) * chunk),
@@ -1396,6 +1431,8 @@
     for copy in moving_copies(0, 0, 0):
         copy.start()
     still_copy(1).start()
+    upper_copy = send(upper_hbm.at[0:2], upper_got, upper_send, upper_recv, peers[4])
+    upper_copy.start()
     small_ref[0] = packed_ref[...]
     small_copy(0).start()
 
@@ -1478,9 +1515,12 @@
 
     near_stage(total - 1)
     early = (total - 1 - 5) // 3 + 1
-    for k in range(early):
+    @pl.loop(0, early)
+    def _(k):
         low_stage(k)
-    for k in range(early - 1):
+
+    @pl.loop(0, early - 1)
+    def _(k):
         high_stage(k)
 
     @pl.loop(early, total)
@@ -1489,7 +1529,10 @@
         high_stage(k - 1)
         low_stage(k)
 
-    high_stage(total - 1)
+    @pl.loop(total - 1, total)
+    def _(k):
+        high_stage(k)
+
     summed_ref[...] = small_ref[len(peers)]
     near_copy(total - 2, (total - 2) % 2).wait_send()
     near_copy(total - 1, (total - 1) % 2).wait_send()
@@ -1502,9 +1545,10 @@
 
     for s in range(len(peers)):
         small_copy(s).wait_send()
-
-
-def summed_grads(f, dy, context, db, n, du, e, dqkv, packed):
+    upper_copy.wait()
+
+
+def summed_grads(f, dy, context, db, n, du, e, dqkv, upper, packed):
     rows, width = dy.shape[1:]
     chunk = 512
     total = du.shape[2] // chunk + 4
@@ -1513,11 +1557,15 @@
     local = pl.BlockSpec(memory_space=pltpu.VMEM)
     return pl.pallas_call(
         grads_kernel,
-        in_specs=[anywhere] * 8 + [local],
-        out_specs=[local, local],
+        in_specs=[anywhere] * 9 + [local],
+        out_specs=[local] * 5 + [anywhere],
         out_shape=[
-            jax.ShapeDtypeStruct((total, QB, chunk), F32),
+            jax.ShapeDtypeStruct((du.shape[2] // 2, QB), F32),
+            jax.ShapeDtypeStruct((QB, du.shape[2] // 2), F32),
+            jax.ShapeDtypeStruct((width // 2, QB), F32),
+            jax.ShapeDtypeStruct((QB, dqkv.shape[2] // 2), F32),
             jax.ShapeDtypeStruct(packed.shape, F32),
+            jax.ShapeDtypeStruct((2,) + upper.shape[1:], LOW),
         ],
         scratch_shapes=[
             pltpu.VMEM((2, 2, rows, width), LOW),
@@ -1543,13 +1591,15 @@
             dma((total,)),
             dma((5,)),
             dma((5,)),
+            dma,
+            dma,
         ],
         compiler_params=pltpu.CompilerParams(
             collective_id=0, has_side_effects=True, vmem_limit_bytes=TAIL_VMEM
         ),
-        cost_estimate=cost_of(150),
+        cost_estimate=cost_of(5000),
         name="summed_grads",
-    )(f, dy, context, db, n, du, e, dqkv, packed)
+    )(f, dy, context, db, n, du, e, dqkv, upper, packed)
 
 
 def swapped(value, axis, bit):
@@ -1581,8 +1631,10 @@
     lead = jnp.where(leading, 1, 0).astype(jnp.int32)
     pieces = lax.axis_size("dp")
 
-    remote_grads = [lax.ppermute(decoder_grads[0, 0, 0], "section", [(0, 1)])]
-    qkv_own = attn_in[0].reshape(width, -1)
+    own_grads = decoder_grads[0, :, 0]
+    remote_grads = lax.ppermute(own_grads, "section", [(0, 1)])
+    given_rows = layer_input[:, 0]
+    qkv_own = jnp.concatenate([attn_in[0, :, part] for part in range(3)], axis=1)
     qkv_oth = swapped(qkv_own, "tensor", 1)
     wo = (attn_out[0], swapped(attn_out[0], "tensor", 1))
     up = (ffn_in[0], swapped(ffn_in[0], "tensor", 1))
@@ -1626,7 +1678,7 @@
         return jnp.stack([lead, slot, own_block, halo_block, edge, active]).astype(jnp.int32)
 
     turns = [(turn, micro) for turn in range(2) for micro in range(micro_count)]
-    received = [jnp.zeros((rows, width), LOW)] * micro_count
+    received = [None] * micro_count
     entered = attended = fed = None
     results = []
     finished = []
@@ -1634,18 +1686,19 @@
         info = info_of(turn, micro)
         if turn + micro > 0:
             info, _ = lax.optimization_barrier((info, result))
+        if turn == 1 and micro == 0:
+            info, remote_grads = lax.optimization_barrier((info, remote_grads))
+        lead_turn = turn == 0
+        given, at = (given_rows, micro) if lead_turn else (received[micro][None], 0)
         *entered, halo = enter(
-            info, layer_input[micro, 0], received[micro], entry_gain, qkv_shift, qkv_own, qkv_oth, entered
+            lead_turn, info, given, at, entry_gain, qkv_shift, qkv_own, qkv_oth, entered
         )
         halo = exchanged(halo)
-        if turn == 0 and micro == 0:
-            later, _ = lax.optimization_barrier((decoder_grads[0, 1, 0], (remote_grads[0], halo)))
-            remote_grads.append(lax.ppermute(later, "section", [(0, 1)]))
-        attended = attend(info, segments[micro], entered[2], halo, bias, attended)
-        if turn == 0 and micro == 0:
-            info, remote_grads[1] = lax.optimization_barrier((info, remote_grads[1]))
+        attended = attend(
+            info, segments[micro], entered[2], halo, None if lead_turn else bias, attended
+        )
         *fed, result = feed(
-            info, entered[0], attended[0], wo, up, down, ffn_both, gains, bert_shift, fed
+            lead_turn, info, entered[0], attended[0], wo, up, down, ffn_both, gains, bert_shift, fed
         )
         if turn == 0:
             received = list(received)
@@ -1657,39 +1710,34 @@
     context, lse, *halo_saved = attended
     f_saved, slope_saved, n_saved, one_saved, two_saved = fed
 
-    received = [jnp.zeros((rows, width), LOW)] * micro_count
+    received = [None] * micro_count
     feed_kept = table_kept = entry_kept = None
-    input_low = []
-    input_lower = []
     for step, (turn, micro) in enumerate([(1 - turn, micro) for turn, micro in turns]):
         info = info_of(turn, micro)
         if step > 0:
-            info, _ = lax.optimization_barrier((info, low))
+            info, _ = lax.optimization_barrier((info, low if step < 3 else entry_kept[1]))
+        lead_turn = turn == 0
+        got, at = ([received[micro][None]], 0) if lead_turn else ([own_grads, remote_grads], micro)
         *feed_kept, dz, grad_context = feed_back(
-            info, received[micro], decoder_grads[0, micro, 0], remote_grads[micro], one_saved, two_saved,
-            slope_saved, wo, up, down, gains, feed_kept,
-        )
-        dq, dk, dv, table_kept, far = attend_back(
-            info, segments[micro], qkv_saved, halo_saved, grad_context, bias, lse, table_kept
-        )
+            lead_turn, info, got, at, one_saved, two_saved, slope_saved, wo, up, down, gains, feed_kept
+        )
+        dq, dk, dv, *tables, far = attend_back(
+            info, segments[micro], qkv_saved, halo_saved, grad_context, None if lead_turn else bias, lse,
+            None if lead_turn else table_kept,
+        )
+        if not lead_turn:
+            table_kept = tables[0]
         far = exchanged(far)
         if turn == 1 and micro == 0:
             info, *finished = lax.optimization_barrier((info, *finished))
-        *entry_kept, low, lower = enter_back(
-            info, dq, dk, dv, far, x_saved, dz, qkv_own, qkv_oth, entry_gain, entry_kept
+        *entry_kept, low = enter_back(
+            lead_turn, info, dq, dk, dv, far, x_saved, dz, qkv_own, qkv_oth, entry_gain, entry_kept
         )
         if turn == 1:
             received = list(received)
             received[micro] = lax.ppermute(low, "section", [(1, 0)])
-        else:
-            input_low.append(low)
-            input_lower.append(lower)
     dy_saved, du_saved, db_saved, stat_feed, stat_bias = feed_kept
-    dqkv_saved, stat_entry = entry_kept
-
-    half = width // 2
-    upper = lax.ppermute(jnp.stack(input_low)[:, :, half:], "section", [(0, 1)]).astype(F32)
-    input_grad = jnp.where(leading, jnp.stack(input_lower), upper)[:, None]
+    dqkv_saved, stat_entry, lower_kept, upper_kept = entry_kept
 
     near_table = jnp.dot(diagonals(trailing, table_kept, micro_count), near_hits.T, precision=lax.Precision.HIGHEST)
 
@@ -1711,16 +1759,11 @@
     packed = jnp.concatenate([part.reshape(-1) for part in parts])
     packed_rows = 8 * (-(-packed.size // (8 * width)))
     packed = jnp.pad(packed, (0, packed_rows * width - packed.size)).reshape(packed_rows, width)
-    summed, packed = summed_grads(
-        f_saved, dy_saved, context, db_saved, n_saved, du_saved, e_saved, dqkv_saved, packed
+    down_sum, up_sum, out_sum, qkv_sum, packed, upper = summed_grads(
+        f_saved, dy_saved, context, db_saved, n_saved, du_saved, e_saved, dqkv_saved, upper_kept, packed
     )
     packed = packed.reshape(-1)
-    quarters = ffn_in.shape[2] // summed.shape[2]
-    piece = width // pieces
-    down_sum = summed[:quarters].reshape(quarters, QB, -1, QB).transpose(0, 2, 1, 3).reshape(-1, piece)
-    up_sum = summed[quarters : 2 * quarters].transpose(1, 0, 2).reshape(piece, -1)
-    out_sum = summed[2 * quarters].reshape(QB, -1, QB).transpose(1, 0, 2).reshape(-1, piece)
-    qkv_sum = summed[2 * quarters + 1 :].transpose(1, 0, 2)
+    input_grad = jnp.where(leading, lower_kept[:micro_count], upper.astype(F32))[:, None]
     unpacked = []
     start = 0
     for part in parts:
@@ -1731,7 +1774,7 @@
     return (
         jnp.where(leading, jnp.stack(finished), jnp.stack(results))[None, :, None],
         input_grad,
-        qkv_sum[None],
+        qkv_sum.reshape(1, width // pieces, 3, -1),
         out_sum[None],
         up_sum[None],
         down_sum[None],

time: 667 us -> 625 us (0.937)
  Pallas kernels: 515 us -> 494 us
  local copies, waits for them, and re-layouts: 39.5 us -> 26.2 us
  starting transfers between devices: 22.5 us -> 15.6 us
    pallas_call x24, Pallas kernels: 316 us -> 291 us  [call_with_slots(): pl.pallas_call(run, grid_spec=pltpu.PrefetchScalarGridSpec(num_scalar_pre...]
    ppermute x3 -> x1, starting transfers between devices: 13.5 us -> 6.05 us  [paired_body(): remote_grads = lax.ppermute(own_grads, 'section', [(0, 1)])]
  transfers between devices with their start and end apart: 14 -> 12, of which waited for: 3 -> 5; matrix products, arithmetic and copies ran while one was open for 5% -> 2% of each run, Pallas kernels for 63% -> 42%
where the time goes in v3:
time: 625 us; the launch traced here: 617 us
  Pallas kernels  494 us (79%)
  waiting for transfers between devices  69.9 us (11%)
  local copies, waits for them, and re-layouts  26.2 us (4%)
  starting transfers between devices  15.6 us (2%)
  other arithmetic  9.04 us (1%)
    pallas_call x24, Pallas kernels, call_with_slots(): pl.pallas_call(run, grid_spec=pltpu.PrefetchScalarGridSpec(num_scalar_pre...  291 us
    pallas_call x1, Pallas kernels, summed_grads(): pl.pallas_call(grads_kernel, in_specs=[anywhere] * 9 + [local], out_specs...  166 us
    ppermute x2, waiting for transfers between devices, paired_body(): finished.append(lax.ppermute(result, 'section', [(1, 0)]))  38.2 us
    ppermute x2, waiting for transfers between devices, paired_body(): received[micro] = lax.ppermute(low, 'section', [(1, 0)])  29.9 us
    pallas_call x8, Pallas kernels, exchanged(): pl.pallas_call(exchange_kernel, in_specs=[pl.BlockSpec(memory_space=pl.AN...  28.5 us
  transfers between devices with their start and end apart: 12, of which 5 were waited for; matrix products, arithmetic and copies ran while one was open for 2% of the time, Pallas kernels for 42%

profile of v3, /device:TPU:0, one launch (start us, length us, event | category | flops | bytes accessed | tf_op | source)
XLA Modules:
  0.0 617.1 jit_solution(7927070576176990820)
XLA Ops:
  1.3 2.1 slice_bitcast_fusion.2
  8.0 6.1 collective-permute-start.5
  15.4 1.7 collective-permute-done.1.refs_5_.refs_8_
  17.1 9.4 %enter.4 = (bf16[3,512,1024]{2,1,0:T(8,128)(2,1)}, bf16[3,512,1024]{2,1,0:T(8,128)(2,1)}, bf16[3,512,3072]{2,1,0:T(8,128)(2,1)}, bf16[2,256,1024]{2,1,0:T(8,128)(2,1)}) custom-call(s32[6]{0:T(128)} %stack.54.refs_0_, bf16[2,512,1024]{2,1,0:T(8,128)(2,1)} %bitcast.125, f32[1,1024]{1,0:T(1,128)} %slice_bitcast_fusion.6.refs_2_.refs_9_, ...), custom_call_target="tpu_custom_call" | custom-call | flops 450000000 | tf_op jit(solution)/shard_map/enter/pallas_call | solution.py:72
  26.6 3.0 exchange.8.refs_6_.refs_7_
  29.6 15.0 %attend.4 = (bf16[3,512,1024]{2,1,0:T(8,128)(2,1)}, f32[3,8,4,256]{3,2,1,0:T(4,128)}, bf16[3,256,1024]{2,1,0:T(8,128)(2,1)}, bf16[3,256,1024]{2,1,0:T(8,128)(2,1)}) custom-call(s32[6]{0:T(128)} %stack.54.refs_0_, s32[1280]{0:T(1024)} %get-tuple-element.308.refs_1_, s32[10,128]{1,0:T(8,128)} %bitcast.142, ...), custom_call_target="tpu_custom_call" | custom-call | flops 1200000000 | tf_op jit(solution)/shard_map/attend/pallas_call | solution.py:72
  44.6 24.4 %feed.4 = (bf16[3,512,4096]{2,1,0:T(8,128)(2,1)}, bf16[3,512,4096]{2,1,0:T(8,128)(2,1)}, bf16[3,512,1024]{2,1,0:T(8,128)(2,1)}, bf16[3,512,1024]{2,1,0:T(8,128)(...) custom-call(s32[6]{0:T(128)} %stack.54.refs_0_, ...), custom_call_target="tpu_custom_call" | custom-call | flops 1450000000 | tf_op jit(solution)/shard_map/feed/pallas_call | solution.py:72
  69.0 1.4 collective-permute-start.6
  70.4 9.4 %enter.5 = (bf16[3,512,1024]{2,1,0:T(8,128)(2,1)}, bf16[3,512,1024]{2,1,0:T(8,128)(2,1)}, bf16[3,512,3072]{2,1,0:T(8,128)(2,1)}, bf16[2,256,1024]{2,1,0:T(8,128)(2,1)}) custom-call(s32[6]{0:T(128)} %stack.52.refs_0_, bf16[2,512,1024]{2,1,0:T(8,128)(2,1)} %bitcast.126, ...), custom_call_target="tpu_custom_call", output_to_operand_aliasing={{0}: (6, {}), {1}: (7, {}), {2}: (8, {})} | custom-call | flops 450000000 | tf_op jit(solution)/shard_map/enter/pallas_call | solution.py:72
  79.8 3.0 exchange.9.refs_6_.refs_7_
  82.9 13.4 %attend.5 = (bf16[3,512,1024]{2,1,0:T(8,128)(2,1)}, f32[3,8,4,256]{3,2,1,0:T(4,128)}, bf16[3,256,1024]{2,1,0:T(8,128)(2,1)}, bf16[3,256,1024]{2,1,0:T(8,128)(2,1)}) custom-call(s32[6]{0:T(128)} %stack.52.refs_0_, s32[1280]{0:T(1024)} %get-tuple-element.307.refs_1_, ...), custom_call_target="tpu_custom_call", output_to_operand_aliasing={{0}: (8, {}), {1}: (9, {}), {2}: (10, {}), {3}: (11, {})} | custom-call | flops 1200000000 | tf_op jit(solution)/shard_map/attend/pallas_call | solution.py:72
  96.3 24.0 %feed.5 = (bf16[3,512,4096]{2,1,0:T(8,128)(2,1)}, bf16[3,512,4096]{2,1,0:T(8,128)(2,1)}, bf16[3,512,1024]{2,1,0:T(8,128)(2,1)}, bf16[3,512,1024]{2,1,0:T(8,128)(...) custom-call(s32[6]{0:T(128)} %stack.52.refs_0_, ...), custom_call_target="tpu_custom_call", output_to_operand_aliasing={{0}: (12, {}), {1}: (13, {}), {2}: (14, {}), {3}: (15, {}),... | custom-call | flops 1450000000 | tf_op jit(solution)/shard_map/feed/pallas_call | solution.py:72
  120.3 1.4 collective-permute-start.8
  123.9 5.1 toeplitz.1.refs_6_.refs_8_
  130.0 4.4 enter.6
  134.4 4.5 exchange.10.refs_7_.refs_8_
  138.9 4.1 attend.6
  142.9 8.5 %feed.6 = (bf16[3,512,4096]{2,1,0:T(8,128)(2,1)}, bf16[3,512,4096]{2,1,0:T(8,128)(2,1)}, bf16[3,512,1024]{2,1,0:T(8,128)(2,1)}, bf16[3,512,1024]{2,1,0:T(8,128)(...) custom-call(s32[6]{0:T(128)} %stack.50.refs_0_, ...), custom_call_target="tpu_custom_call", output_to_operand_aliasing={{0}: (12, {}), {1}: (13, {}), {2}: (14, {}), {3}: (15, {}),... | custom-call | flops 1450000000 | tf_op jit(solution)/shard_map/feed/pallas_call | solution.py:72
  153.8 4.8 enter.7
  158.6 3.0 exchange.11.refs_7_.refs_8_
  161.6 4.1 attend.7
  165.7 8.5 %feed.7 = (bf16[3,512,4096]{2,1,0:T(8,128)(2,1)}, bf16[3,512,4096]{2,1,0:T(8,128)(2,1)}, bf16[3,512,1024]{2,1,0:T(8,128)(2,1)}, bf16[3,512,1024]{2,1,0:T(8,128)(...) custom-call(s32[6]{0:T(128)} %stack.59.refs_0_, ...), custom_call_target="tpu_custom_call", output_to_operand_aliasing={{0}: (12, {}), {1}: (13, {}), {2}: (14, {}), {3}: (15, {}),... | custom-call | flops 1450000000 | tf_op jit(solution)/shard_map/feed/pallas_call | solution.py:72
  175.6 9.3 %feed_back.4 = (bf16[3,512,1024]{2,1,0:T(8,128)(2,1)}, bf16[3,512,4096]{2,1,0:T(8,128)(2,1)}, bf16[3,512,1024]{2,1,0:T(8,128)(2,1)}, f32[3,8,1024]{2,1,0:T(8,128...) custom-call(s32[6]{0:T(128)} %stack.50.refs_0_, bf16[2,512,1024]{2,1,0:T(8,128)(2,1)} %bitcast.123, ...), custom_call_target="tpu_custom_call" | custom-call | flops 1350000000 | tf_op jit(solution)/shard_map/feed_back/pallas_call | solution.py:72
  184.9 5.6 attend_back.4
  190.5 3.0 exchange.12.refs_4_
  193.5 38.2 %collective-permute-done.9 = bf16[512,1024]{1,0:T(8,128)(2,1)S(1)} collective-permute-done((bf16[512,1024]{1,0:T(8,128)(2,1)}, bf16[512,1024]{1,0:T(8,128)(2,1)S(1)}, u32[]{:S(2)}, u32[]{:S(2)}) %collective-permute-start.9) | collective-permute-done | bytes 1048608 | tf_op jit(solution)/shard_map/ppermute | solution.py:1708
  231.8 6.3 %enter_back.4 = (bf16[3,512,3072]{2,1,0:T(8,128)(2,1)}, f32[3,8,1024]{2,1,0:T(8,128)}, f32[3,512,512]{2,1,0:T(8,128)}, bf16[3,512,512]{2,1,0:T(8,128)(2,1)}, bf16[512,1024]{1,0:T(8,128)(2,1)}) custom-call(s32[6]{0:T(128)} %stack.50.refs_0_, bf16[512,1024]{1,0:T(8,128)(2,1)} %get-tuple-element.210.refs_1_, bf16[512,1024]{1,0:T(8,128)(2,1)} %get-tuple-element.211.refs_2_, ...), custom_call_target="tpu_custom_call" | custom-call | flops 600000000 | tf_op jit(solution)/shard_map/enter_back/pallas_call | solution.py:72
  239.3 9.5 %feed_back.5 = (bf16[3,512,1024]{2,1,0:T(8,128)(2,1)}, bf16[3,512,4096]{2,1,0:T(8,128)(2,1)}, bf16[3,512,1024]{2,1,0:T(8,128)(2,1)}, f32[3,8,1024]{2,1,0:T(8,128...) custom-call(s32[6]{0:T(128)} %stack.59.refs_0_, ...), custom_call_target="tpu_custom_call", output_to_operand_aliasing={{0}: (13, {}), {1}: (14, {}), {2}: (15, {}), {3}: (16, {}),... | custom-call | flops 1350000000 | tf_op jit(solution)/shard_map/feed_back/pallas_call | solution.py:72
  248.9 5.8 attend_back.5
  254.6 3.8 exchange.13.refs_4_
  258.4 6.3 %enter_back.5 = (bf16[3,512,3072]{2,1,0:T(8,128)(2,1)}, f32[3,8,1024]{2,1,0:T(8,128)}, f32[3,512,512]{2,1,0:T(8,128)}, bf16[3,512,512]{2,1,0:T(8,128)(2,1)}, bf16[512,1024]{1,0:T(8,128)(2,1)}) custom-call(s32[6]{0:T(128)} %stack.59.refs_0_, ...), custom_call_target="tpu_custom_call", output_to_operand_aliasing={{0}: (10, {}), {1}: (11, {}), {2}: (12, {}), {3}: (13, {})} | custom-call | flops 600000000 | tf_op jit(solution)/shard_map/enter_back/pallas_call | solution.py:72
  266.0 3.8 diagonals.1
  270.9 3.6 maximum_select_fusion
  274.5 25.8 %collective-permute-done.10 = bf16[512,1024]{1,0:T(8,128)(2,1)S(1)} collective-permute-done((bf16[512,1024]{1,0:T(8,128)(2,1)}, bf16[512,1024]{1,0:T(8,128)(2,1)S(1)}, u32[]{:S(2)}, u32[]{:S(2)}) %collective-permute-start.10) | collective-permute-done | bytes 1048608 | tf_op jit(solution)/shard_map/ppermute | solution.py:1738
  301.3 24.8 %feed_back.6 = (bf16[3,512,1024]{2,1,0:T(8,128)(2,1)}, bf16[3,512,4096]{2,1,0:T(8,128)(2,1)}, bf16[3,512,1024]{2,1,0:T(8,128)(2,1)}, f32[3,8,1024]{2,1,0:T(8,128...) custom-call(s32[6]{0:T(128)} %stack.54.refs_0_, ...), custom_call_target="tpu_custom_call", output_to_operand_aliasing={{0}: (12, {}), {1}: (13, {}), {2}: (14, {}), {3}: (15, {}),... | custom-call | flops 1350000000 | tf_op jit(solution)/shard_map/feed_back/pallas_call | solution.py:72
  326.1 23.4 %attend_back.6 = (bf16[512,1024]{1,0:T(8,128)(2,1)}, bf16[512,1024]{1,0:T(8,128)(2,1)}, bf16[512,1024]{1,0:T(8,128)(2,1)}, bf16[2,256,1024]{2,1,0:T(8,128)(2,1)}) custom-call(s32[6]{0:T(128)} %stack.54.refs_0_, s32[1280]{0:T(1024)} %get-tuple-element.308.refs_1_, s32[10,128]{1,0:T(8,128)} %bitcast.145, ...), custom_call_target="tpu_custom_call" | custom-call | flops 1300000000 | tf_op jit(solution)/shard_map/attend_back/pallas_call | solution.py:72
  349.5 3.0 exchange.14.refs_4_
  352.5 12.0 %enter_back.6 = (bf16[3,512,3072]{2,1,0:T(8,128)(2,1)}, f32[3,8,1024]{2,1,0:T(8,128)}, f32[3,512,512]{2,1,0:T(8,128)}, bf16[3,512,512]{2,1,0:T(8,128)(2,1)}, bf16[512,1024]{1,0:T(8,128)(2,1)}) custom-call(s32[6]{0:T(128)} %stack.54.refs_0_, ...), custom_call_target="tpu_custom_call", output_to_operand_aliasing={{0}: (10, {}), {1}: (11, {}), {2}: (12, {}), {3}: (13, {})} | custom-call | flops 600000000 | tf_op jit(solution)/shard_map/enter_back/pallas_call | solution.py:72
  364.5 4.1 collective-permute-done.11
  369.6 25.2 %feed_back.7 = (bf16[3,512,1024]{2,1,0:T(8,128)(2,1)}, bf16[3,512,4096]{2,1,0:T(8,128)(2,1)}, bf16[3,512,1024]{2,1,0:T(8,128)(2,1)}, f32[3,8,1024]{2,1,0:T(8,128...) custom-call(s32[6]{0:T(128)} %stack.52.refs_0_, ...), custom_call_target="tpu_custom_call", output_to_operand_aliasing={{0}: (12, {}), {1}: (13, {}), {2}: (14, {}), {3}: (15, {}),... | custom-call | flops 1350000000 | tf_op jit(solution)/shard_map/feed_back/pallas_call | solution.py:72
  394.8 20.8 %attend_back.7 = (bf16[512,1024]{1,0:T(8,128)(2,1)}, bf16[512,1024]{1,0:T(8,128)(2,1)}, bf16[512,1024]{1,0:T(8,128)(2,1)}, bf16[2,256,1024]{2,1,0:T(8,128)(2,1)}) custom-call(s32[6]{0:T(128)} %stack.52.refs_0_, s32[1280]{0:T(1024)} %get-tuple-element.307.refs_1_, s32[10,128]{1,0:T(8,128)} %bitcast.141, ...), custom_call_target="tpu_custom_call" | custom-call | flops 1300000000 | tf_op jit(solution)/shard_map/attend_back/pallas_call | solution.py:72
  415.6 5.1 exchange.15.refs_4_
  420.7 12.1 %enter_back.7 = (bf16[3,512,3072]{2,1,0:T(8,128)(2,1)}, f32[3,8,1024]{2,1,0:T(8,128)}, f32[3,512,512]{2,1,0:T(8,128)}, bf16[3,512,512]{2,1,0:T(8,128)(2,1)}, bf16[512,1024]{1,0:T(8,128)(2,1)}) custom-call(s32[6]{0:T(128)} %stack.52.refs_0_, ...), custom_call_target="tpu_custom_call", output_to_operand_aliasing={{0}: (10, {}), {1}: (11, {}), {2}: (12, {}), {3}: (13, {})} | custom-call | flops 600000000 | tf_op jit(solution)/shard_map/enter_back/pallas_call | solution.py:72
  435.0 165.8 %summed_grads.1 = (f32[2048,128]{1,0:T(8,128)}, f32[128,2048]{1,0:T(8,128)}, f32[512,128]{1,0:T(8,128)}, f32[128,1536]{1,0:T(8,128)}, f32[16,1024]{1,0:T(8,128)}, /*index=5*/bf16[2,512,512]{2,1,0:T(8,128)(2,1)}) custom-call(bf16[3,512,4096]{2,1,0:T(8,128)(2,1)} %get-tuple-element.267.f_hbm, bf16[3,512,1024]{2,1,0:T(8,128)(2,1)} %get-tuple-element.268.dy_hbm, ...), custom_call_target="tpu_custom_call" | custom-call | flops 249999998976 | tf_op jit(solution)/shard_map/summed_grads/pallas_call | solution.py:1558
  600.9 1.6 fusion.18
  604.2 2.3 copy.98
  606.4 2.3 copy.100
  611.2 3.0 select_bitcast_fusion
  (127 shorter events, 27.8 us)
Async XLA Ops:
  0.6 5.4 copy-start
  0.7 44.0 %collective-permute-start.3 = (bf16[1024,2048]{1,0:T(8,128)(2,1)}, bf16[1024,2048]{1,0:T(8,128)(2,1)}, u32[]{:S(2)}, u32[]{:S(2)}) collective-permute-start(bf16[1024,2048]{1,0:T(8,128)(2,1)} %bitcast.95), channel_id=1, source_target_pairs={{0,1},{1,0},{2,3},{3,2},{4,5},{5,4},{6,7},{7,6},{8,9},{9,8},{10,11... | collective-permute-start | bytes 12582920 | tf_op jit(solution)/shard_map/ppermute | solution.py:1607
  1.2 43.4 %collective-permute-start.4 = (bf16[2048,1024]{1,0:T(8,128)(2,1)}, bf16[2048,1024]{1,0:T(8,128)(2,1)}, u32[]{:S(2)}, u32[]{:S(2)}) collective-permute-start(bf16[2048,1024]{1,0:T(8,128)(2,1)} %bitcast.104), channel_id=1, source_target_pairs={{0,1},{1,0},{2,3},{3,2},{4,5},{5,4},{6,7},{7,6},{8,9},{9,8},{10,11... | collective-permute-start | bytes 12582920 | tf_op jit(solution)/shard_map/ppermute | solution.py:1607
  3.3 0.8 copy-start.19
  3.3 0.8 copy-start.18
  3.3 0.9 copy-start.17
  3.4 1.5 copy-start.16
  3.6 13.5 %copy-start.2 = (bf16[1024,1536]{1,0:T(8,128)(2,1)}, bf16[1024,1536]{1,0:T(8,128)(2,1)S(1)}, u32[]{:S(2)}) copy-start(bf16[1024,1536]{1,0:T(8,128)(2,1)S(1)} %pad_maximum_fusion.refs_4_.refs_7_) | copy-start | bytes 9437188
  3.6 13.5 %collective-permute-start.1 = (bf16[1024,1536]{1,0:T(8,128)(2,1)S(1)}, bf16[1024,1536]{1,0:T(8,128)(2,1)}, u32[]{:S(2)}, u32[]{:S(2)}) collective-permute-start(bf16[1024,1536]{1,0:T(8,128)(2,1)S(1)} %pad_maximum_fusion.refs_4_.refs_7_), channel_id=1, source_target_pairs={{0,1},{1,0},{2,3},{3,2},{4,5},{5,4},{6,7},{7,6},{8,9},{9,8},{10,11... | collective-permute-start | bytes 9437192 | tf_op jit(solution)/shard_map/ppermute | solution.py:1607
  4.2 3.8 collective-permute-start
  4.6 40.0 %collective-permute-start.2 = (bf16[512,1024]{1,0:T(8,128)(2,1)}, bf16[512,1024]{1,0:T(8,128)(2,1)}, u32[]{:S(2)}, u32[]{:S(2)}) collective-permute-start(bf16[512,1024]{1,0:T(8,128)(2,1)} %bitcast.113), channel_id=1, source_target_pairs={{0,1},{1,0},{2,3},{3,2},{4,5},{5,4},{6,7},{7,6},{8,9},{9,8},{10,11... | collective-permute-start | bytes 3145736 | tf_op jit(solution)/shard_map/ppermute | solution.py:1607
  8.0 120.9 %collective-permute-start.5 = (bf16[2,512,1024]{2,1,0:T(8,128)(2,1)}, bf16[2,512,1024]{2,1,0:T(8,128)(2,1)}, u32[]{:S(2)}, u32[]{:S(2)}) collective-permute-start(bf16[2,512,1024]{2,1,0:T(8,128)(2,1)} %bitcast.122), channel_id=1, source_target_pairs={{0,2},{1,3},{4,6},{5,7},{8,10},{9,11},{12,14},{13,15},{16,18},{17,... | collective-permute-start | bytes 6291464 | tf_op jit(solution)/shard_map/ppermute | solution.py:1635
  69.0 59.9 %collective-permute-start.6 = (bf16[512,1024]{1,0:T(8,128)(2,1)}, bf16[512,1024]{1,0:T(8,128)(2,1)S(1)}, u32[]{:S(2)}, u32[]{:S(2)}) collective-permute-start(bf16[512,1024]{1,0:T(8,128)(2,1)} %get-tuple-element.152), channel_id=1, source_target_pairs={{0,2},{1,3},{4,6},{5,7},{8,10},{9,11},{12,14},{13,15},{16,18},{17,... | collective-permute-start | bytes 3145736 | tf_op jit(solution)/shard_map/ppermute | solution.py:1705
  96.3 25.4 %copy-start.20 = (s32[2047]{0:T(1024)S(1)}, s32[2047]{0:T(1024)}, u32[]{:S(2)}) copy-start(s32[2047]{0:T(1024)} %param.15) | copy-start | bytes 24568
  120.3 32.5 %collective-permute-start.8 = (bf16[512,1024]{1,0:T(8,128)(2,1)}, bf16[512,1024]{1,0:T(8,128)(2,1)S(1)}, u32[]{:S(2)}, u32[]{:S(2)}) collective-permute-start(bf16[512,1024]{1,0:T(8,128)(2,1)} %get-tuple-element.167), channel_id=1, source_target_pairs={{0,2},{1,3},{4,6},{5,7},{8,10},{9,11},{12,14},{13,15},{16,18},{17,... | collective-permute-start | bytes 3145736 | tf_op jit(solution)/shard_map/ppermute | solution.py:1705
  129.0 1.0 copy-start.11
  151.5 42.0 %collective-permute-start.7 = (bf16[512,1024]{1,0:T(8,128)(2,1)}, bf16[512,1024]{1,0:T(8,128)(2,1)S(1)}, u32[]{:S(2)}, u32[]{:S(2)}) collective-permute-start(bf16[512,1024]{1,0:T(8,128)(2,1)} %get-tuple-element.183), channel_id=1, source_target_pairs={{2,0},{3,1},{6,4},{7,5},{10,8},{11,9},{14,12},{15,13},{18,16},{19,... | collective-permute-start | bytes 3145736 | tf_op jit(solution)/shard_map/ppermute | solution.py:1708
  152.8 1.0 copy-start.10
  174.3 57.5 %collective-permute-start.9 = (bf16[512,1024]{1,0:T(8,128)(2,1)}, bf16[512,1024]{1,0:T(8,128)(2,1)S(1)}, u32[]{:S(2)}, u32[]{:S(2)}) collective-permute-start(bf16[512,1024]{1,0:T(8,128)(2,1)} %get-tuple-element.198), channel_id=1, source_target_pairs={{2,0},{3,1},{6,4},{7,5},{10,8},{11,9},{14,12},{15,13},{18,16},{19,... | collective-permute-start | bytes 3145736 | tf_op jit(solution)/shard_map/ppermute | solution.py:1708
  193.5 44.5 %copy-start.8 = (bf16[512,1024]{1,0:T(8,128)(2,1)}, bf16[512,1024]{1,0:T(8,128)(2,1)S(1)}, u32[]{:S(2)}) copy-start(bf16[512,1024]{1,0:T(8,128)(2,1)S(1)} %collective-permute-done.7) | copy-start | bytes 3145732
  231.8 6.3 %copy-start.9 = (bf16[512,1024]{1,0:T(8,128)(2,1)}, bf16[512,1024]{1,0:T(8,128)(2,1)S(1)}, u32[]{:S(2)}) copy-start(bf16[512,1024]{1,0:T(8,128)(2,1)S(1)} %collective-permute-done.9) | copy-start | bytes 3145732
  238.0 62.3 %collective-permute-start.10 = (bf16[512,1024]{1,0:T(8,128)(2,1)}, bf16[512,1024]{1,0:T(8,128)(2,1)S(1)}, u32[]{:S(2)}, u32[]{:S(2)}) collective-permute-start(bf16[512,1024]{1,0:T(8,128)(2,1)} %get-tuple-element.215), channel_id=1, source_target_pairs={{2,0},{3,1},{6,4},{7,5},{10,8},{11,9},{14,12},{15,13},{18,16},{19,... | collective-permute-start | bytes 3145736 | tf_op jit(solution)/shard_map/ppermute | solution.py:1738
  264.7 103.9 %collective-permute-start.11 = (bf16[512,1024]{1,0:T(8,128)(2,1)}, bf16[512,1024]{1,0:T(8,128)(2,1)S(1)}, u32[]{:S(2)}, u32[]{:S(2)}) collective-permute-start(bf16[512,1024]{1,0:T(8,128)(2,1)} %get-tuple-element.233), channel_id=1, source_target_pairs={{2,0},{3,1},{6,4},{7,5},{10,8},{11,9},{14,12},{15,13},{18,16},{19,... | collective-permute-start | bytes 3145736 | tf_op jit(solution)/shard_map/ppermute | solution.py:1738
  266.0 4.9 copy-start.7
  300.3 1.0 copy-start.6
  368.6 1.0 copy-start.5
  420.7 12.1 %copy-start.4 = (f32[3,8,1024]{2,1,0:T(8,128)S(1)}, f32[3,8,1024]{2,1,0:T(8,128)}, u32[]{:S(2)}) copy-start(f32[3,8,1024]{2,1,0:T(8,128)} %get-tuple-element.275) | copy-start | bytes 294916
  420.7 13.0 %copy-start.14 = (f32[3,1,4096]{2,1,0:T(1,128)S(1)}, f32[3,1,4096]{2,1,0:T(1,128)}, u32[]{:S(2)}) copy-start(f32[3,1,4096]{2,1,0:T(1,128)} %get-tuple-element.277) | copy-start | bytes 147460
  600.9 10.3 %copy-start.3 = (f32[3,512,512]{2,1,0:T(8,128)S(1)}, f32[3,512,512]{2,1,0:T(8,128)}, u32[]{:S(2)}) copy-start(f32[3,512,512]{2,1,0:T(8,128)} %get-tuple-element.266) | copy-start | bytes 9437188
  609.4 4.8 copy-start.15
  609.4 5.5 copy-start.13
  611.2 4.7 copy-start.12
  611.2 5.6 copy-start.1

commit v4 on v3

--- a/solution.py
+++ b/solution.py
@@ -58,6 +58,8 @@
                 at += 1
 
     def gated(spec):
+        if spec.index_map is None:
+            return spec
         return pl.BlockSpec(spec.block_shape, lambda j, s, *rest: spec.index_map(j * s[5], s, *rest))
 
     in_specs = [gated(spec) for spec in in_specs]
@@ -213,6 +215,16 @@
         target[pl.ds(pl.multiple_of(info[3] * QB, QB), halo_count), :] = halo[...]
 
 
+def turned_rows(info, source, halo, target, halo_count):
+    edge = PAD * QB
+    rows = source.shape[0]
+    target[:, :edge] = jnp.zeros((target.shape[0], edge), target.dtype)
+    target[:, target.shape[1] - edge :] = jnp.zeros((target.shape[0], edge), target.dtype)
+    target[:, pl.ds(pl.multiple_of(info[2] * QB, QB), rows)] = source[...].T
+    if halo_count:
+        target[:, pl.ds(pl.multiple_of(info[3] * QB, QB), halo_count)] = halo[...].T
+
+
 def attend_kernel(halo_count, with_bias, info, seg_ref, *refs):
     refs = list(refs)
     segq_ref, q_ref, k_ref, v_ref = refs[:4]
@@ -224,7 +236,7 @@
     if halo_count:
         refs.pop(6)[0] = kh_ref[...]
         refs.pop(6)[0] = vh_ref[...]
-    segk_ref, kp_ref, vp_ref, vt_ref, mask_ref, score_ref, prob_ref = refs[6:]
+    segk_ref, kp_ref, vt_ref, mask_ref, score_ref, prob_ref = refs[6:]
     rows = q_ref.shape[1]
     pairs = q_ref.shape[2] // (2 * DH)
     first = lax.broadcasted_iota(jnp.int32, (QB, 2 * DH), 1) < DH
@@ -234,8 +246,7 @@
         fill_columns(segq_ref, segk_ref)
 
     placed_rows(info, k_ref.at[0], kh_ref, kp_ref, halo_count)
-    placed_rows(info, v_ref.at[0], vh_ref, vp_ref, halo_count)
-    vt_ref[...] = vp_ref[...].T
+    turned_rows(info, v_ref.at[0], vh_ref, vt_ref, halo_count)
 
     def block(i, at, reach):
         span = (2 * reach + 1) * QB
@@ -331,7 +342,6 @@
         [
             pltpu.VMEM((blocks * QB, QB), jnp.int32),
             pltpu.VMEM((blocks * QB, span), LOW),
-            pltpu.VMEM((blocks * QB, span), LOW),
             pltpu.VMEM((span, blocks * QB), LOW),
             pltpu.VMEM((5 * QB, QB), F32),
             pltpu.VMEM((pairs, 5 * QB, 2 * QB), F32),
@@ -366,7 +376,7 @@
 
     placed_rows(info, k_ref.at[0], kh_ref, kp_ref, halo_count)
     placed_rows(info, v_ref.at[0], vh_ref, vp_ref, halo_count)
-    kt_ref[...] = kp_ref[...].T
+    turned_rows(info, k_ref.at[0], kh_ref, kt_ref, halo_count)
     dk_acc[...] = jnp.zeros_like(dk_acc)
     dv_acc[...] = jnp.zeros_like(dv_acc)
 
@@ -569,17 +579,47 @@
     )
 
 
+def weight_stream(up, down, up_ref, down_ref, sem, steps):
+    chunk = up_ref.shape[2]
+
+    def copies(part, c, slot):
+        at = pl.ds(pl.multiple_of(c * chunk, chunk), chunk)
+        return [
+            pltpu.make_async_copy(up[part].at[:, at], up_ref.at[slot], sem.at[slot, 0]),
+            pltpu.make_async_copy(down[part].at[at, :], down_ref.at[slot], sem.at[slot, 1]),
+        ]
+
+    def start(j):
+        slot = lax.rem(j, 2)
+        for part in range(2):
+
+            @pl.when((j >= part * (steps // 2)) & (j < (part + 1) * (steps // 2)))
+            def _(part=part):
+                for copy in copies(part, j - part * (steps // 2), slot):
+                    copy.start()
+
+    def wait(j):
+        for copy in copies(0, 0, lax.rem(j, 2)):
+            copy.wait()
+
+    return start, wait
+
+
 def feed_kernel(
     lead, info, x_ref, c_ref, wo_own, wo_oth, up_own, up_oth, down_own, down_oth, bias_ref, gain_ref, shift_ref,
-    f_ref, slope_ref, n_ref, one_ref, two_ref, out_ref, acc_ref, carry_ref, hidden_ref
+    f_ref, slope_ref, n_ref, one_ref, two_ref, out_ref, acc_ref, carry_ref, up_ref, down_ref, sem
 ):
     j = pl.program_id(0)
-    steps = pl.num_programs(0)
+    steps = 2 * up_own.shape[1] // up_ref.shape[2]
     half = wo_own.shape[0]
     rows = x_ref.shape[1]
 
+    start, wait = weight_stream((up_own, up_oth), (down_own, down_oth), up_ref, down_ref, sem, steps)
+
     @pl.when(j == 0)
     def _():
+        start(j)
+        start(j + 1)
         joined = (
             dot_nn(c_ref[0, :, :half], wo_own[...])
             + dot_nn(c_ref[0, :, half:], wo_oth[...])
@@ -603,42 +643,18 @@
 
         acc_ref[...] = jnp.zeros_like(acc_ref)
 
-    each = (steps - 1) // 2
-    now = lax.rem(j, 2)
-
-    def rise(up):
-        u = dot_nn(n_ref[0], up[...]) + bias_ref[...]
-        f, slope = gelu_parts(u)
-        low = f.astype(LOW)
-        f_ref[0] = low
-        hidden_ref[now] = low
-        slope_ref[0] = slope.astype(LOW)
-
-    def fall(down):
-        acc_ref[...] += dot_nn(hidden_ref[1 - now], down[...])
-
-    @pl.when(j == 0)
+    wait(j)
+
+    @pl.when((j > 0) & (j + 1 < steps))
     def _():
-        rise(up_own)
-
-    @pl.when((j > 0) & (j < each))
-    def _():
-        rise(up_own)
-        fall(down_own)
-
-    @pl.when(j == each)
-    def _():
-        rise(up_oth)
-        fall(down_own)
-
-    @pl.when((j > each) & (j < steps - 1))
-    def _():
-        rise(up_oth)
-        fall(down_oth)
-
-    @pl.when(j == steps - 1)
-    def _():
-        fall(down_oth)
+        start(j + 1)
+
+    slot = lax.rem(j, 2)
+    u = dot_nn(n_ref[0], up_ref[slot]) + bias_ref[...]
+    f, slope = gelu_parts(u)
+    f_ref[0] = f.astype(LOW)
+    slope_ref[0] = slope.astype(LOW)
+    acc_ref[...] += dot_nn(f_ref[0], down_ref[slot])
 
     @pl.when(j == steps - 1)
     def _():
@@ -658,26 +674,15 @@
             out_ref[...] = joined.astype(LOW)
 
 
-def split_steps(hidden, chunk):
-    each = hidden // chunk
-    near = lambda j: jnp.minimum(j, each - 1)
-    far = lambda j: jnp.maximum(j - each, 0)
-    return 2 * each, near, far
-
-
 def feed(lead, info, x, context, wo, up, down, bias, gains, shifts, previous):
     _, rows, width = x.shape
     hidden = up[0].shape[1]
     chunk = min(FEED_CHUNK, hidden)
-    each = hidden // chunk
-    steps = 2 * each + 1
-    rise = lambda j: jnp.minimum(j, 2 * each - 1)
-    fall = lambda j: jnp.maximum(j - 1, 0)
-    near = lambda j: jnp.minimum(j, each - 1)
-    far = lambda j: jnp.maximum(j - each, 0)
+    steps = 2 * hidden // chunk
+    anywhere = pl.BlockSpec(memory_space=pl.ANY)
     kept = pl.BlockSpec((1, rows, width), lambda j, s: (s[1], 0, 0))
     fixed = lambda a: pl.BlockSpec(a.shape, lambda j, s: (0, 0))
-    moving = pl.BlockSpec((1, rows, chunk), lambda j, s: (s[1], 0, rise(j)))
+    moving = pl.BlockSpec((1, rows, chunk), lambda j, s: (s[1], 0, j))
     keep = None if previous is None else list(previous) + [None]
     return call_with_slots(
         functools.partial(feed_kernel, lead),
@@ -688,11 +693,11 @@
             kept,
             fixed(wo[0]),
             fixed(wo[1]),
-            pl.BlockSpec((width, chunk), lambda j, s: (0, near(rise(j)))),
-            pl.BlockSpec((width, chunk), lambda j, s: (0, far(rise(j)))),
-            pl.BlockSpec((chunk, width), lambda j, s: (near(fall(j)), 0)),
-            pl.BlockSpec((chunk, width), lambda j, s: (far(fall(j)), 0)),
-            pl.BlockSpec((1, chunk), lambda j, s: (0, rise(j))),
+            anywhere,
+            anywhere,
+            anywhere,
+            anywhere,
+            pl.BlockSpec((1, chunk), lambda j, s: (0, j)),
             fixed(gains),
             fixed(shifts),
         ],
@@ -710,7 +715,9 @@
         [
             pltpu.VMEM((rows, width), F32),
             pltpu.VMEM((rows, width), F32),
-            pltpu.VMEM((2, rows, chunk), LOW),
+            pltpu.VMEM((2, width, chunk), LOW),
+            pltpu.VMEM((2, chunk, width), LOW),
+            pltpu.SemaphoreType.DMA((2, 2)),
         ],
         "feed",
         29,
@@ -744,15 +751,23 @@
 
 def feed_back_steps(
     lead, got_refs, one_ref, two_ref, slope_ref, wo_own, wo_oth, up_own, up_oth, down_own, down_oth,
-    gain_ref, dy_ref, du_ref, db_ref, stat_ref, bias_ref, dz_ref, dc_ref, acc_ref, carry_ref
+    gain_ref, dy_ref, du_ref, db_ref, stat_ref, bias_ref, dz_ref, dc_ref, acc_ref, carry_ref, up_ref, down_ref, wo_ref, sem, wo_sem
 ):
     j = pl.program_id(0)
-    steps = pl.num_programs(0)
+    steps = 2 * up_own.shape[1] // up_ref.shape[2]
+    start, wait = weight_stream((up_own, up_oth), (down_own, down_oth), up_ref, down_ref, sem, steps)
+    wo_copies = [
+        pltpu.make_async_copy(source, wo_ref.at[part], wo_sem.at[part]) for part, source in enumerate((wo_own, wo_oth))
+    ]
     half = wo_own.shape[0]
     rows = dy_ref.shape[1]
 
     @pl.when(j == 0)
     def _():
+        start(j)
+        start(j + 1)
+        for copy in wo_copies:
+            copy.start()
         stat_ref[...] = jnp.zeros_like(stat_ref)
         acc_ref[...] = jnp.zeros_like(acc_ref)
 
@@ -772,19 +787,17 @@
             carry_ref[...] = grad
             dy_ref[0] = grad.astype(LOW)
 
-    def part(up, down):
-        grad = dot_nt(dy_ref[0], down[...])
-        du_ref[0] = (grad * slope_ref[0].astype(F32)).astype(LOW)
-        acc_ref[...] += dot_nt(du_ref[0], up[...])
-        bias_ref[0] = sum_rows(du_ref[0].astype(F32))
-
-    @pl.when(j < steps // 2)
+    wait(j)
+
+    @pl.when((j > 0) & (j + 1 < steps))
     def _():
-        part(up_own, down_own)
-
-    @pl.when(j >= steps // 2)
-    def _():
-        part(up_oth, down_oth)
+        start(j + 1)
+
+    slot = lax.rem(j, 2)
+    grad = dot_nt(dy_ref[0], down_ref[slot])
+    du_ref[0] = (grad * slope_ref[0].astype(F32)).astype(LOW)
+    acc_ref[...] += dot_nt(du_ref[0], up_ref[slot])
+    bias_ref[0] = sum_rows(du_ref[0].astype(F32))
 
     @pl.when(j == steps - 1)
     def _():
@@ -803,17 +816,20 @@
             stat_ref[0, 1:2, :] = gain
             dz_ref[...] = carry_ref[...] + back
 
+        for copy in wo_copies:
+            copy.wait()
         low = dz_ref[...].astype(LOW)
         db_ref[0] = low
-        dc_ref[:, :half] = dot_nt(low, wo_own[...]).astype(LOW)
-        dc_ref[:, half:] = dot_nt(low, wo_oth[...]).astype(LOW)
+        dc_ref[:, :half] = dot_nt(low, wo_ref[0]).astype(LOW)
+        dc_ref[:, half:] = dot_nt(low, wo_ref[1]).astype(LOW)
 
 
 def feed_back(lead, info, got, at, one, two, slope, wo, up, down, gains, previous):
     _, rows, width = one.shape
     hidden = up[0].shape[1]
     chunk = min(FEED_CHUNK, hidden)
-    steps, near, far = split_steps(hidden, chunk)
+    steps = 2 * hidden // chunk
+    anywhere = pl.BlockSpec(memory_space=pl.ANY)
     kept = pl.BlockSpec((1, rows, width), lambda j, s: (s[1], 0, 0))
     fixed = lambda a: pl.BlockSpec(a.shape, lambda j, s: (0, 0))
     plain = pl.BlockSpec((rows, width), lambda j, s: (0, 0))
@@ -828,12 +844,12 @@
             kept,
             kept,
             moving,
-            fixed(wo[0]),
-            fixed(wo[1]),
-            pl.BlockSpec((width, chunk), lambda j, s: (0, near(j))),
-            pl.BlockSpec((width, chunk), lambda j, s: (0, far(j))),
-            pl.BlockSpec((chunk, width), lambda j, s: (near(j), 0)),
-            pl.BlockSpec((chunk, width), lambda j, s: (far(j), 0)),
+            anywhere,
+            anywhere,
+            anywhere,
+            anywhere,
+            anywhere,
+            anywhere,
             fixed(gains),
         ],
         [
@@ -856,7 +872,15 @@
         ],
         keep,
         (steps,),
-        [pltpu.VMEM((rows, width), F32), pltpu.VMEM((rows, width), F32)],
+        [
+            pltpu.VMEM((rows, width), F32),
+            pltpu.VMEM((rows, width), F32),
+            pltpu.VMEM((2, width, chunk), LOW),
+            pltpu.VMEM((2, chunk, width), LOW),
+            pltpu.VMEM((2,) + wo[0].shape, LOW),
+            pltpu.SemaphoreType.DMA((2, 2)),
+            pltpu.SemaphoreType.DMA((2,)),
+        ],
         "feed_back",
         27,
     )
@@ -1632,7 +1656,6 @@
     pieces = lax.axis_size("dp")
 
     own_grads = decoder_grads[0, :, 0]
-    remote_grads = lax.ppermute(own_grads, "section", [(0, 1)])
     given_rows = layer_input[:, 0]
     qkv_own = jnp.concatenate([attn_in[0, :, part] for part in range(3)], axis=1)
     qkv_oth = swapped(qkv_own, "tensor", 1)
@@ -1694,6 +1717,9 @@
             lead_turn, info, given, at, entry_gain, qkv_shift, qkv_own, qkv_oth, entered
         )
         halo = exchanged(halo)
+        if turn + micro == 0:
+            later, _ = lax.optimization_barrier((own_grads, halo))
+            remote_grads = lax.ppermute(later, "section", [(0, 1)])
         attended = attend(
             info, segments[micro], entered[2], halo, None if lead_turn else bias, attended
         )

time: 625 us -> 616 us (0.986)
  Pallas kernels: 494 us -> 469 us
  waiting for transfers between devices: 69.9 us -> 88.4 us
    pallas_call x24, Pallas kernels: 291 us -> 268 us  [call_with_slots(): pl.pallas_call(run, grid_spec=pltpu.PrefetchScalarGridSpec(num_scalar_pre...]
    ppermute x5, waiting for transfers between devices: 1.81 us -> 10.3 us  [swapped(): return lax.ppermute(value, axis, pairs)]
    ppermute x2, waiting for transfers between devices: 38.2 us -> 44.5 us  [paired_body(): finished.append(lax.ppermute(result, 'section', [(1, 0)]))]
  transfers between devices with their start and end apart: 12 -> 12, of which waited for: 5 -> 5; matrix products, arithmetic and copies ran while one was open for 2% -> 2% of each run, Pallas kernels for 42% -> 39%
where the time goes in v4:
time: 616 us; the launch traced here: 606 us
  Pallas kernels  469 us (76%)
  waiting for transfers between devices  88.4 us (14%)
  local copies, waits for them, and re-layouts  25.4 us (4%)
  starting transfers between devices  12.9 us (2%)
  other arithmetic  9.04 us (1%)
    pallas_call x24, Pallas kernels, call_with_slots(): pl.pallas_call(run, grid_spec=pltpu.PrefetchScalarGridSpec(num_scalar_pre...  268 us
    pallas_call x1, Pallas kernels, summed_grads(): pl.pallas_call(grads_kernel, in_specs=[anywhere] * 9 + [local], out_specs...  167 us
    ppermute x2, waiting for transfers between devices, paired_body(): finished.append(lax.ppermute(result, 'section', [(1, 0)]))  44.5 us
    ppermute x2, waiting for transfers between devices, paired_body(): received[micro] = lax.ppermute(low, 'section', [(1, 0)])  33.6 us
    pallas_call x8, Pallas kernels, exchanged(): pl.pallas_call(exchange_kernel, in_specs=[pl.BlockSpec(memory_space=pl.AN...  24.2 us
  transfers between devices with their start and end apart: 12, of which 5 were waited for; matrix products, arithmetic and copies ran while one was open for 2% of the time, Pallas kernels for 39%

profile of v4, /device:TPU:0, one launch (start us, length us, event | category | flops | bytes accessed | tf_op | source)
XLA Modules:
  0.0 606.4 jit_solution(15052790890599710943)
XLA Ops:
  1.3 2.1 slice_bitcast_fusion.2
  6.1 1.9 collective-permute-done
  8.7 8.4 %collective-permute-done.1.refs_5_.refs_8_ = bf16[1024,1536]{1,0:T(8,128)(2,1)} collective-permute-done((bf16[1024,1536]{1,0:T(8,128)(2,1)S(1)}, bf16[1024,1536]{1,0:T(8,128)(2,1)}, u32[]{:S(2)}, u32[]{:S(2)}) %collective-permute-start.1) | collective-permute-done | bytes 3145760 | tf_op jit(solution)/shard_map/ppermute | solution.py:1631
  17.1 9.4 %enter.4 = (bf16[3,512,1024]{2,1,0:T(8,128)(2,1)}, bf16[3,512,1024]{2,1,0:T(8,128)(2,1)}, bf16[3,512,3072]{2,1,0:T(8,128)(2,1)}, bf16[2,256,1024]{2,1,0:T(8,128)(2,1)}) custom-call(s32[6]{0:T(128)} %stack.54.refs_0_, bf16[2,512,1024]{2,1,0:T(8,128)(2,1)} %bitcast.125, f32[1,1024]{1,0:T(1,128)} %slice_bitcast_fusion.6.refs_2_.refs_9_, ...), custom_call_target="tpu_custom_call" | custom-call | flops 450000000 | tf_op jit(solution)/shard_map/enter/pallas_call | solution.py:74
  26.6 3.0 exchange.8.refs_6_.refs_7_
  33.6 14.5 %attend.4 = (bf16[3,512,1024]{2,1,0:T(8,128)(2,1)}, f32[3,8,4,256]{3,2,1,0:T(4,128)}, bf16[3,256,1024]{2,1,0:T(8,128)(2,1)}, bf16[3,256,1024]{2,1,0:T(8,128)(2,1)}) custom-call(s32[6]{0:T(128)} %stack.54.refs_0_, s32[1280]{0:T(1024)} %get-tuple-element.310.refs_1_, s32[10,128]{1,0:T(8,128)} %bitcast.141, ...), custom_call_target="tpu_custom_call" | custom-call | flops 1200000000 | tf_op jit(solution)/shard_map/attend/pallas_call | solution.py:74
  48.1 21.3 %feed.4 = (bf16[3,512,4096]{2,1,0:T(8,128)(2,1)}, bf16[3,512,4096]{2,1,0:T(8,128)(2,1)}, bf16[3,512,1024]{2,1,0:T(8,128)(2,1)}, bf16[3,512,1024]{2,1,0:T(8,128)(...) custom-call(s32[6]{0:T(128)} %stack.54.refs_0_, ...), custom_call_target="tpu_custom_call" | custom-call | flops 1450000000 | tf_op jit(solution)/shard_map/feed/pallas_call | solution.py:74
  69.4 2.5 collective-permute-start.6
  71.9 9.4 %enter.5 = (bf16[3,512,1024]{2,1,0:T(8,128)(2,1)}, bf16[3,512,1024]{2,1,0:T(8,128)(2,1)}, bf16[3,512,3072]{2,1,0:T(8,128)(2,1)}, bf16[2,256,1024]{2,1,0:T(8,128)(2,1)}) custom-call(s32[6]{0:T(128)} %stack.52.refs_0_, bf16[2,512,1024]{2,1,0:T(8,128)(2,1)} %bitcast.126, ...), custom_call_target="tpu_custom_call", output_to_operand_aliasing={{0}: (6, {}), {1}: (7, {}), {2}: (8, {})} | custom-call | flops 450000000 | tf_op jit(solution)/shard_map/enter/pallas_call | solution.py:74
  81.3 3.0 exchange.9.refs_6_.refs_7_
  84.3 14.5 %attend.5 = (bf16[3,512,1024]{2,1,0:T(8,128)(2,1)}, f32[3,8,4,256]{3,2,1,0:T(4,128)}, bf16[3,256,1024]{2,1,0:T(8,128)(2,1)}, bf16[3,256,1024]{2,1,0:T(8,128)(2,1)}) custom-call(s32[6]{0:T(128)} %stack.52.refs_0_, s32[1280]{0:T(1024)} %get-tuple-element.309.refs_1_, ...), custom_call_target="tpu_custom_call", output_to_operand_aliasing={{0}: (8, {}), {1}: (9, {}), {2}: (10, {}), {3}: (11, {})} | custom-call | flops 1200000000 | tf_op jit(solution)/shard_map/attend/pallas_call | solution.py:74
  98.9 21.3 %feed.5 = (bf16[3,512,4096]{2,1,0:T(8,128)(2,1)}, bf16[3,512,4096]{2,1,0:T(8,128)(2,1)}, bf16[3,512,1024]{2,1,0:T(8,128)(2,1)}, bf16[3,512,1024]{2,1,0:T(8,128)(...) custom-call(s32[6]{0:T(128)} %stack.52.refs_0_, ...), custom_call_target="tpu_custom_call", output_to_operand_aliasing={{0}: (12, {}), {1}: (13, {}), {2}: (14, {}), {3}: (15, {}),... | custom-call | flops 1450000000 | tf_op jit(solution)/shard_map/feed/pallas_call | solution.py:74
  120.2 1.8 collective-permute-start.8
  124.3 5.1 toeplitz.1.refs_6_.refs_8_
  129.4 4.4 enter.6
  133.9 3.0 exchange.10.refs_7_.refs_8_
  136.9 4.1 attend.6
  141.0 5.7 feed.6
  149.2 4.4 enter.7
  153.6 3.0 exchange.11.refs_7_.refs_8_
  156.6 4.1 attend.7
  160.8 5.6 feed.7
  167.9 6.0 feed_back.4
  173.9 5.6 attend_back.4
  179.5 3.0 exchange.12.refs_4_
  182.6 44.5 %collective-permute-done.9 = bf16[512,1024]{1,0:T(8,128)(2,1)S(1)} collective-permute-done((bf16[512,1024]{1,0:T(8,128)(2,1)}, bf16[512,1024]{1,0:T(8,128)(2,1)S(1)}, u32[]{:S(2)}, u32[]{:S(2)}) %collective-permute-start.9) | collective-permute-done | bytes 1048608 | tf_op jit(solution)/shard_map/ppermute | solution.py:1734
  227.1 6.7 %enter_back.4 = (bf16[3,512,3072]{2,1,0:T(8,128)(2,1)}, f32[3,8,1024]{2,1,0:T(8,128)}, f32[3,512,512]{2,1,0:T(8,128)}, bf16[3,512,512]{2,1,0:T(8,128)(2,1)}, bf16[512,1024]{1,0:T(8,128)(2,1)}) custom-call(s32[6]{0:T(128)} %stack.50.refs_0_, bf16[512,1024]{1,0:T(8,128)(2,1)} %get-tuple-element.212.refs_1_, bf16[512,1024]{1,0:T(8,128)(2,1)} %get-tuple-element.213.refs_2_, ...), custom_call_target="tpu_custom_call" | custom-call | flops 600000000 | tf_op jit(solution)/shard_map/enter_back/pallas_call | solution.py:74
  235.1 6.0 feed_back.5
  241.1 5.5 attend_back.5
  246.6 3.0 exchange.13.refs_4_
  249.6 6.5 %enter_back.5 = (bf16[3,512,3072]{2,1,0:T(8,128)(2,1)}, f32[3,8,1024]{2,1,0:T(8,128)}, f32[3,512,512]{2,1,0:T(8,128)}, bf16[3,512,512]{2,1,0:T(8,128)(2,1)}, bf16[512,1024]{1,0:T(8,128)(2,1)}) custom-call(s32[6]{0:T(128)} %stack.59.refs_0_, ...), custom_call_target="tpu_custom_call", output_to_operand_aliasing={{0}: (10, {}), {1}: (11, {}), {2}: (12, {}), {3}: (13, {})} | custom-call | flops 600000000 | tf_op jit(solution)/shard_map/enter_back/pallas_call | solution.py:74
  257.4 3.8 diagonals.1
  262.3 3.6 maximum_select_fusion
  265.9 28.7 %collective-permute-done.10 = bf16[512,1024]{1,0:T(8,128)(2,1)S(1)} collective-permute-done((bf16[512,1024]{1,0:T(8,128)(2,1)}, bf16[512,1024]{1,0:T(8,128)(2,1)S(1)}, u32[]{:S(2)}, u32[]{:S(2)}) %collective-permute-start.10) | collective-permute-done | bytes 1048608 | tf_op jit(solution)/shard_map/ppermute | solution.py:1764
  295.6 21.3 %feed_back.6 = (bf16[3,512,1024]{2,1,0:T(8,128)(2,1)}, bf16[3,512,4096]{2,1,0:T(8,128)(2,1)}, bf16[3,512,1024]{2,1,0:T(8,128)(2,1)}, f32[3,8,1024]{2,1,0:T(8,128...) custom-call(s32[6]{0:T(128)} %stack.54.refs_0_, ...), custom_call_target="tpu_custom_call", output_to_operand_aliasing={{0}: (12, {}), {1}: (13, {}), {2}: (14, {}), {3}: (15, {}),... | custom-call | flops 1350000000 | tf_op jit(solution)/shard_map/feed_back/pallas_call | solution.py:74
  316.9 23.0 %attend_back.6 = (bf16[512,1024]{1,0:T(8,128)(2,1)}, bf16[512,1024]{1,0:T(8,128)(2,1)}, bf16[512,1024]{1,0:T(8,128)(2,1)}, bf16[2,256,1024]{2,1,0:T(8,128)(2,1)}) custom-call(s32[6]{0:T(128)} %stack.54.refs_0_, s32[1280]{0:T(1024)} %get-tuple-element.310.refs_1_, s32[10,128]{1,0:T(8,128)} %bitcast.144, ...), custom_call_target="tpu_custom_call" | custom-call | flops 1300000000 | tf_op jit(solution)/shard_map/attend_back/pallas_call | solution.py:74
  339.9 3.0 exchange.14.refs_4_
  342.9 12.0 %enter_back.6 = (bf16[3,512,3072]{2,1,0:T(8,128)(2,1)}, f32[3,8,1024]{2,1,0:T(8,128)}, f32[3,512,512]{2,1,0:T(8,128)}, bf16[3,512,512]{2,1,0:T(8,128)(2,1)}, bf16[512,1024]{1,0:T(8,128)(2,1)}) custom-call(s32[6]{0:T(128)} %stack.54.refs_0_, ...), custom_call_target="tpu_custom_call", output_to_operand_aliasing={{0}: (10, {}), {1}: (11, {}), {2}: (12, {}), {3}: (13, {})} | custom-call | flops 600000000 | tf_op jit(solution)/shard_map/enter_back/pallas_call | solution.py:74
  354.9 4.9 collective-permute-done.11
  360.7 21.7 %feed_back.7 = (bf16[3,512,1024]{2,1,0:T(8,128)(2,1)}, bf16[3,512,4096]{2,1,0:T(8,128)(2,1)}, bf16[3,512,1024]{2,1,0:T(8,128)(2,1)}, f32[3,8,1024]{2,1,0:T(8,128...) custom-call(s32[6]{0:T(128)} %stack.52.refs_0_, ...), custom_call_target="tpu_custom_call", output_to_operand_aliasing={{0}: (12, {}), {1}: (13, {}), {2}: (14, {}), {3}: (15, {}),... | custom-call | flops 1350000000 | tf_op jit(solution)/shard_map/feed_back/pallas_call | solution.py:74
  382.4 22.8 %attend_back.7 = (bf16[512,1024]{1,0:T(8,128)(2,1)}, bf16[512,1024]{1,0:T(8,128)(2,1)}, bf16[512,1024]{1,0:T(8,128)(2,1)}, bf16[2,256,1024]{2,1,0:T(8,128)(2,1)}) custom-call(s32[6]{0:T(128)} %stack.52.refs_0_, s32[1280]{0:T(1024)} %get-tuple-element.309.refs_1_, s32[10,128]{1,0:T(8,128)} %bitcast.140, ...), custom_call_target="tpu_custom_call" | custom-call | flops 1300000000 | tf_op jit(solution)/shard_map/attend_back/pallas_call | solution.py:74
  405.2 3.0 exchange.15.refs_4_
  408.2 12.3 %enter_back.7 = (bf16[3,512,3072]{2,1,0:T(8,128)(2,1)}, f32[3,8,1024]{2,1,0:T(8,128)}, f32[3,512,512]{2,1,0:T(8,128)}, bf16[3,512,512]{2,1,0:T(8,128)(2,1)}, bf16[512,1024]{1,0:T(8,128)(2,1)}) custom-call(s32[6]{0:T(128)} %stack.52.refs_0_, ...), custom_call_target="tpu_custom_call", output_to_operand_aliasing={{0}: (10, {}), {1}: (11, {}), {2}: (12, {}), {3}: (13, {})} | custom-call | flops 600000000 | tf_op jit(solution)/shard_map/enter_back/pallas_call | solution.py:74
  422.7 167.5 %summed_grads.1 = (f32[2048,128]{1,0:T(8,128)}, f32[128,2048]{1,0:T(8,128)}, f32[512,128]{1,0:T(8,128)}, f32[128,1536]{1,0:T(8,128)}, f32[16,1024]{1,0:T(8,128)}, /*index=5*/bf16[2,512,512]{2,1,0:T(8,128)(2,1)}) custom-call(bf16[3,512,4096]{2,1,0:T(8,128)(2,1)} %get-tuple-element.269.f_hbm, bf16[3,512,1024]{2,1,0:T(8,128)(2,1)} %get-tuple-element.270.dy_hbm, ...), custom_call_target="tpu_custom_call" | custom-call | flops 249999998976 | tf_op jit(solution)/shard_map/summed_grads/pallas_call | solution.py:1582
  590.2 1.6 fusion.18
  593.5 2.3 copy.98
  595.7 2.3 copy.100
  600.5 3.0 select_bitcast_fusion
  (127 shorter events, 28.6 us)
Async XLA Ops:
  0.6 31.0 %copy-start = (s32[2,1,1024]{2,1,0:T(1,128)S(1)}, s32[2,1,1024]{2,1,0:T(1,128)}, u32[]{:S(2)}) copy-start(s32[2,1,1024]{2,1,0:T(1,128)} %param.14) | copy-start | bytes 24580
  0.7 47.4 %collective-permute-start.3 = (bf16[1024,2048]{1,0:T(8,128)(2,1)}, bf16[1024,2048]{1,0:T(8,128)(2,1)}, u32[]{:S(2)}, u32[]{:S(2)}) collective-permute-start(bf16[1024,2048]{1,0:T(8,128)(2,1)} %bitcast.95), channel_id=1, source_target_pairs={{0,1},{1,0},{2,3},{3,2},{4,5},{5,4},{6,7},{7,6},{8,9},{9,8},{10,11... | collective-permute-start | bytes 12582920 | tf_op jit(solution)/shard_map/ppermute | solution.py:1631
  1.2 46.9 %collective-permute-start.4 = (bf16[2048,1024]{1,0:T(8,128)(2,1)}, bf16[2048,1024]{1,0:T(8,128)(2,1)}, u32[]{:S(2)}, u32[]{:S(2)}) collective-permute-start(bf16[2048,1024]{1,0:T(8,128)(2,1)} %bitcast.104), channel_id=1, source_target_pairs={{0,1},{1,0},{2,3},{3,2},{4,5},{5,4},{6,7},{7,6},{8,9},{9,8},{10,11... | collective-permute-start | bytes 12582920 | tf_op jit(solution)/shard_map/ppermute | solution.py:1631
  3.3 0.8 copy-start.19
  3.3 0.8 copy-start.18
  3.3 0.9 copy-start.17
  3.4 1.5 copy-start.16
  3.6 13.5 %copy-start.2 = (bf16[1024,1536]{1,0:T(8,128)(2,1)}, bf16[1024,1536]{1,0:T(8,128)(2,1)S(1)}, u32[]{:S(2)}) copy-start(bf16[1024,1536]{1,0:T(8,128)(2,1)S(1)} %pad_maximum_fusion.refs_4_.refs_7_) | copy-start | bytes 9437188
  3.6 13.5 %collective-permute-start.1 = (bf16[1024,1536]{1,0:T(8,128)(2,1)S(1)}, bf16[1024,1536]{1,0:T(8,128)(2,1)}, u32[]{:S(2)}, u32[]{:S(2)}) collective-permute-start(bf16[1024,1536]{1,0:T(8,128)(2,1)S(1)} %pad_maximum_fusion.refs_4_.refs_7_), channel_id=1, source_target_pairs={{0,1},{1,0},{2,3},{3,2},{4,5},{5,4},{6,7},{7,6},{8,9},{9,8},{10,11... | collective-permute-start | bytes 9437192 | tf_op jit(solution)/shard_map/ppermute | solution.py:1631
  4.2 3.8 collective-permute-start
  4.6 43.5 %collective-permute-start.2 = (bf16[512,1024]{1,0:T(8,128)(2,1)}, bf16[512,1024]{1,0:T(8,128)(2,1)}, u32[]{:S(2)}, u32[]{:S(2)}) collective-permute-start(bf16[512,1024]{1,0:T(8,128)(2,1)} %bitcast.113), channel_id=1, source_target_pairs={{0,1},{1,0},{2,3},{3,2},{4,5},{5,4},{6,7},{7,6},{8,9},{9,8},{10,11... | collective-permute-start | bytes 3145736 | tf_op jit(solution)/shard_map/ppermute | solution.py:1631
  29.6 99.8 %collective-permute-start.5 = (bf16[2,512,1024]{2,1,0:T(8,128)(2,1)}, bf16[2,512,1024]{2,1,0:T(8,128)(2,1)S(1)}, u32[]{:S(2)}, u32[]{:S(2)}) collective-permute-start(bf16[2,512,1024]{2,1,0:T(8,128)(2,1)} %bitcast.122), channel_id=1, source_target_pairs={{0,2},{1,3},{4,6},{5,7},{8,10},{9,11},{12,14},{13,15},{16,18},{17,... | collective-permute-start | bytes 6291464 | tf_op jit(solution)/shard_map/ppermute | solution.py:1722
  69.4 60.0 %collective-permute-start.6 = (bf16[512,1024]{1,0:T(8,128)(2,1)}, bf16[512,1024]{1,0:T(8,128)(2,1)}, u32[]{:S(2)}, u32[]{:S(2)}) collective-permute-start(bf16[512,1024]{1,0:T(8,128)(2,1)} %get-tuple-element.153), channel_id=1, source_target_pairs={{0,2},{1,3},{4,6},{5,7},{8,10},{9,11},{12,14},{13,15},{16,18},{17,... | collective-permute-start | bytes 3145736 | tf_op jit(solution)/shard_map/ppermute | solution.py:1731
  98.9 23.1 %copy-start.20 = (s32[2047]{0:T(1024)S(1)}, s32[2047]{0:T(1024)}, u32[]{:S(2)}) copy-start(s32[2047]{0:T(1024)} %param.15) | copy-start | bytes 24568
  120.2 28.0 %collective-permute-start.8 = (bf16[512,1024]{1,0:T(8,128)(2,1)}, bf16[512,1024]{1,0:T(8,128)(2,1)S(1)}, u32[]{:S(2)}, u32[]{:S(2)}) collective-permute-start(bf16[512,1024]{1,0:T(8,128)(2,1)} %get-tuple-element.168), channel_id=1, source_target_pairs={{0,2},{1,3},{4,6},{5,7},{8,10},{9,11},{12,14},{13,15},{16,18},{17,... | collective-permute-start | bytes 3145736 | tf_op jit(solution)/shard_map/ppermute | solution.py:1731
  129.4 4.5 copy-start.4
  146.7 35.9 %collective-permute-start.7 = (bf16[512,1024]{1,0:T(8,128)(2,1)}, bf16[512,1024]{1,0:T(8,128)(2,1)S(1)}, u32[]{:S(2)}, u32[]{:S(2)}) collective-permute-start(bf16[512,1024]{1,0:T(8,128)(2,1)} %get-tuple-element.185), channel_id=1, source_target_pairs={{2,0},{3,1},{6,4},{7,5},{10,8},{11,9},{14,12},{15,13},{18,16},{19,... | collective-permute-start | bytes 3145736 | tf_op jit(solution)/shard_map/ppermute | solution.py:1734
  148.2 1.0 copy-start.11
  166.4 60.7 %collective-permute-start.9 = (bf16[512,1024]{1,0:T(8,128)(2,1)}, bf16[512,1024]{1,0:T(8,128)(2,1)S(1)}, u32[]{:S(2)}, u32[]{:S(2)}) collective-permute-start(bf16[512,1024]{1,0:T(8,128)(2,1)} %get-tuple-element.200), channel_id=1, source_target_pairs={{2,0},{3,1},{6,4},{7,5},{10,8},{11,9},{14,12},{15,13},{18,16},{19,... | collective-permute-start | bytes 3145736 | tf_op jit(solution)/shard_map/ppermute | solution.py:1734
  182.6 51.2 %copy-start.9 = (bf16[512,1024]{1,0:T(8,128)(2,1)}, bf16[512,1024]{1,0:T(8,128)(2,1)S(1)}, u32[]{:S(2)}) copy-start(bf16[512,1024]{1,0:T(8,128)(2,1)S(1)} %collective-permute-done.7) | copy-start | bytes 3145732
  227.1 6.7 %copy-start.10 = (bf16[512,1024]{1,0:T(8,128)(2,1)}, bf16[512,1024]{1,0:T(8,128)(2,1)S(1)}, u32[]{:S(2)}) copy-start(bf16[512,1024]{1,0:T(8,128)(2,1)S(1)} %collective-permute-done.9) | copy-start | bytes 3145732
  233.8 60.8 %collective-permute-start.10 = (bf16[512,1024]{1,0:T(8,128)(2,1)}, bf16[512,1024]{1,0:T(8,128)(2,1)S(1)}, u32[]{:S(2)}, u32[]{:S(2)}) collective-permute-start(bf16[512,1024]{1,0:T(8,128)(2,1)} %get-tuple-element.217), channel_id=1, source_target_pairs={{2,0},{3,1},{6,4},{7,5},{10,8},{11,9},{14,12},{15,13},{18,16},{19,... | collective-permute-start | bytes 3145736 | tf_op jit(solution)/shard_map/ppermute | solution.py:1764
  256.1 103.6 %collective-permute-start.11 = (bf16[512,1024]{1,0:T(8,128)(2,1)}, bf16[512,1024]{1,0:T(8,128)(2,1)S(1)}, u32[]{:S(2)}, u32[]{:S(2)}) collective-permute-start(bf16[512,1024]{1,0:T(8,128)(2,1)} %get-tuple-element.235), channel_id=1, source_target_pairs={{2,0},{3,1},{6,4},{7,5},{10,8},{11,9},{14,12},{15,13},{18,16},{19,... | collective-permute-start | bytes 3145736 | tf_op jit(solution)/shard_map/ppermute | solution.py:1764
  257.4 4.9 copy-start.8
  294.6 1.0 copy-start.7
  359.7 1.0 copy-start.6
  408.2 12.3 %copy-start.5 = (f32[3,8,1024]{2,1,0:T(8,128)S(1)}, f32[3,8,1024]{2,1,0:T(8,128)}, u32[]{:S(2)}) copy-start(f32[3,8,1024]{2,1,0:T(8,128)} %get-tuple-element.277) | copy-start | bytes 294916
  408.2 13.2 %copy-start.14 = (f32[3,1,4096]{2,1,0:T(1,128)S(1)}, f32[3,1,4096]{2,1,0:T(1,128)}, u32[]{:S(2)}) copy-start(f32[3,1,4096]{2,1,0:T(1,128)} %get-tuple-element.279) | copy-start | bytes 147460
  590.2 10.3 %copy-start.3 = (f32[3,512,512]{2,1,0:T(8,128)S(1)}, f32[3,512,512]{2,1,0:T(8,128)}, u32[]{:S(2)}) copy-start(f32[3,512,512]{2,1,0:T(8,128)} %get-tuple-element.268) | copy-start | bytes 9437188
  598.7 4.8 copy-start.15
  598.7 5.5 copy-start.13
  600.5 4.7 copy-start.12
  600.5 5.6 copy-start.1

commit v5 on v4

--- a/solution.py
+++ b/solution.py
@@ -359,13 +359,13 @@
     kh_ref = vh_ref = dh_ref = diag_ref = None
     if halo_count:
         kh_ref, vh_ref = refs.pop(6).at[0], refs.pop(6).at[0]
-    dq_ref, dk_ref, dv_ref = refs[6:9]
+    dq_ref, dk_ref, dv_ref = [refs[6].at[part] for part in range(3)]
     if with_bias:
-        diag_ref = refs.pop(9)
+        diag_ref = refs.pop(7)
         diag_ref[...] = jnp.zeros_like(diag_ref)
     if halo_count:
-        dh_ref = refs.pop(9)
-    segk_ref, kp_ref, vp_ref, kt_ref, dk_acc, dv_acc = refs[9:]
+        dh_ref = refs.pop(7)
+    segk_ref, kp_ref, vp_ref, kt_ref, dk_acc, dv_acc = refs[7:]
     rows = q_ref.shape[1]
     pairs = q_ref.shape[2] // (2 * DH)
     first = lax.broadcasted_iota(jnp.int32, (QB, 2 * DH), 1) < DH
@@ -439,9 +439,8 @@
     if bias is not None:
         in_specs.append(pl.BlockSpec((pairs,) + bias.shape[1:], lambda g, s, t: (g, 0, 0)))
         inputs.append(bias)
-    plain_shape = jax.ShapeDtypeStruct((rows, width), LOW)
-    outputs = [plain_shape] * 3
-    out_specs = [plain] * 3
+    outputs = [jax.ShapeDtypeStruct((3, rows, width), LOW)]
+    out_specs = [pl.BlockSpec((3, rows, span), lambda g, s, t: (0, 0, g))]
     if bias is not None:
         outputs.append(slotted(bias.shape, F32))
         out_specs.append(pl.BlockSpec((1, pairs) + bias.shape[1:], lambda g, s, t: (s[1], g, 0, 0)))
@@ -451,7 +450,7 @@
         inputs += list(halo_kept)
         outputs.append(jax.ShapeDtypeStruct((2, halo_count, width), LOW))
         out_specs.append(pl.BlockSpec((2, halo_count, span), lambda g, s, t: (0, 0, lax.rem(g + groups // 2, groups))))
-    keep = None if previous is None else [None] * 3 + [previous] + [None] * (len(outputs) - 4)
+    keep = None if previous is None else [None, previous] + [None] * (len(outputs) - 2)
     return call_with_slots(
         functools.partial(attend_back_kernel, halo_count, bias is not None),
         [info, segments],
@@ -751,7 +750,7 @@
 
 def feed_back_steps(
     lead, got_refs, one_ref, two_ref, slope_ref, wo_own, wo_oth, up_own, up_oth, down_own, down_oth,
-    gain_ref, dy_ref, du_ref, db_ref, stat_ref, bias_ref, dz_ref, dc_ref, acc_ref, carry_ref, up_ref, down_ref, wo_ref, sem, wo_sem
+    gain_ref, dy_ref, du_ref, db_ref, stat_ref, bias_ref, dc_ref, acc_ref, carry_ref, up_ref, down_ref, wo_ref, sem, wo_sem
 ):
     j = pl.program_id(0)
     steps = 2 * up_own.shape[1] // up_ref.shape[2]
@@ -808,18 +807,17 @@
             stat_ref[0, 0:1, :] = gain
             stat_ref[0, 4:5, :] = sum_rows(grad)
             stat_ref[0, 2:3, :] = sum_rows(back)
-            dz_ref[...] = back
+            db_ref[0] = back.astype(LOW)
 
         @when(not lead)
         def _():
             back, gain = rms_norm_back(one_ref[0].astype(F32), acc_ref[...], gain_ref[1:2, :])
             stat_ref[0, 1:2, :] = gain
-            dz_ref[...] = carry_ref[...] + back
+            db_ref[0] = (carry_ref[...] + back).astype(LOW)
 
         for copy in wo_copies:
             copy.wait()
-        low = dz_ref[...].astype(LOW)
-        db_ref[0] = low
+        low = db_ref[0]
         dc_ref[:, :half] = dot_nt(low, wo_ref[0]).astype(LOW)
         dc_ref[:, half:] = dot_nt(low, wo_ref[1]).astype(LOW)
 
@@ -834,7 +832,7 @@
     fixed = lambda a: pl.BlockSpec(a.shape, lambda j, s: (0, 0))
     plain = pl.BlockSpec((rows, width), lambda j, s: (0, 0))
     moving = pl.BlockSpec((1, rows, chunk), lambda j, s: (s[1], 0, j))
-    keep = None if previous is None else list(previous) + [None, None]
+    keep = None if previous is None else list(previous) + [None]
     return call_with_slots(
         functools.partial(feed_back_kernel, lead),
         [info],
@@ -858,7 +856,6 @@
             slotted((rows, width), LOW),
             slotted((8, width), F32),
             slotted((1, 2 * hidden), F32),
-            jax.ShapeDtypeStruct((rows, width), F32),
             jax.ShapeDtypeStruct((rows, width), LOW),
         ],
         [
@@ -867,7 +864,6 @@
             kept,
             pl.BlockSpec((1, 8, width), lambda j, s: (s[1], 0, 0)),
             pl.BlockSpec((1, 1, chunk), lambda j, s: (s[1], 0, j)),
-            plain,
             plain,
         ],
         keep,
@@ -886,32 +882,27 @@
     )
 
 
-def enter_back_kernel(
-    lead, info, dq_ref, dk_ref, dv_ref, far_ref, x_ref, dz_ref, own_ref, oth_ref, gain_ref,
-    d_ref, stat_ref, lower_ref, upper_ref, low_ref, acc_ref
-):
+def enter_back_kernel(lead, info, d3_ref, far_ref, db_ref, *refs):
+    refs = list(refs)
+    x_ref = None if lead else refs.pop(0)
+    own_ref, oth_ref, gain_ref, d_ref, stat_ref, lower_ref, upper_ref, low_ref, acc_ref = refs
     m = pl.program_id(0)
     half = own_ref.shape[1]
     start = pl.ds(pl.multiple_of(info[4], QB), far_ref.shape[1])
+    d_ref[0] = d3_ref[0]
 
     @pl.when(m == 0)
     def _():
         stat_ref[...] = jnp.zeros_like(stat_ref)
         acc_ref[...] = jnp.zeros_like(acc_ref)
-        d_ref[0] = dq_ref[...]
-        stat_ref[0, 0:1, :] = sum_rows(dq_ref[...].astype(F32))
-
-    def with_far(block_ref, part):
-        d_ref[0] = block_ref[...]
-        d_ref[0, start, :] = (block_ref[start, :].astype(F32) + far_ref[part].astype(F32)).astype(LOW)
-
-    @pl.when(m == 1)
+        stat_ref[0, 0:1, :] = sum_rows(d_ref[0].astype(F32))
+
+    @pl.when(m > 0)
     def _():
-        with_far(dk_ref, 0)
+        d_ref[0, start, :] = (d3_ref[0, start, :].astype(F32) + far_ref[0].astype(F32)).astype(LOW)
 
     @pl.when(m == 2)
     def _():
-        with_far(dv_ref, 1)
         stat_ref[0, 1:2, :] = sum_rows(d_ref[0].astype(F32))
 
     acc_ref[...] += dot_nt(d_ref[0, :, :half], own_ref[...]) + dot_nt(d_ref[0, :, half:], oth_ref[...])
@@ -922,7 +913,7 @@
 
         @when(lead)
         def _():
-            total = dz_ref[...] + acc_ref[...]
+            total = db_ref[0].astype(F32) + acc_ref[...]
             low_ref[...] = total.astype(LOW)
             lower_ref[0] = total[:, :split]
             upper_ref[0] = total[:, split:].astype(LOW)
@@ -931,13 +922,13 @@
         def _():
             back, gain = rms_norm_back(x_ref[0].astype(F32), acc_ref[...], gain_ref[...])
             stat_ref[0, 2:3, :] = gain
-            total = dz_ref[...] + back
+            total = db_ref[0].astype(F32) + back
             low_ref[...] = total.astype(LOW)
             lower_ref[0] = total[:, :split]
             upper_ref[0] = total[:, split:].astype(LOW)
 
 
-def enter_back(lead, info, dq, dk, dv, far, x, dz, own, oth, gain, previous):
+def enter_back(lead, info, d3, far, db, x, own, oth, gain, previous):
     _, rows, width = x.shape
     half = own.shape[1] // 3
     plain = pl.BlockSpec((rows, width), lambda m, s: (0, 0))
@@ -947,14 +938,14 @@
     return call_with_slots(
         functools.partial(enter_back_kernel, lead),
         [info],
-        [dq, dk, dv, far, x, dz, own, oth, gain],
+        [d3, far, db] + ([] if lead else [x]) + [own, oth, gain],
         [
-            plain,
-            plain,
-            plain,
-            pl.BlockSpec(far.shape, lambda m, s: (0, 0, 0)),
+            pl.BlockSpec((1, rows, width), lambda m, s: (m, 0, 0)),
+            pl.BlockSpec((1,) + far.shape[1:], lambda m, s: (jnp.maximum(m - 1, 0), 0, 0)),
             kept,
-            plain,
+        ]
+        + ([] if lead else [kept])
+        + [
             weight,
             weight,
             pl.BlockSpec((1, width), lambda m, s: (0, 0)),
@@ -1241,9 +1232,10 @@
         grad_context, backward_grad_out_weight = fold_back(
             grad_branch.astype(jnp.bfloat16), out_weight, context
         )
-        low_q, low_k, low_v, grad_table = attend_back(
+        low_three, grad_table = attend_back(
             info, padded(backward_segment_row), qkv[None], None, grad_context.astype(jnp.bfloat16), bias, log_totals, None
         )
+        low_q, low_k, low_v = low_three
         grad_table = grad_table[0]
         grad_head = (
             jnp.stack([jnp.sum(low.astype(jnp.float32), axis=0) for low in (low_q, low_v)]) * weighting
@@ -1744,10 +1736,10 @@
             info, _ = lax.optimization_barrier((info, low if step < 3 else entry_kept[1]))
         lead_turn = turn == 0
         got, at = ([received[micro][None]], 0) if lead_turn else ([own_grads, remote_grads], micro)
-        *feed_kept, dz, grad_context = feed_back(
+        *feed_kept, grad_context = feed_back(
             lead_turn, info, got, at, one_saved, two_saved, slope_saved, wo, up, down, gains, feed_kept
         )
-        dq, dk, dv, *tables, far = attend_back(
+        d3, *tables, far = attend_back(
             info, segments[micro], qkv_saved, halo_saved, grad_context, None if lead_turn else bias, lse,
             None if lead_turn else table_kept,
         )
@@ -1757,7 +1749,7 @@
         if turn == 1 and micro == 0:
             info, *finished = lax.optimization_barrier((info, *finished))
         *entry_kept, low = enter_back(
-            lead_turn, info, dq, dk, dv, far, x_saved, dz, qkv_own, qkv_oth, entry_gain, entry_kept
+            lead_turn, info, d3, far, feed_kept[2], x_saved, qkv_own, qkv_oth, entry_gain, entry_kept
         )
         if turn == 1:
             received = list(received)

time: 616 us -> 611 us (level)
  Pallas kernels: 469 us -> 459 us
    pallas_call x24, Pallas kernels: 268 us -> 254 us  [call_with_slots(): pl.pallas_call(run, grid_spec=pltpu.PrefetchScalarGridSpec(num_scalar_pre...]
  transfers between devices with their start and end apart: 12 -> 12, of which waited for: 5 -> 5; matrix products, arithmetic and copies ran while one was open for 2% -> 2% of each run, Pallas kernels for 39% -> 38%
where the time goes in v5:
time: 611 us; the launch traced here: 599 us
  Pallas kernels  459 us (75%)
  waiting for transfers between devices  90.5 us (15%)
  local copies, waits for them, and re-layouts  25.3 us (4%)
  starting transfers between devices  12.8 us (2%)
  other arithmetic  9.04 us (1%)
    pallas_call x24, Pallas kernels, call_with_slots(): pl.pallas_call(run, grid_spec=pltpu.PrefetchScalarGridSpec(num_scalar_pre...  254 us
    pallas_call x1, Pallas kernels, summed_grads(): pl.pallas_call(grads_kernel, in_specs=[anywhere] * 9 + [local], out_specs...  168 us
    ppermute x2, waiting for transfers between devices, paired_body(): finished.append(lax.ppermute(result, 'section', [(1, 0)]))  47.6 us
    ppermute x2, waiting for transfers between devices, paired_body(): received[micro] = lax.ppermute(low, 'section', [(1, 0)])  32.5 us
    pallas_call x8, Pallas kernels, exchanged(): pl.pallas_call(exchange_kernel, in_specs=[pl.BlockSpec(memory_space=pl.AN...  27.9 us
  transfers between devices with their start and end apart: 12, of which 5 were waited for; matrix products, arithmetic and copies ran while one was open for 2% of the time, Pallas kernels for 38%

profile of v5, /device:TPU:0, one launch (start us, length us, event | category | flops | bytes accessed | tf_op | source)
XLA Modules:
  0.0 598.8 jit_solution(14535724951722257706)
XLA Ops:
  1.3 2.1 slice_bitcast_fusion.2
  6.1 1.9 collective-permute-done
  8.7 8.4 %collective-permute-done.1.refs_5_.refs_6_ = bf16[1024,1536]{1,0:T(8,128)(2,1)} collective-permute-done((bf16[1024,1536]{1,0:T(8,128)(2,1)S(1)}, bf16[1024,1536]{1,0:T(8,128)(2,1)}, u32[]{:S(2)}, u32[]{:S(2)}) %collective-permute-start.1) | collective-permute-done | bytes 3145760 | tf_op jit(solution)/shard_map/ppermute | solution.py:1623
  17.1 9.4 %enter.4 = (bf16[3,512,1024]{2,1,0:T(8,128)(2,1)}, bf16[3,512,1024]{2,1,0:T(8,128)(2,1)}, bf16[3,512,3072]{2,1,0:T(8,128)(2,1)}, bf16[2,256,1024]{2,1,0:T(8,128)(2,1)}) custom-call(s32[6]{0:T(128)} %stack.54.refs_0_, bf16[2,512,1024]{2,1,0:T(8,128)(2,1)} %bitcast.125, f32[1,1024]{1,0:T(1,128)} %slice_bitcast_fusion.6.refs_2_.refs_7_.refs_6_, ...), custom_call_target="tpu_custom_call" | custom-call | flops 450000000 | tf_op jit(solution)/shard_map/enter/pallas_call | solution.py:74
  26.6 3.0 exchange.8.refs_6_.refs_7_
  33.5 12.8 %attend.4 = (bf16[3,512,1024]{2,1,0:T(8,128)(2,1)}, f32[3,8,4,256]{3,2,1,0:T(4,128)}, bf16[3,256,1024]{2,1,0:T(8,128)(2,1)}, bf16[3,256,1024]{2,1,0:T(8,128)(2,1)}) custom-call(s32[6]{0:T(128)} %stack.54.refs_0_, s32[1280]{0:T(1024)} %get-tuple-element.286.refs_1_, s32[10,128]{1,0:T(8,128)} %bitcast.141, ...), custom_call_target="tpu_custom_call" | custom-call | flops 1200000000 | tf_op jit(solution)/shard_map/attend/pallas_call | solution.py:74
  46.4 21.3 %feed.4 = (bf16[3,512,4096]{2,1,0:T(8,128)(2,1)}, bf16[3,512,4096]{2,1,0:T(8,128)(2,1)}, bf16[3,512,1024]{2,1,0:T(8,128)(2,1)}, bf16[3,512,1024]{2,1,0:T(8,128)(...) custom-call(s32[6]{0:T(128)} %stack.54.refs_0_, ...), custom_call_target="tpu_custom_call" | custom-call | flops 1450000000 | tf_op jit(solution)/shard_map/feed/pallas_call | solution.py:74
  67.7 2.4 collective-permute-start.6
  70.1 9.4 %enter.5 = (bf16[3,512,1024]{2,1,0:T(8,128)(2,1)}, bf16[3,512,1024]{2,1,0:T(8,128)(2,1)}, bf16[3,512,3072]{2,1,0:T(8,128)(2,1)}, bf16[2,256,1024]{2,1,0:T(8,128)(2,1)}) custom-call(s32[6]{0:T(128)} %stack.52.refs_0_, bf16[2,512,1024]{2,1,0:T(8,128)(2,1)} %bitcast.126, ...), custom_call_target="tpu_custom_call", output_to_operand_aliasing={{0}: (6, {}), {1}: (7, {}), {2}: (8, {})} | custom-call | flops 450000000 | tf_op jit(solution)/shard_map/enter/pallas_call | solution.py:74
  79.5 4.7 exchange.9.refs_6_.refs_7_
  84.2 13.7 %attend.5 = (bf16[3,512,1024]{2,1,0:T(8,128)(2,1)}, f32[3,8,4,256]{3,2,1,0:T(4,128)}, bf16[3,256,1024]{2,1,0:T(8,128)(2,1)}, bf16[3,256,1024]{2,1,0:T(8,128)(2,1)}) custom-call(s32[6]{0:T(128)} %stack.52.refs_0_, s32[1280]{0:T(1024)} %get-tuple-element.285.refs_1_, ...), custom_call_target="tpu_custom_call", output_to_operand_aliasing={{0}: (8, {}), {1}: (9, {}), {2}: (10, {}), {3}: (11, {})} | custom-call | flops 1200000000 | tf_op jit(solution)/shard_map/attend/pallas_call | solution.py:74
  97.9 21.3 %feed.5 = (bf16[3,512,4096]{2,1,0:T(8,128)(2,1)}, bf16[3,512,4096]{2,1,0:T(8,128)(2,1)}, bf16[3,512,1024]{2,1,0:T(8,128)(2,1)}, bf16[3,512,1024]{2,1,0:T(8,128)(...) custom-call(s32[6]{0:T(128)} %stack.52.refs_0_, ...), custom_call_target="tpu_custom_call", output_to_operand_aliasing={{0}: (12, {}), {1}: (13, {}), {2}: (14, {}), {3}: (15, {}),... | custom-call | flops 1450000000 | tf_op jit(solution)/shard_map/feed/pallas_call | solution.py:74
  119.2 1.6 collective-permute-start.8
  123.1 5.1 toeplitz.1.refs_6_.refs_8_
  128.1 4.4 enter.6
  132.6 3.0 exchange.10.refs_7_.refs_8_
  135.6 4.1 attend.6
  139.7 5.6 feed.6
  145.4 1.7 collective-permute-start.7
  148.1 4.4 enter.7
  152.5 3.0 exchange.11.refs_7_.refs_8_
  155.5 4.1 attend.7
  159.6 5.6 feed.7
  166.7 5.3 feed_back.4
  172.1 5.5 attend_back.4
  177.6 3.0 exchange.12.refs_2_
  180.7 47.6 %collective-permute-done.9 = bf16[512,1024]{1,0:T(8,128)(2,1)S(1)} collective-permute-done((bf16[512,1024]{1,0:T(8,128)(2,1)}, bf16[512,1024]{1,0:T(8,128)(2,1)S(1)}, u32[]{:S(2)}, u32[]{:S(2)}) %collective-permute-start.9) | collective-permute-done | bytes 1048608 | tf_op jit(solution)/shard_map/ppermute | solution.py:1726
  228.3 5.5 enter_back.4
  235.1 5.3 feed_back.5
  240.4 5.5 attend_back.5
  245.9 3.0 exchange.13.refs_2_
  248.9 5.7 enter_back.5
  255.8 3.8 diagonals.1
  260.7 3.6 maximum_select_fusion
  264.3 28.1 %collective-permute-done.10 = bf16[512,1024]{1,0:T(8,128)(2,1)S(1)} collective-permute-done((bf16[512,1024]{1,0:T(8,128)(2,1)}, bf16[512,1024]{1,0:T(8,128)(2,1)S(1)}, u32[]{:S(2)}, u32[]{:S(2)}) %collective-permute-start.10) | collective-permute-done | bytes 1048608 | tf_op jit(solution)/shard_map/ppermute | solution.py:1756
  293.4 20.6 %feed_back.6 = (bf16[3,512,1024]{2,1,0:T(8,128)(2,1)}, bf16[3,512,4096]{2,1,0:T(8,128)(2,1)}, bf16[3,512,1024]{2,1,0:T(8,128)(2,1)}, f32[3,8,1024]{2,1,0:T(8,128...) custom-call(s32[6]{0:T(128)} %stack.54.refs_0_, ...), custom_call_target="tpu_custom_call", output_to_operand_aliasing={{0}: (12, {}), {1}: (13, {}), {2}: (14, {}), {3}: (15, {}),... | custom-call | flops 1350000000 | tf_op jit(solution)/shard_map/feed_back/pallas_call | solution.py:74
  314.0 20.2 %attend_back.6 = (bf16[3,512,1024]{2,1,0:T(8,128)(2,1)}, bf16[2,256,1024]{2,1,0:T(8,128)(2,1)}) custom-call(s32[6]{0:T(128)} %stack.54.refs_0_, s32[1280]{0:T(1024)} %get-tuple-element.286.refs_1_, s32[10,128]{1,0:T(8,128)} %bitcast.144, bf16[3,512,3072]{2,1,0:T(8,128)(2,1)} %get-tuple-element.177.refs_3_.refs_4_.refs_5_, ...), custom_call_target="tpu_custom_call" | custom-call | flops 1300000000 | tf_op jit(solution)/shard_map/attend_back/pallas_call | solution.py:74
  334.2 5.1 exchange.14.refs_2_
  339.3 11.0 %enter_back.6 = (bf16[3,512,3072]{2,1,0:T(8,128)(2,1)}, f32[3,8,1024]{2,1,0:T(8,128)}, f32[3,512,512]{2,1,0:T(8,128)}, bf16[3,512,512]{2,1,0:T(8,128)(2,1)}, bf16[512,1024]{1,0:T(8,128)(2,1)}) custom-call(s32[6]{0:T(128)} %stack.54.refs_0_, ...), custom_call_target="tpu_custom_call", output_to_operand_aliasing={{0}: (7, {}), {1}: (8, {}), {2}: (9, {}), {3}: (10, {})} | custom-call | flops 600000000 | tf_op jit(solution)/shard_map/enter_back/pallas_call | solution.py:74
  350.3 4.5 collective-permute-done.11
  355.7 20.8 %feed_back.7 = (bf16[3,512,1024]{2,1,0:T(8,128)(2,1)}, bf16[3,512,4096]{2,1,0:T(8,128)(2,1)}, bf16[3,512,1024]{2,1,0:T(8,128)(2,1)}, f32[3,8,1024]{2,1,0:T(8,128...) custom-call(s32[6]{0:T(128)} %stack.52.refs_0_, ...), custom_call_target="tpu_custom_call", output_to_operand_aliasing={{0}: (12, {}), {1}: (13, {}), {2}: (14, {}), {3}: (15, {}),... | custom-call | flops 1350000000 | tf_op jit(solution)/shard_map/feed_back/pallas_call | solution.py:74
  376.6 21.4 %attend_back.7 = (bf16[3,512,1024]{2,1,0:T(8,128)(2,1)}, bf16[2,256,1024]{2,1,0:T(8,128)(2,1)}) custom-call(s32[6]{0:T(128)} %stack.52.refs_0_, s32[1280]{0:T(1024)} %get-tuple-element.285.refs_1_, s32[10,128]{1,0:T(8,128)} %bitcast.140, bf16[3,512,3072]{2,1,0:T(8,128)(2,1)} %get-tuple-element.177.refs_3_.refs_4_.refs_5_, ...), custom_call_target="tpu_custom_call" | custom-call | flops 1300000000 | tf_op jit(solution)/shard_map/attend_back/pallas_call | solution.py:74
  398.0 3.0 exchange.15.refs_2_
  401.0 11.3 %enter_back.7 = (bf16[3,512,3072]{2,1,0:T(8,128)(2,1)}, f32[3,8,1024]{2,1,0:T(8,128)}, f32[3,512,512]{2,1,0:T(8,128)}, bf16[3,512,512]{2,1,0:T(8,128)(2,1)}, bf16[512,1024]{1,0:T(8,128)(2,1)}) custom-call(s32[6]{0:T(128)} %stack.52.refs_0_, ...), custom_call_target="tpu_custom_call", output_to_operand_aliasing={{0}: (7, {}), {1}: (8, {}), {2}: (9, {}), {3}: (10, {})} | custom-call | flops 600000000 | tf_op jit(solution)/shard_map/enter_back/pallas_call | solution.py:74
  414.5 167.9 %summed_grads.1 = (f32[2048,128]{1,0:T(8,128)}, f32[128,2048]{1,0:T(8,128)}, f32[512,128]{1,0:T(8,128)}, f32[128,1536]{1,0:T(8,128)}, f32[16,1024]{1,0:T(8,128)}, /*index=5*/bf16[2,512,512]{2,1,0:T(8,128)(2,1)}) custom-call(bf16[3,512,4096]{2,1,0:T(8,128)(2,1)} %get-tuple-element.246.f_hbm, bf16[3,512,1024]{2,1,0:T(8,128)(2,1)} %get-tuple-element.247.dy_hbm, ...), custom_call_target="tpu_custom_call" | custom-call | flops 249999998976 | tf_op jit(solution)/shard_map/summed_grads/pallas_call | solution.py:1574
  585.7 2.3 copy.98
  587.9 2.3 copy.100
  592.7 3.0 select_bitcast_fusion
  (127 shorter events, 28.6 us)
Async XLA Ops:
  0.6 31.0 %copy-start = (s32[2,1,1024]{2,1,0:T(1,128)S(1)}, s32[2,1,1024]{2,1,0:T(1,128)}, u32[]{:S(2)}) copy-start(s32[2,1,1024]{2,1,0:T(1,128)} %param.14) | copy-start | bytes 24580
  0.7 45.7 %collective-permute-start.3 = (bf16[1024,2048]{1,0:T(8,128)(2,1)}, bf16[1024,2048]{1,0:T(8,128)(2,1)}, u32[]{:S(2)}, u32[]{:S(2)}) collective-permute-start(bf16[1024,2048]{1,0:T(8,128)(2,1)} %bitcast.95), channel_id=1, source_target_pairs={{0,1},{1,0},{2,3},{3,2},{4,5},{5,4},{6,7},{7,6},{8,9},{9,8},{10,11... | collective-permute-start | bytes 12582920 | tf_op jit(solution)/shard_map/ppermute | solution.py:1623
  1.2 45.2 %collective-permute-start.4 = (bf16[2048,1024]{1,0:T(8,128)(2,1)}, bf16[2048,1024]{1,0:T(8,128)(2,1)}, u32[]{:S(2)}, u32[]{:S(2)}) collective-permute-start(bf16[2048,1024]{1,0:T(8,128)(2,1)} %bitcast.104), channel_id=1, source_target_pairs={{0,1},{1,0},{2,3},{3,2},{4,5},{5,4},{6,7},{7,6},{8,9},{9,8},{10,11... | collective-permute-start | bytes 12582920 | tf_op jit(solution)/shard_map/ppermute | solution.py:1623
  3.3 0.8 copy-start.19
  3.3 0.8 copy-start.18
  3.3 0.9 copy-start.17
  3.4 1.5 copy-start.16
  3.6 13.5 %copy-start.2 = (bf16[1024,1536]{1,0:T(8,128)(2,1)}, bf16[1024,1536]{1,0:T(8,128)(2,1)S(1)}, u32[]{:S(2)}) copy-start(bf16[1024,1536]{1,0:T(8,128)(2,1)S(1)} %pad_maximum_fusion.refs_4_.refs_5_) | copy-start | bytes 9437188
  3.6 13.5 %collective-permute-start.1 = (bf16[1024,1536]{1,0:T(8,128)(2,1)S(1)}, bf16[1024,1536]{1,0:T(8,128)(2,1)}, u32[]{:S(2)}, u32[]{:S(2)}) collective-permute-start(bf16[1024,1536]{1,0:T(8,128)(2,1)S(1)} %pad_maximum_fusion.refs_4_.refs_5_), channel_id=1, source_target_pairs={{0,1},{1,0},{2,3},{3,2},{4,5},{5,4},{6,7},{7,6},{8,9},{9,8},{10,11... | collective-permute-start | bytes 9437192 | tf_op jit(solution)/shard_map/ppermute | solution.py:1623
  4.2 3.8 collective-permute-start
  4.6 41.7 %collective-permute-start.2 = (bf16[512,1024]{1,0:T(8,128)(2,1)}, bf16[512,1024]{1,0:T(8,128)(2,1)}, u32[]{:S(2)}, u32[]{:S(2)}) collective-permute-start(bf16[512,1024]{1,0:T(8,128)(2,1)} %bitcast.113), channel_id=1, source_target_pairs={{0,1},{1,0},{2,3},{3,2},{4,5},{5,4},{6,7},{7,6},{8,9},{9,8},{10,11... | collective-permute-start | bytes 3145736 | tf_op jit(solution)/shard_map/ppermute | solution.py:1623
  29.6 98.6 %collective-permute-start.5 = (bf16[2,512,1024]{2,1,0:T(8,128)(2,1)}, bf16[2,512,1024]{2,1,0:T(8,128)(2,1)S(1)}, u32[]{:S(2)}, u32[]{:S(2)}) collective-permute-start(bf16[2,512,1024]{2,1,0:T(8,128)(2,1)} %bitcast.122), channel_id=1, source_target_pairs={{0,2},{1,3},{4,6},{5,7},{8,10},{9,11},{12,14},{13,15},{16,18},{17,... | collective-permute-start | bytes 6291464 | tf_op jit(solution)/shard_map/ppermute | solution.py:1714
  67.7 60.5 %collective-permute-start.6 = (bf16[512,1024]{1,0:T(8,128)(2,1)}, bf16[512,1024]{1,0:T(8,128)(2,1)}, u32[]{:S(2)}, u32[]{:S(2)}) collective-permute-start(bf16[512,1024]{1,0:T(8,128)(2,1)} %get-tuple-element.141), channel_id=1, source_target_pairs={{0,2},{1,3},{4,6},{5,7},{8,10},{9,11},{12,14},{13,15},{16,18},{17,... | collective-permute-start | bytes 3145736 | tf_op jit(solution)/shard_map/ppermute | solution.py:1723
  97.9 22.9 %copy-start.20 = (s32[2047]{0:T(1024)S(1)}, s32[2047]{0:T(1024)}, u32[]{:S(2)}) copy-start(s32[2047]{0:T(1024)} %param.15) | copy-start | bytes 24568
  119.2 27.9 %collective-permute-start.8 = (bf16[512,1024]{1,0:T(8,128)(2,1)}, bf16[512,1024]{1,0:T(8,128)(2,1)S(1)}, u32[]{:S(2)}, u32[]{:S(2)}) collective-permute-start(bf16[512,1024]{1,0:T(8,128)(2,1)} %get-tuple-element.156), channel_id=1, source_target_pairs={{0,2},{1,3},{4,6},{5,7},{8,10},{9,11},{12,14},{13,15},{16,18},{17,... | collective-permute-start | bytes 3145736 | tf_op jit(solution)/shard_map/ppermute | solution.py:1723
  128.1 4.5 copy-start.4
  145.4 35.3 %collective-permute-start.7 = (bf16[512,1024]{1,0:T(8,128)(2,1)}, bf16[512,1024]{1,0:T(8,128)(2,1)S(1)}, u32[]{:S(2)}, u32[]{:S(2)}) collective-permute-start(bf16[512,1024]{1,0:T(8,128)(2,1)} %get-tuple-element.173), channel_id=1, source_target_pairs={{2,0},{3,1},{6,4},{7,5},{10,8},{11,9},{14,12},{15,13},{18,16},{19,... | collective-permute-start | bytes 3145736 | tf_op jit(solution)/shard_map/ppermute | solution.py:1726
  147.1 1.0 copy-start.11
  165.3 63.0 %collective-permute-start.9 = (bf16[512,1024]{1,0:T(8,128)(2,1)}, bf16[512,1024]{1,0:T(8,128)(2,1)S(1)}, u32[]{:S(2)}, u32[]{:S(2)}) collective-permute-start(bf16[512,1024]{1,0:T(8,128)(2,1)} %get-tuple-element.188), channel_id=1, source_target_pairs={{2,0},{3,1},{6,4},{7,5},{10,8},{11,9},{14,12},{15,13},{18,16},{19,... | collective-permute-start | bytes 3145736 | tf_op jit(solution)/shard_map/ppermute | solution.py:1726
  180.6 53.1 %copy-start.9 = (bf16[512,1024]{1,0:T(8,128)(2,1)}, bf16[512,1024]{1,0:T(8,128)(2,1)S(1)}, u32[]{:S(2)}) copy-start(bf16[512,1024]{1,0:T(8,128)(2,1)S(1)} %collective-permute-done.7) | copy-start | bytes 3145732
  228.3 5.5 copy-start.10
  233.8 58.6 %collective-permute-start.10 = (bf16[512,1024]{1,0:T(8,128)(2,1)}, bf16[512,1024]{1,0:T(8,128)(2,1)S(1)}, u32[]{:S(2)}, u32[]{:S(2)}) collective-permute-start(bf16[512,1024]{1,0:T(8,128)(2,1)} %get-tuple-element.203), channel_id=1, source_target_pairs={{2,0},{3,1},{6,4},{7,5},{10,8},{11,9},{14,12},{15,13},{18,16},{19,... | collective-permute-start | bytes 3145736 | tf_op jit(solution)/shard_map/ppermute | solution.py:1756
  254.5 100.2 %collective-permute-start.11 = (bf16[512,1024]{1,0:T(8,128)(2,1)}, bf16[512,1024]{1,0:T(8,128)(2,1)S(1)}, u32[]{:S(2)}, u32[]{:S(2)}) collective-permute-start(bf16[512,1024]{1,0:T(8,128)(2,1)} %get-tuple-element.218), channel_id=1, source_target_pairs={{2,0},{3,1},{6,4},{7,5},{10,8},{11,9},{14,12},{15,13},{18,16},{19,... | collective-permute-start | bytes 3145736 | tf_op jit(solution)/shard_map/ppermute | solution.py:1756
  255.8 4.9 copy-start.8
  292.4 1.0 copy-start.7
  354.8 1.0 copy-start.6
  401.0 11.4 %copy-start.5 = (f32[3,8,1024]{2,1,0:T(8,128)S(1)}, f32[3,8,1024]{2,1,0:T(8,128)}, u32[]{:S(2)}) copy-start(f32[3,8,1024]{2,1,0:T(8,128)} %get-tuple-element.253) | copy-start | bytes 294916
  401.0 12.3 %copy-start.14 = (f32[3,1,4096]{2,1,0:T(1,128)S(1)}, f32[3,1,4096]{2,1,0:T(1,128)}, u32[]{:S(2)}) copy-start(f32[3,1,4096]{2,1,0:T(1,128)} %get-tuple-element.255) | copy-start | bytes 147460
  582.4 10.3 %copy-start.3 = (f32[3,512,512]{2,1,0:T(8,128)S(1)}, f32[3,512,512]{2,1,0:T(8,128)}, u32[]{:S(2)}) copy-start(f32[3,512,512]{2,1,0:T(8,128)} %get-tuple-element.245) | copy-start | bytes 9437188
  590.9 4.8 copy-start.15
  590.9 5.5 copy-start.13
  592.7 4.7 copy-start.12
  592.7 5.6 copy-start.1

commit v6 on v5

--- a/solution.py
+++ b/solution.py
@@ -1511,9 +1511,7 @@
             near_copy(k, slot).start()
             product(0, to_held)
 
-            @pl.when(k >= 1)
-            def _():
-                near_stage(k - 1)
+            near_stage(k)
 
             for s in range(len(peers)):
 
@@ -1529,7 +1527,6 @@
             still_copy(p + 2).start()
         base += count
 
-    near_stage(total - 1)
     early = (total - 1 - 5) // 3 + 1
     @pl.loop(0, early)
     def _(k):

time: 611 us -> 621 us (1.016)
  Pallas kernels: 459 us -> 472 us
    pallas_call x1, Pallas kernels: 168 us -> 181 us  [summed_grads(): pl.pallas_call(grads_kernel, in_specs=[anywhere] * 9 + [local], out_specs...]
  transfers between devices with their start and end apart: 12 -> 12, of which waited for: 5 -> 5; matrix products, arithmetic and copies ran while one was open for 2% -> 2% of each run, Pallas kernels for 38% -> 37%
where the time goes in v6:
time: 621 us; the launch traced here: 611 us
  Pallas kernels  472 us (76%)
  waiting for transfers between devices  90.5 us (15%)
  local copies, waits for them, and re-layouts  25.3 us (4%)
  starting transfers between devices  12.8 us (2%)
  other arithmetic  9.04 us (1%)
    pallas_call x24, Pallas kernels, call_with_slots(): pl.pallas_call(run, grid_spec=pltpu.PrefetchScalarGridSpec(num_scalar_pre...  254 us
    pallas_call x1, Pallas kernels, summed_grads(): pl.pallas_call(grads_kernel, in_specs=[anywhere] * 9 + [local], out_specs...  181 us
    ppermute x2, waiting for transfers between devices, paired_body(): finished.append(lax.ppermute(result, 'section', [(1, 0)]))  47.6 us
    ppermute x2, waiting for transfers between devices, paired_body(): received[micro] = lax.ppermute(low, 'section', [(1, 0)])  32.5 us
    pallas_call x8, Pallas kernels, exchanged(): pl.pallas_call(exchange_kernel, in_specs=[pl.BlockSpec(memory_space=pl.AN...  27.9 us
  transfers between devices with their start and end apart: 12, of which 5 were waited for; matrix products, arithmetic and copies ran while one was open for 2% of the time, Pallas kernels for 37%

profile of v6, /device:TPU:0, one launch (start us, length us, event | category | flops | bytes accessed | tf_op | source)
XLA Modules:
  0.0 611.4 jit_solution(3893262684416986647)
XLA Ops:
  1.3 2.1 slice_bitcast_fusion.2
  6.1 1.9 collective-permute-done
  8.7 8.4 %collective-permute-done.1.refs_5_.refs_6_ = bf16[1024,1536]{1,0:T(8,128)(2,1)} collective-permute-done((bf16[1024,1536]{1,0:T(8,128)(2,1)S(1)}, bf16[1024,1536]{1,0:T(8,128)(2,1)}, u32[]{:S(2)}, u32[]{:S(2)}) %collective-permute-start.1) | collective-permute-done | bytes 3145760 | tf_op jit(solution)/shard_map/ppermute | solution.py:1620
  17.1 9.4 %enter.4 = (bf16[3,512,1024]{2,1,0:T(8,128)(2,1)}, bf16[3,512,1024]{2,1,0:T(8,128)(2,1)}, bf16[3,512,3072]{2,1,0:T(8,128)(2,1)}, bf16[2,256,1024]{2,1,0:T(8,128)(2,1)}) custom-call(s32[6]{0:T(128)} %stack.54.refs_0_, bf16[2,512,1024]{2,1,0:T(8,128)(2,1)} %bitcast.125, f32[1,1024]{1,0:T(1,128)} %slice_bitcast_fusion.6.refs_2_.refs_7_.refs_6_, ...), custom_call_target="tpu_custom_call" | custom-call | flops 450000000 | tf_op jit(solution)/shard_map/enter/pallas_call | solution.py:74
  26.6 3.0 exchange.8.refs_6_.refs_7_
  33.5 12.8 %attend.4 = (bf16[3,512,1024]{2,1,0:T(8,128)(2,1)}, f32[3,8,4,256]{3,2,1,0:T(4,128)}, bf16[3,256,1024]{2,1,0:T(8,128)(2,1)}, bf16[3,256,1024]{2,1,0:T(8,128)(2,1)}) custom-call(s32[6]{0:T(128)} %stack.54.refs_0_, s32[1280]{0:T(1024)} %get-tuple-element.286.refs_1_, s32[10,128]{1,0:T(8,128)} %bitcast.141, ...), custom_call_target="tpu_custom_call" | custom-call | flops 1200000000 | tf_op jit(solution)/shard_map/attend/pallas_call | solution.py:74
  46.4 21.3 %feed.4 = (bf16[3,512,4096]{2,1,0:T(8,128)(2,1)}, bf16[3,512,4096]{2,1,0:T(8,128)(2,1)}, bf16[3,512,1024]{2,1,0:T(8,128)(2,1)}, bf16[3,512,1024]{2,1,0:T(8,128)(...) custom-call(s32[6]{0:T(128)} %stack.54.refs_0_, ...), custom_call_target="tpu_custom_call" | custom-call | flops 1450000000 | tf_op jit(solution)/shard_map/feed/pallas_call | solution.py:74
  67.7 2.4 collective-permute-start.6
  70.1 9.4 %enter.5 = (bf16[3,512,1024]{2,1,0:T(8,128)(2,1)}, bf16[3,512,1024]{2,1,0:T(8,128)(2,1)}, bf16[3,512,3072]{2,1,0:T(8,128)(2,1)}, bf16[2,256,1024]{2,1,0:T(8,128)(2,1)}) custom-call(s32[6]{0:T(128)} %stack.52.refs_0_, bf16[2,512,1024]{2,1,0:T(8,128)(2,1)} %bitcast.126, ...), custom_call_target="tpu_custom_call", output_to_operand_aliasing={{0}: (6, {}), {1}: (7, {}), {2}: (8, {})} | custom-call | flops 450000000 | tf_op jit(solution)/shard_map/enter/pallas_call | solution.py:74
  79.5 4.7 exchange.9.refs_6_.refs_7_
  84.2 13.6 %attend.5 = (bf16[3,512,1024]{2,1,0:T(8,128)(2,1)}, f32[3,8,4,256]{3,2,1,0:T(4,128)}, bf16[3,256,1024]{2,1,0:T(8,128)(2,1)}, bf16[3,256,1024]{2,1,0:T(8,128)(2,1)}) custom-call(s32[6]{0:T(128)} %stack.52.refs_0_, s32[1280]{0:T(1024)} %get-tuple-element.285.refs_1_, ...), custom_call_target="tpu_custom_call", output_to_operand_aliasing={{0}: (8, {}), {1}: (9, {}), {2}: (10, {}), {3}: (11, {})} | custom-call | flops 1200000000 | tf_op jit(solution)/shard_map/attend/pallas_call | solution.py:74
  97.8 21.3 %feed.5 = (bf16[3,512,4096]{2,1,0:T(8,128)(2,1)}, bf16[3,512,4096]{2,1,0:T(8,128)(2,1)}, bf16[3,512,1024]{2,1,0:T(8,128)(2,1)}, bf16[3,512,1024]{2,1,0:T(8,128)(...) custom-call(s32[6]{0:T(128)} %stack.52.refs_0_, ...), custom_call_target="tpu_custom_call", output_to_operand_aliasing={{0}: (12, {}), {1}: (13, {}), {2}: (14, {}), {3}: (15, {}),... | custom-call | flops 1450000000 | tf_op jit(solution)/shard_map/feed/pallas_call | solution.py:74
  119.1 1.6 collective-permute-start.8
  123.0 5.1 toeplitz.1.refs_6_.refs_8_
  128.1 4.4 enter.6
  132.5 3.0 exchange.10.refs_7_.refs_8_
  135.6 4.1 attend.6
  139.7 5.6 feed.6
  145.3 1.7 collective-permute-start.7
  148.0 4.4 enter.7
  152.4 3.0 exchange.11.refs_7_.refs_8_
  155.4 4.1 attend.7
  159.6 5.6 feed.7
  166.7 5.3 feed_back.4
  172.0 5.5 attend_back.4
  177.5 3.0 exchange.12.refs_2_
  180.6 47.6 %collective-permute-done.9 = bf16[512,1024]{1,0:T(8,128)(2,1)S(1)} collective-permute-done((bf16[512,1024]{1,0:T(8,128)(2,1)}, bf16[512,1024]{1,0:T(8,128)(2,1)S(1)}, u32[]{:S(2)}, u32[]{:S(2)}) %collective-permute-start.9) | collective-permute-done | bytes 1048608 | tf_op jit(solution)/shard_map/ppermute | solution.py:1723
  228.2 5.5 enter_back.4
  235.0 5.3 feed_back.5
  240.3 5.5 attend_back.5
  245.8 3.0 exchange.13.refs_2_
  248.8 5.7 enter_back.5
  255.8 3.8 diagonals.1
  260.7 3.6 maximum_select_fusion
  264.3 28.0 %collective-permute-done.10 = bf16[512,1024]{1,0:T(8,128)(2,1)S(1)} collective-permute-done((bf16[512,1024]{1,0:T(8,128)(2,1)}, bf16[512,1024]{1,0:T(8,128)(2,1)S(1)}, u32[]{:S(2)}, u32[]{:S(2)}) %collective-permute-start.10) | collective-permute-done | bytes 1048608 | tf_op jit(solution)/shard_map/ppermute | solution.py:1753
  293.3 20.6 %feed_back.6 = (bf16[3,512,1024]{2,1,0:T(8,128)(2,1)}, bf16[3,512,4096]{2,1,0:T(8,128)(2,1)}, bf16[3,512,1024]{2,1,0:T(8,128)(2,1)}, f32[3,8,1024]{2,1,0:T(8,128...) custom-call(s32[6]{0:T(128)} %stack.54.refs_0_, ...), custom_call_target="tpu_custom_call", output_to_operand_aliasing={{0}: (12, {}), {1}: (13, {}), {2}: (14, {}), {3}: (15, {}),... | custom-call | flops 1350000000 | tf_op jit(solution)/shard_map/feed_back/pallas_call | solution.py:74
  313.9 20.2 %attend_back.6 = (bf16[3,512,1024]{2,1,0:T(8,128)(2,1)}, bf16[2,256,1024]{2,1,0:T(8,128)(2,1)}) custom-call(s32[6]{0:T(128)} %stack.54.refs_0_, s32[1280]{0:T(1024)} %get-tuple-element.286.refs_1_, s32[10,128]{1,0:T(8,128)} %bitcast.144, bf16[3,512,3072]{2,1,0:T(8,128)(2,1)} %get-tuple-element.177.refs_3_.refs_4_.refs_5_, ...), custom_call_target="tpu_custom_call" | custom-call | flops 1300000000 | tf_op jit(solution)/shard_map/attend_back/pallas_call | solution.py:74
  334.2 5.1 exchange.14.refs_2_
  339.3 11.0 %enter_back.6 = (bf16[3,512,3072]{2,1,0:T(8,128)(2,1)}, f32[3,8,1024]{2,1,0:T(8,128)}, f32[3,512,512]{2,1,0:T(8,128)}, bf16[3,512,512]{2,1,0:T(8,128)(2,1)}, bf16[512,1024]{1,0:T(8,128)(2,1)}) custom-call(s32[6]{0:T(128)} %stack.54.refs_0_, ...), custom_call_target="tpu_custom_call", output_to_operand_aliasing={{0}: (7, {}), {1}: (8, {}), {2}: (9, {}), {3}: (10, {})} | custom-call | flops 600000000 | tf_op jit(solution)/shard_map/enter_back/pallas_call | solution.py:74
  350.2 4.5 collective-permute-done.11
  355.7 20.8 %feed_back.7 = (bf16[3,512,1024]{2,1,0:T(8,128)(2,1)}, bf16[3,512,4096]{2,1,0:T(8,128)(2,1)}, bf16[3,512,1024]{2,1,0:T(8,128)(2,1)}, f32[3,8,1024]{2,1,0:T(8,128...) custom-call(s32[6]{0:T(128)} %stack.52.refs_0_, ...), custom_call_target="tpu_custom_call", output_to_operand_aliasing={{0}: (12, {}), {1}: (13, {}), {2}: (14, {}), {3}: (15, {}),... | custom-call | flops 1350000000 | tf_op jit(solution)/shard_map/feed_back/pallas_call | solution.py:74
  376.5 21.4 %attend_back.7 = (bf16[3,512,1024]{2,1,0:T(8,128)(2,1)}, bf16[2,256,1024]{2,1,0:T(8,128)(2,1)}) custom-call(s32[6]{0:T(128)} %stack.52.refs_0_, s32[1280]{0:T(1024)} %get-tuple-element.285.refs_1_, s32[10,128]{1,0:T(8,128)} %bitcast.140, bf16[3,512,3072]{2,1,0:T(8,128)(2,1)} %get-tuple-element.177.refs_3_.refs_4_.refs_5_, ...), custom_call_target="tpu_custom_call" | custom-call | flops 1300000000 | tf_op jit(solution)/shard_map/attend_back/pallas_call | solution.py:74
  397.9 3.0 exchange.15.refs_2_
  400.9 11.3 %enter_back.7 = (bf16[3,512,3072]{2,1,0:T(8,128)(2,1)}, f32[3,8,1024]{2,1,0:T(8,128)}, f32[3,512,512]{2,1,0:T(8,128)}, bf16[3,512,512]{2,1,0:T(8,128)(2,1)}, bf16[512,1024]{1,0:T(8,128)(2,1)}) custom-call(s32[6]{0:T(128)} %stack.52.refs_0_, ...), custom_call_target="tpu_custom_call", output_to_operand_aliasing={{0}: (7, {}), {1}: (8, {}), {2}: (9, {}), {3}: (10, {})} | custom-call | flops 600000000 | tf_op jit(solution)/shard_map/enter_back/pallas_call | solution.py:74
  414.5 180.5 %summed_grads.1 = (f32[2048,128]{1,0:T(8,128)}, f32[128,2048]{1,0:T(8,128)}, f32[512,128]{1,0:T(8,128)}, f32[128,1536]{1,0:T(8,128)}, f32[16,1024]{1,0:T(8,128)}, /*index=5*/bf16[2,512,512]{2,1,0:T(8,128)(2,1)}) custom-call(bf16[3,512,4096]{2,1,0:T(8,128)(2,1)} %get-tuple-element.246.f_hbm, bf16[3,512,1024]{2,1,0:T(8,128)(2,1)} %get-tuple-element.247.dy_hbm, ...), custom_call_target="tpu_custom_call" | custom-call | flops 249999998976 | tf_op jit(solution)/shard_map/summed_grads/pallas_call | solution.py:1571
  598.3 2.3 copy.98
  600.6 2.3 copy.100
  605.3 3.0 select_bitcast_fusion
  (127 shorter events, 28.6 us)
Async XLA Ops:
  0.6 31.0 %copy-start = (s32[2,1,1024]{2,1,0:T(1,128)S(1)}, s32[2,1,1024]{2,1,0:T(1,128)}, u32[]{:S(2)}) copy-start(s32[2,1,1024]{2,1,0:T(1,128)} %param.14) | copy-start | bytes 24580
  0.7 45.7 %collective-permute-start.3 = (bf16[1024,2048]{1,0:T(8,128)(2,1)}, bf16[1024,2048]{1,0:T(8,128)(2,1)}, u32[]{:S(2)}, u32[]{:S(2)}) collective-permute-start(bf16[1024,2048]{1,0:T(8,128)(2,1)} %bitcast.95), channel_id=1, source_target_pairs={{0,1},{1,0},{2,3},{3,2},{4,5},{5,4},{6,7},{7,6},{8,9},{9,8},{10,11... | collective-permute-start | bytes 12582920 | tf_op jit(solution)/shard_map/ppermute | solution.py:1620
  1.2 45.2 %collective-permute-start.4 = (bf16[2048,1024]{1,0:T(8,128)(2,1)}, bf16[2048,1024]{1,0:T(8,128)(2,1)}, u32[]{:S(2)}, u32[]{:S(2)}) collective-permute-start(bf16[2048,1024]{1,0:T(8,128)(2,1)} %bitcast.104), channel_id=1, source_target_pairs={{0,1},{1,0},{2,3},{3,2},{4,5},{5,4},{6,7},{7,6},{8,9},{9,8},{10,11... | collective-permute-start | bytes 12582920 | tf_op jit(solution)/shard_map/ppermute | solution.py:1620
  3.3 0.8 copy-start.19
  3.3 0.8 copy-start.18
  3.3 0.9 copy-start.17
  3.4 1.5 copy-start.16
  3.6 13.5 %copy-start.2 = (bf16[1024,1536]{1,0:T(8,128)(2,1)}, bf16[1024,1536]{1,0:T(8,128)(2,1)S(1)}, u32[]{:S(2)}) copy-start(bf16[1024,1536]{1,0:T(8,128)(2,1)S(1)} %pad_maximum_fusion.refs_4_.refs_5_) | copy-start | bytes 9437188
  3.6 13.5 %collective-permute-start.1 = (bf16[1024,1536]{1,0:T(8,128)(2,1)S(1)}, bf16[1024,1536]{1,0:T(8,128)(2,1)}, u32[]{:S(2)}, u32[]{:S(2)}) collective-permute-start(bf16[1024,1536]{1,0:T(8,128)(2,1)S(1)} %pad_maximum_fusion.refs_4_.refs_5_), channel_id=1, source_target_pairs={{0,1},{1,0},{2,3},{3,2},{4,5},{5,4},{6,7},{7,6},{8,9},{9,8},{10,11... | collective-permute-start | bytes 9437192 | tf_op jit(solution)/shard_map/ppermute | solution.py:1620
  4.2 3.8 collective-permute-start
  4.6 41.7 %collective-permute-start.2 = (bf16[512,1024]{1,0:T(8,128)(2,1)}, bf16[512,1024]{1,0:T(8,128)(2,1)}, u32[]{:S(2)}, u32[]{:S(2)}) collective-permute-start(bf16[512,1024]{1,0:T(8,128)(2,1)} %bitcast.113), channel_id=1, source_target_pairs={{0,1},{1,0},{2,3},{3,2},{4,5},{5,4},{6,7},{7,6},{8,9},{9,8},{10,11... | collective-permute-start | bytes 3145736 | tf_op jit(solution)/shard_map/ppermute | solution.py:1620
  29.6 98.5 %collective-permute-start.5 = (bf16[2,512,1024]{2,1,0:T(8,128)(2,1)}, bf16[2,512,1024]{2,1,0:T(8,128)(2,1)S(1)}, u32[]{:S(2)}, u32[]{:S(2)}) collective-permute-start(bf16[2,512,1024]{2,1,0:T(8,128)(2,1)} %bitcast.122), channel_id=1, source_target_pairs={{0,2},{1,3},{4,6},{5,7},{8,10},{9,11},{12,14},{13,15},{16,18},{17,... | collective-permute-start | bytes 6291464 | tf_op jit(solution)/shard_map/ppermute | solution.py:1711
  67.7 60.4 %collective-permute-start.6 = (bf16[512,1024]{1,0:T(8,128)(2,1)}, bf16[512,1024]{1,0:T(8,128)(2,1)}, u32[]{:S(2)}, u32[]{:S(2)}) collective-permute-start(bf16[512,1024]{1,0:T(8,128)(2,1)} %get-tuple-element.141), channel_id=1, source_target_pairs={{0,2},{1,3},{4,6},{5,7},{8,10},{9,11},{12,14},{13,15},{16,18},{17,... | collective-permute-start | bytes 3145736 | tf_op jit(solution)/shard_map/ppermute | solution.py:1720
  97.8 22.9 %copy-start.20 = (s32[2047]{0:T(1024)S(1)}, s32[2047]{0:T(1024)}, u32[]{:S(2)}) copy-start(s32[2047]{0:T(1024)} %param.15) | copy-start | bytes 24568
  119.1 27.9 %collective-permute-start.8 = (bf16[512,1024]{1,0:T(8,128)(2,1)}, bf16[512,1024]{1,0:T(8,128)(2,1)S(1)}, u32[]{:S(2)}, u32[]{:S(2)}) collective-permute-start(bf16[512,1024]{1,0:T(8,128)(2,1)} %get-tuple-element.156), channel_id=1, source_target_pairs={{0,2},{1,3},{4,6},{5,7},{8,10},{9,11},{12,14},{13,15},{16,18},{17,... | collective-permute-start | bytes 3145736 | tf_op jit(solution)/shard_map/ppermute | solution.py:1720
  128.1 4.5 copy-start.4
  145.3 35.3 %collective-permute-start.7 = (bf16[512,1024]{1,0:T(8,128)(2,1)}, bf16[512,1024]{1,0:T(8,128)(2,1)S(1)}, u32[]{:S(2)}, u32[]{:S(2)}) collective-permute-start(bf16[512,1024]{1,0:T(8,128)(2,1)} %get-tuple-element.173), channel_id=1, source_target_pairs={{2,0},{3,1},{6,4},{7,5},{10,8},{11,9},{14,12},{15,13},{18,16},{19,... | collective-permute-start | bytes 3145736 | tf_op jit(solution)/shard_map/ppermute | solution.py:1723
  147.0 1.0 copy-start.11
  165.2 63.0 %collective-permute-start.9 = (bf16[512,1024]{1,0:T(8,128)(2,1)}, bf16[512,1024]{1,0:T(8,128)(2,1)S(1)}, u32[]{:S(2)}, u32[]{:S(2)}) collective-permute-start(bf16[512,1024]{1,0:T(8,128)(2,1)} %get-tuple-element.188), channel_id=1, source_target_pairs={{2,0},{3,1},{6,4},{7,5},{10,8},{11,9},{14,12},{15,13},{18,16},{19,... | collective-permute-start | bytes 3145736 | tf_op jit(solution)/shard_map/ppermute | solution.py:1723
  180.6 53.1 %copy-start.9 = (bf16[512,1024]{1,0:T(8,128)(2,1)}, bf16[512,1024]{1,0:T(8,128)(2,1)S(1)}, u32[]{:S(2)}) copy-start(bf16[512,1024]{1,0:T(8,128)(2,1)S(1)} %collective-permute-done.7) | copy-start | bytes 3145732
  228.2 5.5 copy-start.10
  233.7 58.6 %collective-permute-start.10 = (bf16[512,1024]{1,0:T(8,128)(2,1)}, bf16[512,1024]{1,0:T(8,128)(2,1)S(1)}, u32[]{:S(2)}, u32[]{:S(2)}) collective-permute-start(bf16[512,1024]{1,0:T(8,128)(2,1)} %get-tuple-element.203), channel_id=1, source_target_pairs={{2,0},{3,1},{6,4},{7,5},{10,8},{11,9},{14,12},{15,13},{18,16},{19,... | collective-permute-start | bytes 3145736 | tf_op jit(solution)/shard_map/ppermute | solution.py:1753
  254.5 100.2 %collective-permute-start.11 = (bf16[512,1024]{1,0:T(8,128)(2,1)}, bf16[512,1024]{1,0:T(8,128)(2,1)S(1)}, u32[]{:S(2)}, u32[]{:S(2)}) collective-permute-start(bf16[512,1024]{1,0:T(8,128)(2,1)} %get-tuple-element.218), channel_id=1, source_target_pairs={{2,0},{3,1},{6,4},{7,5},{10,8},{11,9},{14,12},{15,13},{18,16},{19,... | collective-permute-start | bytes 3145736 | tf_op jit(solution)/shard_map/ppermute | solution.py:1753
  255.8 4.9 copy-start.8
  292.3 1.0 copy-start.7
  354.7 1.0 copy-start.6
  400.9 11.4 %copy-start.5 = (f32[3,8,1024]{2,1,0:T(8,128)S(1)}, f32[3,8,1024]{2,1,0:T(8,128)}, u32[]{:S(2)}) copy-start(f32[3,8,1024]{2,1,0:T(8,128)} %get-tuple-element.253) | copy-start | bytes 294916
  400.9 12.3 %copy-start.14 = (f32[3,1,4096]{2,1,0:T(1,128)S(1)}, f32[3,1,4096]{2,1,0:T(1,128)}, u32[]{:S(2)}) copy-start(f32[3,1,4096]{2,1,0:T(1,128)} %get-tuple-element.255) | copy-start | bytes 147460
  595.0 10.3 %copy-start.3 = (f32[3,512,512]{2,1,0:T(8,128)S(1)}, f32[3,512,512]{2,1,0:T(8,128)}, u32[]{:S(2)}) copy-start(f32[3,512,512]{2,1,0:T(8,128)} %get-tuple-element.245) | copy-start | bytes 9437188
  603.5 4.8 copy-start.15
  603.5 5.5 copy-start.13
  605.3 4.7 copy-start.12
  605.3 5.6 copy-start.1
